TPU v7x, 128 devices: a whole 4x4x4 slice. The times are simulated.
128 devices in a mesh: shard: 16 (over z, y_lo, core), replica: 8 (over x, y_hi).
Axes of the slice: x: 4, y: 4 (y_hi: 2, y_lo: 2; y = y_hi * 2 + y_lo), z: 4, core: 2. Of those that a mesh axis runs over, the one named last changes fastest.
Arguments:
- tokens: bfloat16 [24576, 1024], P(('shard', 'replica')), may hold values from -6 to 6
- norm_one: bfloat16 [1024], P('shard'), may hold values from 0.5 to 1.5
- query_weight: bfloat16 [1024, 1024], P('shard'), may hold values from -0.1875 to 0.1875
- key_matrix: bfloat16 [1024, 512], P('shard'), may hold values from -0.1875 to 0.1875
- value_matrix: bfloat16 [1024, 512], P('shard'), may hold values from -0.1875 to 0.1875
- out_weight: bfloat16 [1024, 1024], P('shard'), may hold values from -1.5 to 1.5
- norm_two: bfloat16 [1024], P('shard'), may hold values from 0.5 to 1.5
- router: bfloat16 [1024, 32], P('shard'), may hold values from -0.09375 to 0.09375
- experts: bfloat16 [32, 3, 1024, 512], P('shard'), may hold values from -4 to 4
- routes: int32 [24576, 8], P(('shard', 'replica')), may hold values from 0 to 31, all different within a row; in each aligned block of 192 rows (0 to 191, 192 to 383, ...) at most 60 rows name the same one
- segments: int32 [24576], P(('shard', 'replica')), may hold values from 0 to 47, as said below
- cotangent: bfloat16 [24576, 1024], P(('shard', 'replica')), may hold values from -6 to 6
Outputs:
- layer_out: bfloat16 [24576, 1024], P(('shard', 'replica'))
- grad_tokens: bfloat16 [24576, 1024], P(('shard', 'replica'))
- grad_norm_one: float32 [1024], P('shard')
- grad_query: float32 [1024, 1024], P('shard')
- grad_key: float32 [1024, 512], P('shard')
- grad_value: float32 [1024, 512], P('shard')
- grad_out_weight: float32 [1024, 1024], P('shard')
- grad_norm_two: float32 [1024], P('shard')
- grad_router: float32 [1024, 32], P('shard')
- grad_experts: float32 [32, 3, 1024, 512], P('shard')
Inputs may be any that keep to these rules, and one draw needn't show every extreme that they name: `routes`: each row names 8 different experts; among the 192 rows of one device no expert is named by more than 60 rows. `segments`: segment numbers never fall. Sequence s (tokens s * 1536 to (s + 1) * 1536 - 1) holds documents 3 s, 3 s + 1 and 3 s + 2, none empty; document 3 s + 1 begins within the first 192 tokens of its sequence and ends within the last 192.
All inputs are finite; a program needn't handle non-finite values.
Results may differ from a plain program's by a relative error of at most 0.025.
Values may be sent and summed in bfloat16 or wider, within the bound.
No kernel may reach another device: no remote copies, remote signals or barrier semaphores. Data moves between devices by JAX's collectives and lax.ppermute only.
A program may use at most 192 MiB of HBM per device.

v0:
```python
import jax
import jax.numpy as jnp
from jax import lax
from jax.sharding import PartitionSpec as P

MODEL_WIDTH = 1024
H = 16
KVH = 8
HD = 64
E = 32
TOP = 8
SEQ = 1536


EPSILON = 1e-06
MASKED = -1e30


def rms_norm(value_vectors, gain_vector):
    inverse = lax.rsqrt(jnp.mean(value_vectors * value_vectors, axis=-1, keepdims=True) + EPSILON)
    return value_vectors * inverse * gain_vector


def rotate(value_vectors, positions):
    half_width = value_vectors.shape[-1] // 2
    frequency = 10000.0 ** (
        -2.0 * jnp.arange(half_width, dtype=jnp.float32) / value_vectors.shape[-1]
    )
    angles = positions[:, None] * frequency[None, :]
    cosine = jnp.cos(angles)[:, None, :]
    sine_part = jnp.sin(angles)[:, None, :]
    front_half = value_vectors[..., :half_width]
    back_half = value_vectors[..., half_width:]
    return jnp.concatenate(
        [front_half * cosine - back_half * sine_part, front_half * sine_part + back_half * cosine],
        axis=-1,
    )


def expert_slots(picks, capacity):
    flat_picks = picks.reshape(-1)
    onehot = (flat_picks[:, None] == jnp.arange(E, dtype=jnp.int32)[None, :]).astype(jnp.int32)
    before = jnp.cumsum(onehot, axis=0) - onehot
    slot_number = jnp.sum(before * onehot, axis=1)
    target = flat_picks * capacity + slot_number
    source = (
        jnp.zeros((E * capacity,), jnp.int32)
        .at[target]
        .set(jnp.arange(flat_picks.shape[0], dtype=jnp.int32))
    )
    live_slot = jnp.zeros((E * capacity,), jnp.float32).at[target].set(1.0)
    return (target, source, live_slot)


def expert_forward(inputs, weights):
    gate_part = jnp.einsum(
        "erd,edf->erf", inputs, weights[:, 0], preferred_element_type=jnp.float32
    )
    up_part = jnp.einsum("erd,edf->erf", inputs, weights[:, 1], preferred_element_type=jnp.float32)
    hidden = (jax.nn.silu(gate_part) * up_part).astype(jnp.bfloat16)
    produced = jnp.einsum(
        "erf,edf->erd", hidden, weights[:, 2], preferred_element_type=jnp.float32
    ).astype(jnp.bfloat16)
    return (gate_part, up_part, hidden, produced)


def expert_backward(weights, gate_part, up_part, grad_output):
    grad_hidden = jnp.einsum(
        "erd,edf->erf", grad_output, weights[:, 2], preferred_element_type=jnp.float32
    )
    sigmoid_part = jax.nn.sigmoid(gate_part)
    grad_gate = (
        grad_hidden * up_part * sigmoid_part * (1.0 + gate_part * (1.0 - sigmoid_part))
    ).astype(jnp.bfloat16)
    grad_up = (grad_hidden * (gate_part * sigmoid_part)).astype(jnp.bfloat16)
    grad_inputs = jnp.einsum(
        "erf,edf->erd", grad_gate, weights[:, 0], preferred_element_type=jnp.float32
    ) + jnp.einsum("erf,edf->erd", grad_up, weights[:, 1], preferred_element_type=jnp.float32)
    return (grad_gate, grad_up, grad_inputs.astype(jnp.bfloat16))


def expert_weight_grads(inputs, hidden, grad_gate, grad_up, grad_output):
    gate_term = jnp.einsum("erd,erf->edf", inputs, grad_gate, preferred_element_type=jnp.float32)
    up_term = jnp.einsum("erd,erf->edf", inputs, grad_up, preferred_element_type=jnp.float32)
    down_term = jnp.einsum("erd,erf->edf", grad_output, hidden, preferred_element_type=jnp.float32)
    return jnp.stack([gate_term, up_term, down_term], axis=1)


def per_device(
    tokens,
    norm_one,
    query_weight,
    key_matrix,
    value_matrix,
    out_weight,
    norm_two,
    router,
    experts,
    routes,
    segments,
    cotangent,
):
    row_count = tokens.shape[0]
    replica_count = lax.axis_size("replica")
    group_size = H // KVH
    scale_factor = HD ** (-0.5)
    capacity = row_count * TOP * 5 // (4 * E)
    device_place = lax.axis_index("shard") * replica_count + lax.axis_index("replica")
    token_index = device_place * row_count + jnp.arange(row_count, dtype=jnp.int32)
    positions = (token_index % SEQ).astype(jnp.float32)
    tokens_wide = tokens.astype(jnp.float32)
    dense_set = (
        lax.all_gather(norm_one, "shard", axis=0, tiled=True),
        lax.all_gather(query_weight, "shard", axis=0, tiled=True),
        lax.all_gather(key_matrix, "shard", axis=0, tiled=True),
        lax.all_gather(value_matrix, "shard", axis=0, tiled=True),
        lax.all_gather(out_weight, "shard", axis=0, tiled=True),
        lax.all_gather(norm_two, "shard", axis=0, tiled=True),
        lax.all_gather(router, "shard", axis=0, tiled=True),
    )
    normed_one = rms_norm(tokens_wide, dense_set[0].astype(jnp.float32)).astype(jnp.bfloat16)
    query_raw = jnp.dot(normed_one, dense_set[1], preferred_element_type=jnp.float32).reshape(
        row_count, H, HD
    )
    key_raw = jnp.dot(normed_one, dense_set[2], preferred_element_type=jnp.float32).reshape(
        row_count, KVH, HD
    )
    value_low = (
        jnp.dot(normed_one, dense_set[3], preferred_element_type=jnp.float32)
        .astype(jnp.bfloat16)
        .reshape(row_count, KVH, HD)
    )
    query_low = (
        rotate(query_raw, positions).astype(jnp.bfloat16).reshape(row_count, KVH, group_size, HD)
    )
    key_low = rotate(key_raw, positions).astype(jnp.bfloat16)
    keys_all, values_all, key_segments = (
        lax.all_gather(key_low, "replica", axis=0, tiled=True),
        lax.all_gather(value_low, "replica", axis=0, tiled=True),
        lax.all_gather(segments, "replica", axis=0, tiled=True),
    )

    def key_blocks(keys_here, values_here, segments_here):
        key_total = keys_here.shape[0]
        block_width = min(512, key_total)
        block_count = key_total // block_width
        key_index = lax.axis_index("shard") * key_total + jnp.arange(key_total, dtype=jnp.int32)
        return (
            keys_here.reshape(block_count, block_width, KVH, HD),
            values_here.reshape(block_count, block_width, KVH, HD),
            key_index.reshape(block_count, block_width),
            segments_here.reshape(block_count, block_width),
        )

    key_blocks_kept = key_blocks(keys_all, values_all, key_segments)

    def scores_of(block_keys, block_index, block_segments):
        scores = (
            jnp.einsum("qhgd,khd->hgqk", query_low, block_keys, preferred_element_type=jnp.float32)
            * scale_factor
        )
        allowed = (block_index[None, :] <= token_index[:, None]) & (
            block_segments[None, :] == segments[:, None]
        )
        return (scores, allowed)

    def running_total(running, key_block):
        largest, summed = running
        scores, allowed = scores_of(key_block[0], key_block[2], key_block[3])
        scores = jnp.where(allowed, scores, MASKED)
        newest = jnp.maximum(largest, jnp.max(scores, axis=-1))
        summed = summed * jnp.exp(largest - newest) + jnp.sum(
            jnp.where(allowed, jnp.exp(scores - newest[..., None]), 0.0), axis=-1
        )
        return ((newest, summed), None)

    start_state = (
        jnp.full((KVH, group_size, row_count), MASKED, jnp.float32),
        jnp.zeros((KVH, group_size, row_count), jnp.float32),
    )
    (largest, summed), unused = lax.scan(running_total, start_state, key_blocks_kept)
    log_total = largest + jnp.log(summed)

    def softmax_of(block_keys, block_index, block_segments):
        scores, allowed = scores_of(block_keys, block_index, block_segments)
        return jnp.where(allowed, jnp.exp(scores - log_total[..., None]), 0.0)

    def attend(running, key_block):
        chances = softmax_of(key_block[0], key_block[2], key_block[3]).astype(jnp.bfloat16)
        return (
            running
            + jnp.einsum(
                "hgqk,khd->qhgd", chances, key_block[1], preferred_element_type=jnp.float32
            ),
            None,
        )

    attended, unused = lax.scan(
        attend, jnp.zeros((row_count, KVH, group_size, HD), jnp.float32), key_blocks_kept
    )
    mixed_low = attended.reshape(row_count, H * HD).astype(jnp.bfloat16)
    middle = tokens_wide + jnp.dot(mixed_low, dense_set[4], preferred_element_type=jnp.float32)
    normed_two = rms_norm(middle, dense_set[5].astype(jnp.float32)).astype(jnp.bfloat16)
    logits = jnp.dot(normed_two, dense_set[6], preferred_element_type=jnp.float32)
    pick_mask = (routes[:, :, None] == jnp.arange(E, dtype=jnp.int32)[None, None, :]).astype(
        jnp.float32
    )
    gate_fraction = jax.nn.softmax(jnp.sum(pick_mask * logits[:, None, :], axis=-1), axis=-1)
    target, source, live_slot = expert_slots(routes, capacity)
    owner_token = source // TOP
    is_live = live_slot[:, None] > 0
    dispatched = jnp.where(is_live, normed_two[owner_token], jnp.zeros((), jnp.bfloat16)).reshape(
        E, capacity, MODEL_WIDTH
    )
    arrived = lax.all_to_all(dispatched, "shard", split_axis=0, concat_axis=1, tiled=True)
    gate_part, up_part, hidden, produced = expert_forward(arrived, experts)
    returned = lax.all_to_all(produced, "shard", split_axis=1, concat_axis=0, tiled=True)
    picked_wide = (
        returned.reshape(E * capacity, MODEL_WIDTH)[target]
        .reshape(row_count, TOP, MODEL_WIDTH)
        .astype(jnp.float32)
    )
    layer_out = (middle + jnp.sum(picked_wide * gate_fraction[:, :, None], axis=1)).astype(
        jnp.bfloat16
    )
    grad_wide = cotangent.astype(jnp.float32)
    gate_grad = jnp.sum(picked_wide * grad_wide[:, None, :], axis=-1)
    chosen_grad = gate_fraction * (
        gate_grad - jnp.sum(gate_fraction * gate_grad, axis=-1, keepdims=True)
    )
    logit_grad = jnp.sum(chosen_grad[:, :, None] * pick_mask, axis=1).astype(jnp.bfloat16)
    flat_share = gate_fraction.reshape(-1)
    slot_grad = (
        jnp.where(is_live, flat_share[source][:, None] * grad_wide[owner_token], 0.0)
        .astype(jnp.bfloat16)
        .reshape(E, capacity, MODEL_WIDTH)
    )
    dense_back = (
        lax.all_gather(norm_one, "shard", axis=0, tiled=True),
        lax.all_gather(query_weight, "shard", axis=0, tiled=True),
        lax.all_gather(key_matrix, "shard", axis=0, tiled=True),
        lax.all_gather(value_matrix, "shard", axis=0, tiled=True),
        lax.all_gather(out_weight, "shard", axis=0, tiled=True),
        lax.all_gather(norm_two, "shard", axis=0, tiled=True),
        lax.all_gather(router, "shard", axis=0, tiled=True),
    )
    keys_back, values_back, segments_back = (
        lax.all_gather(key_low, "replica", axis=0, tiled=True),
        lax.all_gather(value_low, "replica", axis=0, tiled=True),
        lax.all_gather(segments, "replica", axis=0, tiled=True),
    )
    key_blocks_back = key_blocks(keys_back, values_back, segments_back)
    slot_grad_here = lax.all_to_all(slot_grad, "shard", split_axis=0, concat_axis=1, tiled=True)
    grad_gate, grad_up, grad_inputs = expert_backward(experts, gate_part, up_part, slot_grad_here)
    expert_grad = expert_weight_grads(arrived, hidden, grad_gate, grad_up, slot_grad_here)
    returned_grad = lax.all_to_all(grad_inputs, "shard", split_axis=1, concat_axis=0, tiled=True)
    grad_rows = jnp.sum(
        returned_grad.reshape(E * capacity, MODEL_WIDTH)[target]
        .reshape(row_count, TOP, MODEL_WIDTH)
        .astype(jnp.float32),
        axis=1,
    )
    normed_two_grad = (
        jnp.dot(logit_grad, dense_back[6].T, preferred_element_type=jnp.float32) + grad_rows
    )
    router_grad = jnp.dot(normed_two.T, logit_grad, preferred_element_type=jnp.float32)
    unused_two, pull_two = jax.vjp(rms_norm, middle, dense_back[5].astype(jnp.float32))
    middle_norm_grad, gain_two_grad = pull_two(normed_two_grad)
    middle_grad = grad_wide + middle_norm_grad
    branch_grad = middle_grad.astype(jnp.bfloat16)
    out_weight_grad = jnp.dot(mixed_low.T, branch_grad, preferred_element_type=jnp.float32)
    mixed_grad = (
        jnp.dot(branch_grad, dense_back[4].T, preferred_element_type=jnp.float32)
        .astype(jnp.bfloat16)
        .reshape(row_count, KVH, group_size, HD)
    )

    def find_delta(running, key_block):
        chances = softmax_of(key_block[0], key_block[2], key_block[3])
        pressure = jnp.einsum(
            "qhgd,khd->hgqk", mixed_grad, key_block[1], preferred_element_type=jnp.float32
        )
        return (running + jnp.sum(chances * pressure, axis=-1), None)

    delta, unused = lax.scan(
        find_delta, jnp.zeros((KVH, group_size, row_count), jnp.float32), key_blocks_back
    )

    def spread(running, key_block):
        chances = softmax_of(key_block[0], key_block[2], key_block[3])
        pressure = jnp.einsum(
            "qhgd,khd->hgqk", mixed_grad, key_block[1], preferred_element_type=jnp.float32
        )
        score_grad = (chances * (pressure - delta[..., None])).astype(jnp.bfloat16)
        running = (
            running
            + jnp.einsum(
                "hgqk,khd->qhgd", score_grad, key_block[0], preferred_element_type=jnp.float32
            )
            * scale_factor
        )
        key_part = (
            jnp.einsum("hgqk,qhgd->khd", score_grad, query_low, preferred_element_type=jnp.float32)
            * scale_factor
        )
        value_part = jnp.einsum(
            "hgqk,qhgd->khd",
            chances.astype(jnp.bfloat16),
            mixed_grad,
            preferred_element_type=jnp.float32,
        )
        return (running, (key_part, value_part))

    query_grad, (key_parts, value_parts) = lax.scan(
        spread, jnp.zeros((row_count, KVH, group_size, HD), jnp.float32), key_blocks_back
    )
    key_total = key_parts.shape[0] * key_parts.shape[1]
    key_here, value_here = (
        lax.psum_scatter(
            key_parts.reshape(key_total, KVH, HD).astype(jnp.bfloat16),
            "replica",
            scatter_dimension=0,
            tiled=True,
        ).astype(jnp.float32),
        lax.psum_scatter(
            value_parts.reshape(key_total, KVH, HD).astype(jnp.bfloat16),
            "replica",
            scatter_dimension=0,
            tiled=True,
        ).astype(jnp.float32),
    )
    query_grad_low = (
        rotate(query_grad.reshape(row_count, H, HD), -positions)
        .astype(jnp.bfloat16)
        .reshape(row_count, H * HD)
    )
    key_grad_low = rotate(key_here, -positions).astype(jnp.bfloat16).reshape(row_count, KVH * HD)
    value_grad_low = value_here.astype(jnp.bfloat16).reshape(row_count, KVH * HD)
    query_weight_grad = jnp.dot(normed_one.T, query_grad_low, preferred_element_type=jnp.float32)
    key_weight_grad = jnp.dot(normed_one.T, key_grad_low, preferred_element_type=jnp.float32)
    value_weight_grad = jnp.dot(normed_one.T, value_grad_low, preferred_element_type=jnp.float32)
    normed_grad = (
        jnp.dot(query_grad_low, dense_back[1].T, preferred_element_type=jnp.float32)
        + jnp.dot(key_grad_low, dense_back[2].T, preferred_element_type=jnp.float32)
        + jnp.dot(value_grad_low, dense_back[3].T, preferred_element_type=jnp.float32)
    )
    unused_one, pull_one = jax.vjp(rms_norm, tokens_wide, dense_back[0].astype(jnp.float32))
    tokens_norm_grad, gain_one_grad = pull_one(normed_grad)
    tokens_grad = (middle_grad + tokens_norm_grad).astype(jnp.bfloat16)
    shards_back = (
        lax.psum_scatter(
            gain_one_grad.astype(jnp.bfloat16), "shard", scatter_dimension=0, tiled=True
        ).astype(jnp.float32),
        lax.psum_scatter(
            query_weight_grad.astype(jnp.bfloat16), "shard", scatter_dimension=0, tiled=True
        ).astype(jnp.float32),
        lax.psum_scatter(
            key_weight_grad.astype(jnp.bfloat16), "shard", scatter_dimension=0, tiled=True
        ).astype(jnp.float32),
        lax.psum_scatter(
            value_weight_grad.astype(jnp.bfloat16), "shard", scatter_dimension=0, tiled=True
        ).astype(jnp.float32),
        lax.psum_scatter(
            out_weight_grad.astype(jnp.bfloat16), "shard", scatter_dimension=0, tiled=True
        ).astype(jnp.float32),
        lax.psum_scatter(
            gain_two_grad.astype(jnp.bfloat16), "shard", scatter_dimension=0, tiled=True
        ).astype(jnp.float32),
        lax.psum_scatter(
            router_grad.astype(jnp.bfloat16), "shard", scatter_dimension=0, tiled=True
        ).astype(jnp.float32),
    )
    summed_back = (
        lax.psum(shards_back[0].astype(jnp.bfloat16), "replica").astype(jnp.float32),
        lax.psum(shards_back[1].astype(jnp.bfloat16), "replica").astype(jnp.float32),
        lax.psum(shards_back[2].astype(jnp.bfloat16), "replica").astype(jnp.float32),
        lax.psum(shards_back[3].astype(jnp.bfloat16), "replica").astype(jnp.float32),
        lax.psum(shards_back[4].astype(jnp.bfloat16), "replica").astype(jnp.float32),
        lax.psum(shards_back[5].astype(jnp.bfloat16), "replica").astype(jnp.float32),
        lax.psum(shards_back[6].astype(jnp.bfloat16), "replica").astype(jnp.float32),
        lax.psum(expert_grad.astype(jnp.bfloat16), "replica").astype(jnp.float32),
    )
    return (
        layer_out,
        tokens_grad,
        summed_back[0],
        summed_back[1],
        summed_back[2],
        summed_back[3],
        summed_back[4],
        summed_back[5],
        summed_back[6],
        summed_back[7],
    )


def solution(mesh):
    return jax.shard_map(
        per_device,
        mesh=mesh,
        in_specs=(
            P(("shard", "replica"), None),
            P("shard"),
            P("shard", None),
            P("shard", None),
            P("shard", None),
            P("shard", None),
            P("shard"),
            P("shard", None),
            P("shard", None, None, None),
            P(("shard", "replica"), None),
            P(("shard", "replica")),
            P(("shard", "replica"), None),
        ),
        out_specs=(
            P(("shard", "replica"), None),
            P(("shard", "replica"), None),
            P("shard"),
            P("shard", None),
            P("shard", None),
            P("shard", None),
            P("shard", None),
            P("shard"),
            P("shard", None),
            P("shard", None, None, None),
        ),
        check_vma=False,
    )
```

profile of v0, /device:TPU:0, one launch (start us, length us, event | category | flops | bytes accessed | tf_op | source)
XLA Modules:
  0.0 1461.0 jit_solution(7297949015997942253)
XLA Ops:
  13.1 31.8 %all-reduce.6 = (bf16[1024]{0:T(1024)(128)(2,1)S(1)}, bf16[1024]{0:T(1024)(128)(2,1)S(1)}) all-reduce(bf16[1024]{0:T(1024)(128)(2,1)S(1)} %dynamic-update-slice, bf16[1024]{0:T(1024)(128)(2,1)S(1)} %dynamic-update-slice.2), channel_id=1, replica_groups=mesh['shard'=16,'replica'=8] {'shard'}, use_global_device_ids=true, to_apply=%add | all-reduce | flops 2048 | bytes 8192
  50.3 28.8 %all-gather.8.cloned.1.call-done = bf16[1024,512]{1,0:T(8,128)(2,1)} async-done(((bf16[64,512]{1,0:T(8,128)(2,1)}), bf16[1024,512]{1,0:T(8,128)(2,1)}) %all-gather.8.cloned.1.call-update) | async-done | bytes 1048592 | tf_op jit(solution)/shard_map/all_gather | solution.py:116
  84.4 13.3 all-reduce.1
  123.7 56.9 %all-gather.14.cloned.1.call-done = bf16[1536,8,64]{2,1,0:T(8,128)(2,1)} async-done(((bf16[192,8,64]{2,1,0:T(8,128)(2,1)}), bf16[1536,8,64]{2,1,0:T(8,128)(2,1)}) %all-gather.14.cloned.1.call-update) | async-done | bytes 1572880 | tf_op jit(solution)/shard_map/all_gather | solution.py:138
  184.3 24.0 %while.50 = (s32[]{:T(128)}, f32[8,2,192]{2,1,0:T(2,128)S(1)}, f32[8,2,192]{2,1,0:T(2,128)S(1)}, s32[3,512]{1,0:T(4,128)S(1)}, s32[3,512]{1,0:T(4,128)S(1)}, /*i...) while((s32[]{:T(128)}, f32[8,2,192]{2,1,0:T(2,128)S(1)}, ...), condition=%wide.region_4.5_spmd.clone, body=%wide.region_1.4_spmd.clone.sunk | while | flops 214219968 | bytes 14100868 | solution.py:181
  208.4 36.5 %all-gather.10.cloned.1.call-done = bf16[1536,8,64]{2,1,0:T(8,128)(2,1)} async-done(((bf16[192,8,64]{2,1,0:T(8,128)(2,1)}), bf16[1536,8,64]{2,1,0:T(8,128)(2,1)}) %all-gather.10.cloned.1.call-update) | async-done | bytes 1572880 | tf_op jit(solution)/shard_map/all_gather | solution.py:139
  249.6 15.1 %while.51 = (s32[]{:T(128)}, f32[192,8,2,64]{0,3,2,1:T(8,128)}, bf16[3,512,8,64]{1,3,2,0:T(8,128)(2,1)}, s32[3,512]{1,0:T(4,128)S(1)}, s32[3,512]{1,0:T(4,128)S(...) while((s32[]{:T(128)}, f32[192,8,2,64]{0,3,2,1:T(8,128)}, ...), condition=%wide.region_6.7_spmd.clone, body=%wide.region_5.6_spmd.clone.sunk | while | flops 409632960 | bytes 3636615 | solution.py:198
  266.0 13.2 all-gather.18.cloned.1.call-done
  304.3 62.0 %all-gather = bf16[16,64,32]{1,2,0:T(8,128)(2,1)S(1)} all-gather(bf16[1,64,32]{1,2,0:T(8,128)(2,1)S(1)} %bitcast.394), channel_id=1, replica_groups=mesh['shard'=16,'replica'=8] {'shard'}, dimensions={0}, use_global_device_ids=true | all-gather | bytes 69632 | tf_op jit(solution)/shard_map/all_gather | solution.py:119
  423.3 31.1 %all-to-all-done.2 = bf16[32,60,1024]{2,1,0:T(8,128)(2,1)} async-done(((bf16[32,60,1024]{2,1,0:T(8,128)(2,1)}), bf16[32,60,1024]{2,1,0:T(8,128)(2,1)}, u32[]{:S(2)}, u32[]{:S(2)}) %all-to-all-start.2) | async-done | bytes 3932192 | tf_op jit(solution)/shard_map/all_to_all | solution.py:253
  500.9 33.2 %all-to-all-done.1 = bf16[2,960,1024]{2,0,1:T(2,128)(2,1)} async-done(((bf16[2,960,1024]{2,0,1:T(2,128)(2,1)}), bf16[2,960,1024]{2,0,1:T(2,128)(2,1)}, u32[]{:S(2)}, u32[]{:S(2)}) %all-to-all-start.1) | async-done | bytes 3932192 | tf_op jit(solution)/shard_map/all_to_all | solution.py:217
  566.2 20.0 %all-to-all-done.3 = bf16[2,960,1024]{2,0,1:T(2,128)(2,1)} async-done(((bf16[2,960,1024]{2,0,1:T(2,128)(2,1)}), bf16[2,960,1024]{2,0,1:T(2,128)(2,1)}, u32[]{:S(2)}, u32[]{:S(2)}) %all-to-all-start.3) | async-done | bytes 3932192 | tf_op jit(solution)/shard_map/all_to_all | solution.py:256
  616.0 14.9 %while.52 = (s32[]{:T(128)}, f32[8,2,192]{2,1,0:T(2,128)S(1)}, s32[3,512]{1,0:T(4,128)S(1)}, s32[3,512]{1,0:T(4,128)S(1)}, s32[192]{0:T(256)S(1)}, /*index=5*/bf...) while((s32[]{:T(128)}, f32[8,2,192]{2,1,0:T(2,128)S(1)}, ...), condition=%wide.region_24.25_spmd.clone, body=%wide.region_22.24_spmd.clone.sunk | while | flops 410815680 | bytes 14822291 | solution.py:285
  631.0 50.4 %while.53 = (s32[]{:T(128)}, f32[192,8,2,64]{0,3,2,1:T(8,128)}, bf16[3,512,8,64]{1,3,2,0:T(8,128)(2,1)}, bf16[3,512,8,64]{1,3,2,0:T(8,128)(2,1)}, bf16[3,512,8,6...) while((s32[]{:T(128)}, f32[192,8,2,64]{0,3,2,1:T(8,128)}, ...), condition=%wide.region_26.27_spmd.clone, body=%wide.region_25.26_spmd.clone.sunk | while | flops 1023508672 | bytes 80302704 | solution.py:314
  700.9 60.6 %reduce-scatter.22.cloned.1.call-done = bf16[192,512]{1,0:T(8,128)(2,1)} async-done(((bf16[1536,512]{1,0:T(8,128)(2,1)}), bf16[192,512]{1,0:T(8,128)(2,1)}) %reduce-scatter.22.cloned.1.call-update) | async-done | bytes 196624
  764.4 73.9 %reduce-scatter.24.cloned.1.call-done = bf16[192,512]{1,0:T(8,128)(2,1)} async-done(((bf16[1536,512]{1,0:T(8,128)(2,1)}), bf16[192,512]{1,0:T(8,128)(2,1)}) %reduce-scatter.24.cloned.1.call-update) | async-done | bytes 196624 | tf_op jit(solution)/shard_map/reshape | solution.py:338
  860.7 43.9 %reduce-scatter.20.cloned.1.call-done = bf16[64,1024]{1,0:T(8,128)(2,1)} async-done(((bf16[1024,1024]{1,0:T(8,128)(2,1)}), bf16[64,1024]{1,0:T(8,128)(2,1)}) %reduce-scatter.20.cloned.1.call-update) | async-done | bytes 131088 | tf_op jit(solution)/shard_map/reduce_scatter | solution.py:363
  904.6 65.0 %reduce-scatter.14.cloned.1.call-done = bf16[64,1024]{1,0:T(8,128)(2,1)} async-done(((bf16[1024,1024]{1,0:T(8,128)(2,1)}), bf16[64,1024]{1,0:T(8,128)(2,1)}) %reduce-scatter.14.cloned.1.call-update) | async-done | bytes 131088 | tf_op jit(solution)/shard_map/reduce_scatter | solution.py:354
  969.7 62.9 %reduce-scatter.16.cloned.1.call-done = bf16[64,512]{1,0:T(8,128)(2,1)} async-done(((bf16[1024,512]{1,0:T(8,128)(2,1)}), bf16[64,512]{1,0:T(8,128)(2,1)}) %reduce-scatter.16.cloned.1.call-update) | async-done | bytes 65552 | tf_op jit(solution)/shard_map/reduce_scatter | solution.py:357
  1032.6 62.4 %reduce-scatter.18.cloned.1.call-done = bf16[64,512]{1,0:T(8,128)(2,1)} async-done(((bf16[1024,512]{1,0:T(8,128)(2,1)}), bf16[64,512]{1,0:T(8,128)(2,1)}) %reduce-scatter.18.cloned.1.call-update) | async-done | bytes 65552 | tf_op jit(solution)/shard_map/reduce_scatter | solution.py:360
  1097.4 59.3 %reduce-scatter.26.cloned.1.call-done = bf16[64,32]{1,0:T(8,128)(2,1)} async-done(((bf16[1024,32]{1,0:T(8,128)(2,1)}), bf16[64,32]{1,0:T(8,128)(2,1)}) %reduce-scatter.26.cloned.1.call-update) | async-done | bytes 4112
  1161.5 42.1 %all-reduce.5 = (bf16[1024]{0:T(1024)(128)(2,1)S(1)}, bf16[1024]{0:T(1024)(128)(2,1)S(1)}) all-reduce(bf16[1024]{0:T(1024)(128)(2,1)S(1)} %get-tuple-element.669, bf16[1024]{0:T(1024)(128)(2,1)S(1)} %get-tuple-element.667), channel_id=4, replica_groups=mesh['shard'=16,'replica'=8] {'shard'}, use_global_device_ids=true, to_apply=%region_31.32.clone | all-reduce | flops 2048 | bytes 8192
  1203.7 28.9 %all-reduce.7 = (bf16[64]{0:T(256)(128)(2,1)S(1)}, bf16[64]{0:T(256)(128)(2,1)S(1)}, bf16[64,32]{0,1:T(8,128)(2,1)S(1)}) all-reduce(bf16[64]{0:T(256)(128)(2,1)S(1)} %dynamic-slice.4, bf16[64]{0:T(256)(128)(2,1)S(1)} %dynamic-slice.6, bf16[64,32]{0,1:T(8,128)(2,1)S(1)} %copy.238), channel_id=1, replica_groups=mesh['shard'=16,'replica'=8] {'replica'}, use_global_device_ids=true, to_apply=%region_32.33 | all-reduce | flops 2176 | bytes 8704 | tf_op jit(solution)/shard_map/psum | solution.py:374
  1235.2 206.6 %all-reduce.11.cloned.1.call-done = (bf16[2,3,1024,512]{3,2,0,1:T(8,128)(2,1)}, bf16[64,1024]{1,0:T(8,128)(2,1)}, bf16[64,512]{1,0:T(8,128)(2,1)}, bf16[64,512]{1,0:T(8,128)(2,1)}, bf16[64,1024]{1,0:T(8,128)(2,1)}) async-done(((bf16[2,3,1024,512]{3,2,0,1:T(8,128)(2,1)}, bf16[64,1024]{1,0:T(8,128)(2,1)}, bf16[64,512]{1,0:T(8,128)(2,1)}, bf16[64,512]{1,0:T(8,128)(2,1)}, bf16[64,1024]{1,0:T(8,128)(2,1)}), ...) | async-done | bytes 6684688 | tf_op jit(solution)/shard_map/psum | solution.py:381
  (380 shorter events, 410.4 us)
Async XLA Ops:
  7.2 39.9 %all-gather.12.cloned.1.call-start = ((), (), s32[]{:S(2)}) async-start(), calls=%async_computation.13 | async-start | bytes 1114112 | tf_op jit(solution)/shard_map/all_gather | solution.py:115
  7.9 71.2 %all-gather.8.cloned.1.call-start = ((), (), s32[]{:S(2)}) async-start(), calls=%async_computation.11 | async-start | bytes 1114112 | tf_op jit(solution)/shard_map/all_gather | solution.py:116
  8.7 112.1 %all-gather.16.cloned.1.call-start = ((), (), s32[]{:S(2)}) async-start(), calls=%async_computation.15 | async-start | bytes 2228224 | tf_op jit(solution)/shard_map/all_gather | solution.py:114
  9.4 171.2 %all-gather.14.cloned.1.call-start = ((), (), s32[]{:S(2)}) async-start(), calls=%async_computation.14 | async-start | bytes 3538944 | tf_op jit(solution)/shard_map/all_gather | solution.py:138
  44.9 75.9 %copy-start.30 = (f32[1024]{0:T(1024)}, f32[1024]{0:T(1024)S(1)}, u32[]{:S(2)}) copy-start(f32[1024]{0:T(1024)S(1)} %convert_element_type.197) | copy-start | bytes 12292
  46.1 74.7 %copy-start.39 = (f32[192]{0:T(256)}, f32[192]{0:T(256)S(1)}, u32[]{:S(2)}) copy-start(f32[192]{0:T(256)S(1)} %fusion.141) | copy-start | bytes 2308
  50.2 194.7 %all-gather.10.cloned.1.call-start = ((), (), s32[]{:S(2)}) async-start(), calls=%async_computation.12 | async-start | bytes 3538944 | tf_op jit(solution)/shard_map/all_gather | solution.py:139
  81.9 197.3 %all-gather.18.cloned.1.call-start = ((), (), s32[]{:S(2)}) async-start(), calls=%async_computation.16 | async-start | bytes 2228224 | tf_op jit(solution)/shard_map/all_gather | solution.py:117
  282.6 100.5 %copy-start = (bf16[192,1024]{1,0:T(8,128)(2,1)}, bf16[192,1024]{1,0:T(8,128)(2,1)S(1)}, u32[]{:S(2)}) copy-start(bf16[192,1024]{1,0:T(8,128)(2,1)S(1)} %multiply_convert_fusion.3) | copy-start | bytes 1179652
  299.6 99.8 %all-to-all-start = ((bf16[32,60,1024]{2,1,0:T(8,128)(2,1)}), bf16[32,60,1024]{2,1,0:T(8,128)(2,1)}, u32[]{:S(2)}, u32[]{:S(2)}) async-start(bf16[32,60,1024]{2,1,0:T(8,128)(2,1)} %broadcast_select_fusion.1), calls=%async_computation | async-start | bytes 8388608 | tf_op jit(solution)/shard_map/all_to_all | solution.py:215
  399.5 54.9 %all-to-all-start.2 = ((bf16[32,60,1024]{2,1,0:T(8,128)(2,1)}), bf16[32,60,1024]{2,1,0:T(8,128)(2,1)}, u32[]{:S(2)}, u32[]{:S(2)}) async-start(bf16[32,60,1024]{2,1,0:T(8,128)(2,1)} %select_convert_fusion), calls=%async_computation.2 | async-start | bytes 8388608 | tf_op jit(solution)/shard_map/all_to_all | solution.py:253
  481.6 52.5 %all-to-all-start.1 = ((bf16[2,960,1024]{2,0,1:T(2,128)(2,1)}), bf16[2,960,1024]{2,0,1:T(2,128)(2,1)}, u32[]{:S(2)}, u32[]{:S(2)}) async-start(bf16[2,960,1024]{2,0,1:T(2,128)(2,1)} %copy.186), calls=%async_computation.1 | async-start | bytes 7864320 | tf_op jit(solution)/shard_map/all_to_all | solution.py:217
  534.1 52.1 %all-to-all-start.3 = ((bf16[2,960,1024]{2,0,1:T(2,128)(2,1)}), bf16[2,960,1024]{2,0,1:T(2,128)(2,1)}, u32[]{:S(2)}, u32[]{:S(2)}) async-start(bf16[2,960,1024]{2,0,1:T(2,128)(2,1)} %copy.196), calls=%async_computation.3 | async-start | bytes 7864320 | tf_op jit(solution)/shard_map/all_to_all | solution.py:256
  538.6 222.9 %reduce-scatter.22.cloned.1.call-start = ((), (), s32[]{:S(2)}) async-start(), calls=%async_computation.21 | async-start | bytes 1769472
  688.0 150.3 %reduce-scatter.24.cloned.1.call-start = ((), (), s32[]{:S(2)}) async-start(), calls=%async_computation.22 | async-start | bytes 1769472 | tf_op jit(solution)/shard_map/reshape | solution.py:338
  694.7 209.9 %reduce-scatter.20.cloned.1.call-start = ((), (), s32[]{:S(2)}) async-start(), calls=%async_computation.20 | async-start | bytes 2228224 | tf_op jit(solution)/shard_map/reduce_scatter | solution.py:363
  698.2 271.4 %reduce-scatter.14.cloned.1.call-start = ((), (), s32[]{:S(2)}) async-start(), calls=%async_computation.17 | async-start | bytes 2228224 | tf_op jit(solution)/shard_map/reduce_scatter | solution.py:354
  700.9 331.7 %reduce-scatter.16.cloned.1.call-start = ((), (), s32[]{:S(2)}) async-start(), calls=%async_computation.18 | async-start | bytes 1114112 | tf_op jit(solution)/shard_map/reduce_scatter | solution.py:357
  764.3 330.6 %reduce-scatter.18.cloned.1.call-start = ((), (), s32[]{:S(2)}) async-start(), calls=%async_computation.19 | async-start | bytes 1114112 | tf_op jit(solution)/shard_map/reduce_scatter | solution.py:360
  840.9 315.8 %reduce-scatter.26.cloned.1.call-start = ((), (), s32[]{:S(2)}) async-start(), calls=%async_computation.23 | async-start | bytes 278528
  855.1 586.7 %all-reduce.11.cloned.1.call-start = ((), (), s32[]{:S(2)}) async-start(), calls=%async_computation.24 | async-start | bytes 13369344 | tf_op jit(solution)/shard_map/psum | solution.py:381
  860.7 234.9 %copy-start.15 = (bf16[1024,1024]{1,0:T(8,128)(2,1)S(1)}, bf16[1024,1024]{1,0:T(8,128)(2,1)}, u32[]{:S(2)}) copy-start(bf16[1024,1024]{1,0:T(8,128)(2,1)} %all-gather.16.cloned.1.call-done) | copy-start | bytes 6291460
  1097.4 136.8 %copy-start.42 = (f32[192]{0:T(256)S(1)}, f32[192]{0:T(256)}, u32[]{:S(2)}) copy-start(f32[192]{0:T(256)} %copy-done.41) | copy-start | bytes 2308
  1097.4 136.8 %copy-start.13 = (f32[192,1024]{1,0:T(8,128)S(1)}, f32[192,1024]{1,0:T(8,128)}, u32[]{:S(2)}) copy-start(f32[192,1024]{1,0:T(8,128)} %copy-done.12) | copy-start | bytes 2359300
  (54 other events, 483.3 us)
Sparse Core Ops, SparseCore 0:
  9.7 35.0 all-gather.11
  46.5 32.5 all-gather.7
  80.8 34.3 all-gather.15
  118.0 62.5 all-gather.13
  183.3 61.5 all-gather.9
  246.4 32.7 all-gather.17
  688.1 73.3 reduce-scatter.21
  765.3 73.0 reduce-scatter.23
  840.7 63.8 reduce-scatter.19
  906.9 62.7 reduce-scatter.13
  972.0 60.4 reduce-scatter.15
  1034.9 60.0 reduce-scatter.17
  1097.9 58.7 reduce-scatter.25
  1160.3 281.5 all-reduce.10
where the time goes:
time: 1470 us; the launch traced here: 1460 us
  waiting for transfers between devices  857 us (58%)
  blocking collectives  178 us (12%)
  local copies, waits for them, and re-layouts  166 us (11%)
  matrix products  162 us (11%)
  other arithmetic  59.7 us (4%)
  starting transfers between devices  19.7 us (1%)
  between operations  17.3 us (1%)
    psum x1, waiting for transfers between devices, per_device(): lax.psum(expert_grad.astype(jnp.bfloat16), 'replica').astype(jnp.float32)  207 us
    unnamed x16, waiting for transfers between devices  123 us
    unnamed x3, blocking collectives  87.1 us
    reshape x1, waiting for transfers between devices, per_device(): value_here.astype(jnp.bfloat16).reshape(row_count, KVH * HD)  73.9 us
    reduce_scatter x1, waiting for transfers between devices, per_device(): lax.psum_scatter(query_weight_grad.astype(jnp.bfloat16), 'shard', scatter...  65 us
    reduce_scatter x1, waiting for transfers between devices, per_device(): lax.psum_scatter(key_weight_grad.astype(jnp.bfloat16), 'shard', scatter_d...  62.9 us
    reduce_scatter x1, waiting for transfers between devices, per_device(): lax.psum_scatter(value_weight_grad.astype(jnp.bfloat16), 'shard', scatter...  62.4 us
    all_gather x1, blocking collectives, per_device(): lax.all_gather(router, 'shard', axis=0, tiled=True)  62 us
  transfers between devices with their start and end apart: 18, of which 15 were waited for; matrix products, arithmetic and copies ran while one was open for 16% of the time, Pallas kernels for 0%

commit v1 on v0

v1 whole, which is shorter than its diff:
```python
import jax
import jax.numpy as jnp
from jax import lax
from jax.experimental import pallas as pl
from jax.experimental.pallas import tpu as pltpu
from jax.sharding import PartitionSpec as P

D = 1024
H = 16
KVH = 8
HD = 64
FF = 512
E = 32
TOP = 8
SEQ = 1536
TOK = 192
NS = 16
NR = 8
SLOTS = 64
QB = 256
NQ = SEQ // QB
EPSILON = 1e-06
MASKED = -1e30
SCALE = HD ** (-0.5)
BF = jnp.bfloat16
F32 = jnp.float32

NT = (((1,), (1,)), ((), ()))
TN = (((0,), (0,)), ((), ()))


def mm(a, b, dims=(((1,), (0,)), ((), ()))):
    return lax.dot_general(a, b, dims, preferred_element_type=F32)


def split_all(x, axis):
    return lax.all_to_all(x, axis, 0, 0, tiled=True)


def spread_all(x, axis, count):
    return split_all(jnp.broadcast_to(x[None], (count,) + x.shape), axis)


def stacked_heads(block):
    return jnp.concatenate([block[:, :HD], block[:, HD:]], axis=0)


def allowed_keys(key_block, query_block, start_row):
    key_index = lax.broadcasted_iota(jnp.int32, (QB, 2 * QB), 0) + key_block * QB
    column = lax.broadcasted_iota(jnp.int32, (1, 2 * QB), 1)
    query_row = jnp.where(column >= QB, column - QB, column) + query_block * QB
    return (key_index >= start_row) & (key_index <= query_row)


def attend_kernel(q_ref, k_ref, v_ref, start_ref, out_ref, lse_ref):
    i = pl.program_id(0)
    q2 = stacked_heads(q_ref[...])
    start_row = jnp.concatenate([start_ref[0], start_ref[0]], axis=1)

    def step(j, carry):
        largest, summed, total = carry
        rows = pl.ds(pl.multiple_of(j * QB, QB), QB)
        scores = mm(k_ref[rows, :], q2, NT)
        scores = jnp.where(allowed_keys(j, i, start_row), scores, MASKED)
        newest = jnp.maximum(largest, jnp.max(scores, axis=0, keepdims=True))
        chances = jnp.exp(scores - newest)
        factor = jnp.exp(largest - newest)
        summed = summed * factor + jnp.sum(chances, axis=0, keepdims=True)
        total = total * factor + mm(v_ref[rows, :], chances.astype(BF), TN)
        return (newest, summed, total)

    largest, summed, total = lax.fori_loop(
        0,
        i + 1,
        step,
        (
            jnp.full((1, 2 * QB), MASKED, F32),
            jnp.zeros((1, 2 * QB), F32),
            jnp.zeros((HD, 2 * QB), F32),
        ),
    )
    total = total / summed
    out_ref[...] = jnp.concatenate([total[:, :QB], total[:, QB:]], axis=0).T.astype(BF)
    lse_ref[0] = largest + jnp.log(summed)


def attend(q, k, v, start):
    whole = lambda width: pl.BlockSpec((SEQ, width), lambda i: (0, 0))
    return pl.pallas_call(
        attend_kernel,
        grid=(NQ,),
        in_specs=[
            pl.BlockSpec((QB, 2 * HD), lambda i: (i, 0)),
            whole(HD),
            whole(HD),
            pl.BlockSpec((1, 1, QB), lambda i: (i, 0, 0)),
        ],
        out_specs=[
            pl.BlockSpec((QB, 2 * HD), lambda i: (i, 0)),
            pl.BlockSpec((1, 1, 2 * QB), lambda i: (i, 0, 0)),
        ],
        out_shape=[
            jax.ShapeDtypeStruct((SEQ, 2 * HD), BF),
            jax.ShapeDtypeStruct((NQ, 1, 2 * QB), F32),
        ],
        compiler_params=pltpu.CompilerParams(vmem_limit_bytes=40 * 1024 * 1024),
    )(q, k, v, start)


def attend_back_kernel(
    q_ref,
    k_ref,
    v_ref,
    grad_ref,
    start_ref,
    lse_ref,
    cos_t_ref,
    sin_t_ref,
    cos_ref,
    sin_ref,
    dq_ref,
    dkv_ref,
    chances_ref,
    pressure_ref,
    dk_ref,
    dv_ref,
):
    i = pl.program_id(0)

    @pl.when(i == 0)
    def clear():
        dk_ref[...] = jnp.zeros_like(dk_ref)
        dv_ref[...] = jnp.zeros_like(dv_ref)

    q2 = stacked_heads(q_ref[...])
    grad2 = stacked_heads(grad_ref[...])
    start_row = jnp.concatenate([start_ref[0], start_ref[0]], axis=1)
    lse = lse_ref[0]

    def first(j, delta):
        rows = pl.ds(pl.multiple_of(j * QB, QB), QB)
        scores = mm(k_ref[rows, :], q2, NT)
        chances = jnp.where(allowed_keys(j, i, start_row), jnp.exp(scores - lse), 0.0)
        pressure = mm(v_ref[rows, :], grad2, NT)
        chances_ref[rows, :] = chances
        pressure_ref[rows, :] = pressure
        return delta + jnp.sum(chances * pressure, axis=0, keepdims=True)

    delta = lax.fori_loop(0, i + 1, first, jnp.zeros((1, 2 * QB), F32))

    def second(j, total):
        rows = pl.ds(pl.multiple_of(j * QB, QB), QB)
        chances = chances_ref[rows, :]
        score_grad = (chances * (pressure_ref[rows, :] - delta)).astype(BF)
        dv_ref[rows, :] += mm(chances.astype(BF), grad2)
        dk_ref[rows, :] += mm(score_grad, q2)
        return total + mm(k_ref[rows, :], score_grad, TN)

    total = lax.fori_loop(0, i + 1, second, jnp.zeros((HD, 2 * QB), F32)) * SCALE
    cosine, sine = cos_t_ref[...], sin_t_ref[...]
    half = HD // 2
    parts = []
    for head in range(2):
        front = total[:half, head * QB : (head + 1) * QB]
        back = total[half:, head * QB : (head + 1) * QB]
        parts += [front * cosine + back * sine, back * cosine - front * sine]
    dq_ref[...] = jnp.concatenate(parts, axis=0).T.astype(BF)

    @pl.when(i == NQ - 1)
    def finish():
        for j in range(NQ):
            rows = slice(j * QB, (j + 1) * QB)
            dk = dk_ref[rows, :]
            swapped = jnp.concatenate([dk[:, half:], dk[:, :half]], axis=1)
            dk = dk * cos_ref[rows, :] - swapped * sin_ref[rows, :]
            dkv_ref[rows, :] = jnp.concatenate([dk, dv_ref[rows, :]], axis=1).astype(BF)


def attend_back(q, k, v, grad, start, lse, cos_t, sin_t, cos, sin):
    whole = lambda width: pl.BlockSpec((SEQ, width), lambda i: (0, 0))
    block = pl.BlockSpec((QB, 2 * HD), lambda i: (i, 0))
    table = pl.BlockSpec((HD // 2, QB), lambda i: (0, i))
    return pl.pallas_call(
        attend_back_kernel,
        grid=(NQ,),
        in_specs=[
            block,
            whole(HD),
            whole(HD),
            block,
            pl.BlockSpec((1, 1, QB), lambda i: (i, 0, 0)),
            pl.BlockSpec((1, 1, 2 * QB), lambda i: (i, 0, 0)),
            table,
            table,
            whole(HD),
            whole(HD),
        ],
        out_specs=[block, whole(2 * HD)],
        out_shape=[
            jax.ShapeDtypeStruct((SEQ, 2 * HD), BF),
            jax.ShapeDtypeStruct((SEQ, 2 * HD), BF),
        ],
        scratch_shapes=[
            pltpu.VMEM((SEQ, 2 * QB), F32),
            pltpu.VMEM((SEQ, 2 * QB), F32),
            pltpu.VMEM((SEQ, HD), F32),
            pltpu.VMEM((SEQ, HD), F32),
        ],
        compiler_params=pltpu.CompilerParams(vmem_limit_bytes=40 * 1024 * 1024),
    )(q, k, v, grad, start, lse, cos_t, sin_t, cos, sin)


def swap_halves(weights):
    parts = weights.reshape(weights.shape[0], -1, 2, HD // 2)
    return parts[:, :, ::-1, :].reshape(weights.shape)


def hi_lo(value):
    high = value.astype(BF)
    rest = value - high.astype(F32)
    middle = rest.astype(BF)
    return high, middle, (rest - middle.astype(F32)).astype(BF)


def per_device(
    tokens,
    norm_one,
    query_weight,
    key_matrix,
    value_matrix,
    out_weight,
    norm_two,
    router,
    experts,
    routes,
    segments,
    cotangent,
):
    shard = lax.axis_index("shard")
    replica = lax.axis_index("replica")

    segment_row = jnp.pad(segments.astype(BF)[None, :], ((0, 15), (0, D - TOK)))
    sequence = spread_all(jnp.concatenate([tokens, segment_row], axis=0), "replica", NR)
    tokens_seq = sequence[:, :TOK].reshape(SEQ, D)
    segments_seq = sequence[:, TOK, :TOK].astype(jnp.int32).reshape(SEQ)

    own_heads = jnp.concatenate(
        [
            lax.dynamic_slice(query_weight, (0, replica * 128), (64, 128)),
            lax.dynamic_slice(key_matrix, (0, replica * HD), (64, HD)),
            lax.dynamic_slice(value_matrix, (0, replica * HD), (64, HD)),
        ],
        axis=1,
    )
    small = jnp.concatenate(
        [out_weight, own_heads, router, norm_one[:, None], norm_two[:, None], jnp.zeros((64, 94), BF)],
        axis=1,
    )
    gathered = lax.all_gather(small, "shard", axis=0, tiled=True)
    out_full = gathered[:, :1024]
    heads_full = gathered[:, 1024:1280]
    router_full = gathered[:, 1280:1312]
    gain_one = gathered[:, 1312].astype(F32)
    gain_two = gathered[:, 1313].astype(F32)

    chosen = jnp.any(routes[:, :, None] == jnp.arange(E, dtype=jnp.int32), axis=1)
    earlier = jnp.tril(jnp.ones((TOK, TOK), BF), -1)
    slot = jnp.where(chosen, mm(earlier, chosen.astype(BF)), -1.0)
    cot_rows = jnp.concatenate([cotangent, slot.astype(BF), jnp.zeros((TOK, 96), BF)], axis=1)
    cot_all = lax.all_gather(cot_rows, "shard", axis=0, tiled=True)

    half = HD // 2
    frequency = 10000.0 ** (-2.0 * jnp.arange(half, dtype=F32) / HD)
    angles = jnp.arange(SEQ, dtype=F32)[:, None] * frequency[None, :]
    cosine, sine = jnp.cos(angles), jnp.sin(angles)
    cos_head = jnp.concatenate([cosine, cosine], axis=1)
    sin_head = jnp.concatenate([-sine, sine], axis=1)
    wide = tokens_seq.astype(F32)
    inverse = lax.rsqrt(jnp.mean(wide * wide, axis=-1, keepdims=True) + EPSILON)
    normed_one = (wide * inverse * gain_one).astype(BF)
    weights_ext = jnp.concatenate([heads_full, swap_halves(heads_full[:, :192])], axis=1)
    raw = mm(normed_one, weights_ext)
    turned = raw[:, :192] * jnp.tile(cos_head, (1, 3)) + raw[:, 256:448] * jnp.tile(sin_head, (1, 3))
    q_low = (turned[:, :128].astype(BF).astype(F32) * SCALE).astype(BF)
    k_low = turned[:, 128:192].astype(BF)
    v_low = raw[:, 192:256].astype(BF)
    first_segment = shard * 3
    count_one = jnp.sum((segments_seq == first_segment).astype(jnp.int32))
    count_two = jnp.sum((segments_seq == first_segment + 1).astype(jnp.int32))
    start = jnp.where(
        segments_seq == first_segment,
        0,
        jnp.where(segments_seq == first_segment + 1, count_one, count_one + count_two),
    ).reshape(NQ, 1, QB)
    mixed_heads, lse = attend(q_low, k_low, v_low, start)

    mixed = split_all(mixed_heads.reshape(NR, TOK, 128), "replica")
    mixed_low = mixed.transpose(1, 0, 2).reshape(TOK, H * HD)
    tokens_wide = tokens.astype(F32)
    middle = tokens_wide + mm(mixed_low, out_full)
    inverse_two = lax.rsqrt(jnp.mean(middle * middle, axis=-1, keepdims=True) + EPSILON)
    normed_two = (middle * inverse_two * gain_two).astype(BF)
    logits = jnp.where(chosen, mm(normed_two, router_full), MASKED)
    powers = jnp.where(chosen, jnp.exp(logits - jnp.max(logits, axis=-1, keepdims=True)), 0.0)
    gates = powers / jnp.sum(powers, axis=-1, keepdims=True)

    gate_high, gate_middle, gate_low = hi_lo(gates)
    rows_out = jnp.concatenate(
        [normed_two, gate_high, gate_middle, gate_low, jnp.zeros((TOK, 32), BF)], axis=1
    )
    rows_all = lax.all_gather(rows_out, "shard", axis=0, tiled=True)

    def own_columns(array, first):
        picked = lax.dynamic_slice(array, (0, first + 2 * shard), (NS * TOK, 2))
        return picked.astype(F32).reshape(NS, TOK, 2).transpose(0, 2, 1)

    own_slots = own_columns(cot_all, 1024)
    own_gates = own_columns(rows_all, 1024) + own_columns(rows_all, 1056) + own_columns(rows_all, 1088)
    slot_index = jnp.arange(SLOTS, dtype=F32)
    picks = own_slots[:, :, None, :] == slot_index[None, None, :, None]
    picks_low = picks.astype(BF)
    slot_gates = jnp.sum(jnp.where(picks, own_gates[:, :, None, :], 0.0), axis=-1)
    slot_gates = slot_gates.transpose(1, 0, 2).reshape(2, NS * SLOTS, 1)

    def pick_rows(array):
        return (
            jnp.einsum(
                "bect,btd->ebcd",
                picks_low,
                array[:, :D].reshape(NS, TOK, D),
                preferred_element_type=F32,
            )
            .astype(BF)
            .reshape(2, NS * SLOTS, D)
        )

    arrived = pick_rows(rows_all)
    cot_arrived = pick_rows(cot_all)
    gate_w, up_w, down_w = experts[:, 0], experts[:, 1], experts[:, 2]
    bmm = lambda text, a, b: jnp.einsum(text, a, b, preferred_element_type=F32)
    gate_part = bmm("erd,edf->erf", arrived, gate_w)
    up_part = bmm("erd,edf->erf", arrived, up_w)
    sigmoid = jax.nn.sigmoid(gate_part)
    hidden = (gate_part * sigmoid * up_part).astype(BF)
    produced = bmm("erf,edf->erd", hidden, down_w).astype(BF)
    gate_grads = jnp.sum(cot_arrived.astype(F32) * produced.astype(F32), axis=-1)
    grad_out = (slot_gates * cot_arrived.astype(F32)).astype(BF)
    grad_hidden = bmm("erd,edf->erf", grad_out, down_w)
    grad_gate = (grad_hidden * up_part * sigmoid * (1.0 + gate_part * (1.0 - sigmoid))).astype(BF)
    grad_up = (grad_hidden * (gate_part * sigmoid)).astype(BF)
    grad_in = (
        bmm("erf,edf->erd", grad_gate, gate_w) + bmm("erf,edf->erd", grad_up, up_w)
    ).astype(BF)
    expert_grad = jnp.stack(
        [
            bmm("erd,erf->edf", arrived, grad_gate),
            bmm("erd,erf->edf", arrived, grad_up),
            bmm("erd,erf->edf", grad_out, hidden),
        ],
        axis=1,
    ).astype(BF)

    gg = jnp.stack(hi_lo(gate_grads.reshape(2, NS, SLOTS)), axis=2)
    gg = jnp.pad(gg, ((0, 0), (0, 0), (0, 1), (0, D - SLOTS)))
    grad_in = jnp.concatenate([grad_in.reshape(2, NS, SLOTS, D)[:, :, :60], gg], axis=2)
    back = split_all(grad_in.transpose(1, 0, 2, 3), "shard").reshape(E, SLOTS, D)
    returned = split_all(
        produced.reshape(2, NS, SLOTS, D).transpose(1, 0, 2, 3), "shard"
    ).reshape(E * SLOTS, D)
    expert_parts = split_all(expert_grad.reshape(NR, 2 * 3 * D // NR, FF), "replica")
    expert_sum = jnp.sum(expert_parts.reshape(NR, -1, FF).astype(F32), axis=0).astype(BF)
    expert_total = spread_all(expert_sum, "replica", NR).reshape(2, 3, D, FF).astype(F32)

    spots = slot[:, :, None] == slot_index
    spots_low = spots.astype(BF).reshape(TOK, E * SLOTS)
    grad_rows = mm(spots_low, back.reshape(E * SLOTS, D))
    gg_back = jnp.sum(back[:, 60:63, :SLOTS].astype(F32), axis=1)
    gate_grad = jnp.sum(jnp.where(spots, gg_back[None], 0.0), axis=-1)
    chosen_grad = gates * (gate_grad - jnp.sum(gates * gate_grad, axis=-1, keepdims=True))
    logit_grad = chosen_grad.astype(BF)
    weighted_high = jnp.where(spots, gate_high[:, :, None], jnp.zeros((), BF)).reshape(TOK, E * SLOTS)
    weighted_low = jnp.where(spots, gate_middle[:, :, None], jnp.zeros((), BF)).reshape(TOK, E * SLOTS)
    layer_out = (middle + mm(weighted_high, returned) + mm(weighted_low, returned)).astype(BF)

    normed_two_grad = mm(logit_grad, router_full, NT) + grad_rows
    router_grad = mm(normed_two, logit_grad, TN)
    hat = middle * inverse_two
    gain_two_grad = jnp.sum(normed_two_grad * hat, axis=0)
    dyg = normed_two_grad * gain_two
    middle_grad = cotangent.astype(F32) + inverse_two * (
        dyg - hat * jnp.mean(dyg * hat, axis=-1, keepdims=True)
    )
    branch_grad = middle_grad.astype(BF)
    out_grad = mm(mixed_low, branch_grad, TN)
    mixed_grad = mm(branch_grad, out_full, NT).astype(BF)
    grad_heads = split_all(mixed_grad.reshape(TOK, NR, 128).transpose(1, 0, 2), "replica")

    dq, dkv = attend_back(
        q_low,
        k_low,
        v_low,
        grad_heads.reshape(SEQ, 128),
        start,
        lse,
        cosine.T,
        sine.T,
        cos_head,
        sin_head,
    )
    head_grad = jnp.concatenate([dq, dkv], axis=1)
    by_token = split_all(head_grad.reshape(NR, TOK, 256), "replica")
    heads_grad = mm(normed_one, head_grad, TN).astype(BF)
    heads_parts = split_all(heads_grad.reshape(NS, 64, 256), "shard")
    heads_sum = jnp.sum(heads_parts.astype(F32), axis=0).astype(BF)

    dense = jnp.concatenate(
        [out_grad, router_grad, gain_two_grad[:, None], jnp.zeros((D, 95), F32)], axis=1
    ).astype(BF)
    dense_parts = split_all(dense.reshape(NS, 64, 1152), "shard")
    dense_sum = jnp.sum(dense_parts.astype(F32), axis=0).astype(BF)
    dense_here = split_all(dense_sum.reshape(NR, 8, 1152), "replica")
    dense_total = jnp.sum(dense_here.astype(F32), axis=0).astype(BF)

    last = jnp.concatenate([heads_sum.reshape(128, 128), dense_total.reshape(72, 128)], axis=0)
    last = spread_all(jnp.pad(last, ((0, 8), (0, 0))), "replica", NR)
    head_total = last[:, :128].reshape(NR, 64, 256).astype(F32)
    dense_total = last[:, 128:200].reshape(64, 1152).astype(F32)
    query_grad = head_total[:, :, :128].transpose(1, 0, 2).reshape(64, 1024)
    key_grad = head_total[:, :, 128:192].transpose(1, 0, 2).reshape(64, 512)
    value_grad = head_total[:, :, 192:].transpose(1, 0, 2).reshape(64, 512)
    norm_one_grad = (
        jnp.sum(query_grad * query_weight.astype(F32), axis=1)
        + jnp.sum(key_grad * key_matrix.astype(F32), axis=1)
        + jnp.sum(value_grad * value_matrix.astype(F32), axis=1)
    ) / norm_one.astype(F32)

    qkv_full = lax.all_gather(
        jnp.concatenate([query_weight, key_matrix, value_matrix], axis=1), "shard", axis=0, tiled=True
    )
    by_token = by_token.transpose(1, 0, 2)
    normed_grad = (
        mm(by_token[:, :, :128].reshape(TOK, 1024), qkv_full[:, :1024], NT)
        + mm(by_token[:, :, 128:192].reshape(TOK, 512), qkv_full[:, 1024:1536], NT)
        + mm(by_token[:, :, 192:].reshape(TOK, 512), qkv_full[:, 1536:], NT)
    )
    inverse_one = lax.rsqrt(jnp.mean(tokens_wide * tokens_wide, axis=-1, keepdims=True) + EPSILON)
    hat_one = tokens_wide * inverse_one
    dyg_one = normed_grad * gain_one
    tokens_grad = (
        middle_grad
        + inverse_one * (dyg_one - hat_one * jnp.mean(dyg_one * hat_one, axis=-1, keepdims=True))
    ).astype(BF)
    return (
        layer_out,
        tokens_grad,
        norm_one_grad,
        query_grad,
        key_grad,
        value_grad,
        dense_total[:, :1024],
        dense_total[:, 1056],
        dense_total[:, 1024:1056],
        expert_total,
    )


def solution(mesh):
    return jax.shard_map(
        per_device,
        mesh=mesh,
        in_specs=(
            P(("shard", "replica"), None),
            P("shard"),
            P("shard", None),
            P("shard", None),
            P("shard", None),
            P("shard", None),
            P("shard"),
            P("shard", None),
            P("shard", None, None, None),
            P(("shard", "replica"), None),
            P(("shard", "replica")),
            P(("shard", "replica"), None),
        ),
        out_specs=(
            P(("shard", "replica"), None),
            P(("shard", "replica"), None),
            P("shard"),
            P("shard", None),
            P("shard", None),
            P("shard", None),
            P("shard", None),
            P("shard"),
            P("shard", None),
            P("shard", None, None, None),
        ),
        check_vma=False,
    )
```

time: 1470 us -> 701 us (0.48)
  waiting for transfers between devices: 857 us -> 337 us
  blocking collectives: 178 us -> 14 us
  local copies, waits for them, and re-layouts: 166 us -> 84.2 us
  matrix products: 162 us -> 86 us
  starting transfers between devices: 19.7 us -> 57.1 us
  Pallas kernels: 0 us -> 26.5 us
    reduce_scatter x4 -> x0, waiting for transfers between devices: 234 us -> none  [the longest x1 65 us: per_device(): lax.psum_scatter(query_weight_grad.astype(jnp.bfloat16), 'shard', scatter...]
    all_to_all x4 -> x11, waiting for transfers between devices: 84.2 us -> 305 us  [split_all(): return lax.all_to_all(x, axis, 0, 0, tiled=True)]
    psum x1 -> x0, waiting for transfers between devices: 207 us -> none  [per_device(): lax.psum(expert_grad.astype(jnp.bfloat16), 'replica').astype(jnp.float32)]
    unnamed x16 -> x4, waiting for transfers between devices: 123 us -> 0.07 us
    all_gather x6 -> x4, waiting for transfers between devices: 135 us -> 31.4 us  [the longest x1 31.4 us: per_device(): rows_all = lax.all_gather(rows_out, 'shard', axis=0, tiled=True)]
    unnamed x3 -> x0, blocking collectives: 87.1 us -> none
    dot_general x51 -> x26, matrix products: 162 us -> 86 us  [the longest x9 56.3 us: per_device(): bmm = lambda text, a, b: jnp.einsum(text, a, b, preferred_element_type=F32)]
    reshape x1 -> x0, waiting for transfers between devices: 73.9 us -> none  [per_device(): value_here.astype(jnp.bfloat16).reshape(row_count, KVH * HD)]
  transfers between devices with their start and end apart: 18 -> 15, of which waited for: 15 -> 12; matrix products, arithmetic and copies ran while one was open for 16% -> 22% of each run, Pallas kernels for 0% -> 4%
where the time goes in v1:
time: 701 us; the launch traced here: 689 us
  waiting for transfers between devices  337 us (48%)
  matrix products  86 us (12%)
  local copies, waits for them, and re-layouts  84.2 us (12%)
  other arithmetic  67.6 us (10%)
  starting transfers between devices  57.1 us (8%)
  Pallas kernels  26.5 us (4%)
  between operations  16.6 us (2%)
  blocking collectives  14 us (2%)
    all_to_all x11, waiting for transfers between devices, split_all(): return lax.all_to_all(x, axis, 0, 0, tiled=True)  305 us
    all_to_all x11, starting transfers between devices, split_all(): return lax.all_to_all(x, axis, 0, 0, tiled=True)  56.9 us
    dot_general x9, matrix products, per_device(): bmm = lambda text, a, b: jnp.einsum(text, a, b, preferred_element_type=F32)  56.3 us
    all_gather x1, waiting for transfers between devices, per_device(): rows_all = lax.all_gather(rows_out, 'shard', axis=0, tiled=True)  31.4 us
    dot_general x15, matrix products, mm(): return lax.dot_general(a, b, dims, preferred_element_type=F32)  27.2 us
    unnamed x122, local copies, waits for them, and re-layouts  15.4 us
    pallas_call x1, Pallas kernels, attend_back(): pl.pallas_call(attend_back_kernel, grid=(NQ,), in_specs=[block, whole(HD)...  15.4 us
  transfers between devices with their start and end apart: 15, of which 12 were waited for; matrix products, arithmetic and copies ran while one was open for 22% of the time, Pallas kernels for 4%

profile of v1, /device:TPU:0, one launch (start us, length us, event | category | flops | bytes accessed | tf_op | source)
XLA Modules:
  0.0 688.9 jit_solution(13761163152528865446)
XLA Ops:
  20.4 7.0 %all-to-all-start = ((bf16[8,208,1024]{2,1,0:T(8,128)(2,1)}), bf16[8,208,1024]{2,1,0:T(8,128)(2,1)}, u32[]{:S(2)}, u32[]{:S(2)}) async-start(bf16[8,208,1024]{2,1,0:T(8,128)(2,1)} %broadcast_in_dim.136), calls=%async_computation | async-start | bytes 6815744 | tf_op jit(solution)/shard_map/all_to_all | solution.py:37
  38.4 39.1 %all-to-all-done = bf16[8,208,1024]{2,1,0:T(8,128)(2,1)} async-done(((bf16[8,208,1024]{2,1,0:T(8,128)(2,1)}), bf16[8,208,1024]{2,1,0:T(8,128)(2,1)}, u32[]{:S(2)}, u32[]{:S(2)}) %all-to-all-start) | async-done | bytes 3407904 | tf_op jit(solution)/shard_map/all_to_all | solution.py:37
  85.1 5.3 slice_convert_fusion
  118.2 11.1 %shard_map.195 = (bf16[1536,128]{1,0:T(8,128)(2,1)S(1)}, f32[6,1,512]{2,1,0:T(1,128)S(1)}) custom-call(bf16[1536,128]{1,0:T(8,128)(2,1)S(1)} %multiply_convert_fusion.4.q_ref, bf16[1536,64]{1,0:T(8,128)(2,1)S(1)} %slice.147.k_ref, bf16[1536,64]{1,0:T(8,128)(2,1)S(1)} %copy.314.v_ref, s32[6,1,256]{2,1,0:T(1,128)S(1)} %select_n.96.start_ref), custom_call_target="tpu_custom_call" | custom-call | tf_op jit(solution)/shard_map/pallas_call | solution.py:89
  129.4 14.0 %all_to_all.60 = bf16[8,192,128]{2,1,0:T(8,128)(2,1)S(1)} all-to-all(bf16[8,192,128]{2,1,0:T(8,128)(2,1)S(1)} %bitcast.177), channel_id=1, replica_groups=mesh['shard'=16,'replica'=8] {'replica'}, dimensions={0} | all-to-all | bytes 786432 | tf_op jit(solution)/shard_map/all_to_all | solution.py:37
  163.8 31.4 %all-gather.7.cloned.1.call-done = bf16[3072,1152]{1,0:T(8,128)(2,1)} async-done(((bf16[192,1152]{1,0:T(8,128)(2,1)}), bf16[3072,1152]{1,0:T(8,128)(2,1)}) %all-gather.7.cloned.1.call-update) | async-done | bytes 7077904 | tf_op jit(solution)/shard_map/all_gather | solution.py:311
  199.7 7.5 %fusion.12 = f32[2,1024,512]{2,1,0:T(8,128)} fusion(bf16[2,1024,1024]{2,1,0:T(8,128)(2,1)S(1)} %bitcast.192, bf16[2,3,1024,512]{3,2,1,0:T(8,128)(2,1)} %param.20), kind=kOutput, calls=%fused_computation.28 | convolution fusion | flops 2147483648 | bytes 10485760 | tf_op jit(solution)/shard_map/erd,edf->erf/dot_general | solution.py:340
  207.2 6.1 fusion.15
  222.3 10.1 %multiply_convert_fusion = (bf16[2,1024,512]{2,1,0:T(8,128)(2,1)}, bf16[2,1024,512]{2,1,0:T(8,128)(2,1)}, bf16[2,1024,512]{2,1,0:T(8,128)(2,1)S(1)}) fusion(f32[2,1024,512]{2,1,0:T(8,128)S(1)} %copy-done.52, f32[2,1024,512]{2,1,0:T(8,128)} %fusion.15, bf16[2,1024,1024]{2,1,0:T(8,128)(2,1)S(1)} %fusion, bf16[2,3,1024,512]{3,2,1,0:T(8,128)(2,1)} %param.20), kind=kOutput, calls=%fused_computation.16 | convolution fusion | flops 2163212288 | bytes 20971520 | tf_op jit(solution)/shard_map/erd,edf->erf/dot_general | solution.py:340
  232.4 6.8 fusion.1
  257.6 48.4 %all-to-all-done.3 = bf16[16,2,64,1024]{3,2,1,0:T(8,128)(2,1)} async-done(((bf16[16,2,64,1024]{3,2,1,0:T(8,128)(2,1)}), bf16[16,2,64,1024]{3,2,1,0:T(8,128)(2,1)}, u32[]{:S(2)}, u32[]{:S(2)}) %all-to-all-start.3) | async-done | bytes 4194336 | tf_op jit(solution)/shard_map/all_to_all | solution.py:37
  317.4 6.4 all-to-all-start.4
  343.5 15.4 %shard_map.196 = (bf16[1536,128]{1,0:T(8,128)(2,1)S(1)}, bf16[1536,128]{1,0:T(8,128)(2,1)S(1)}) custom-call(bf16[1536,128]{1,0:T(8,128)(2,1)S(1)} %multiply_convert_fusion.4.q_ref, bf16[1536,64]{1,0:T(8,128)(2,1)S(1)} %slice.147.k_ref, bf16[1536,64]{1,0:T(8,128)(2,1)S(1)} %copy.314.v_ref, bf16[1536,128]{1,0:T(8,128)(2,1)S(1)} %bitcast.176, ...), custom_call_target="tpu_custom_call" | custom-call | tf_op jit(solution)/shard_map/pallas_call | solution.py:183
  361.0 27.6 %all-to-all-done.2 = bf16[16,2,64,1024]{3,2,1,0:T(8,128)(2,1)} async-done(((bf16[16,2,64,1024]{3,2,1,0:T(8,128)(2,1)}), bf16[16,2,64,1024]{3,2,1,0:T(8,128)(2,1)}, u32[]{:S(2)}, u32[]{:S(2)}) %all-to-all-start.2) | async-done | bytes 4194336 | tf_op jit(solution)/shard_map/all_to_all | solution.py:37
  407.4 6.6 convert_bitcast_fusion.2
  414.0 24.0 %all-to-all-done.7 = bf16[16,64,1152]{2,1,0:T(8,128)(2,1)S(1)} async-done(((bf16[16,64,1152]{2,1,0:T(8,128)(2,1)}), bf16[16,64,1152]{2,1,0:T(8,128)(2,1)S(1)}, u32[]{:S(2)}, u32[]{:S(2)}) %all-to-all-start.7) | async-done | bytes 2359328 | tf_op jit(solution)/shard_map/all_to_all | solution.py:37
  442.5 6.7 convert_bitcast_fusion.3
  455.9 5.2 all-to-all-start.8
  469.1 6.5 all-to-all-start.10
  477.7 85.1 %all-to-all-done.10 = bf16[8,768,512]{2,1,0:T(8,128)(2,1)} async-done(((bf16[8,768,512]{2,1,0:T(8,128)(2,1)}), bf16[8,768,512]{2,1,0:T(8,128)(2,1)}, u32[]{:S(2)}, u32[]{:S(2)}) %all-to-all-start.10) | async-done | bytes 6291488 | tf_op jit(solution)/shard_map/all_to_all | solution.py:37
  572.0 5.8 all-to-all-done.9
  581.1 5.2 all-to-all-start.11
  607.5 65.1 %all-to-all-done.11 = bf16[8,768,512]{2,1,0:T(8,128)(2,1)} async-done(((bf16[8,768,512]{2,1,0:T(8,128)(2,1)}), bf16[8,768,512]{2,1,0:T(8,128)(2,1)}, u32[]{:S(2)}, u32[]{:S(2)}) %all-to-all-start.11) | async-done | bytes 6291488 | tf_op jit(solution)/shard_map/all_to_all | solution.py:37
  672.6 9.3 %convert.55 = f32[2,3,1024,512]{3,2,1,0:T(8,128)} convert(bf16[2,3,1024,512]{3,2,1,0:T(8,128)(2,1)} %bitcast.63) | non-fusion elementwise | flops 3145728 | bytes 18874368 | tf_op jit(solution)/shard_map/convert_element_type | solution.py:372
  (288 shorter events, 216.4 us)
Async XLA Ops:
  7.2 83.2 %all-gather.5.cloned.1.call-start = ((), (), s32[]{:S(2)}) async-start(), calls=%async_computation.12 | async-start | bytes 3063808 | tf_op jit(solution)/shard_map/all_gather | solution.py:259
  12.8 138.0 %all-gather.9.cloned.1.call-start = ((), (), s32[]{:S(2)}) async-start(), calls=%async_computation.14 | async-start | bytes 7520256 | tf_op jit(solution)/shard_map/all_gather | solution.py:270
  20.4 57.1 %all-to-all-start = ((bf16[8,208,1024]{2,1,0:T(8,128)(2,1)}), bf16[8,208,1024]{2,1,0:T(8,128)(2,1)}, u32[]{:S(2)}, u32[]{:S(2)}) async-start(bf16[8,208,1024]{2,1,0:T(8,128)(2,1)} %broadcast_in_dim.136), calls=%async_computation | async-start | bytes 6815744 | tf_op jit(solution)/shard_map/all_to_all | solution.py:37
  27.4 167.7 %all-gather.7.cloned.1.call-start = ((), (), s32[]{:S(2)}) async-start(), calls=%async_computation.13 | async-start | bytes 7520256 | tf_op jit(solution)/shard_map/all_gather | solution.py:311
  111.9 31.4 %copy-start.12 = (bf16[192,1024]{1,0:T(8,128)(2,1)S(1)}, bf16[192,1024]{1,0:T(8,128)(2,1)}, u32[]{:S(2)}) copy-start(bf16[192,1024]{1,0:T(8,128)(2,1)} %param.12) | copy-start | bytes 1179652
  117.0 30.6 %copy-start.25 = (bf16[1024,1408]{1,0:T(8,128)(2,1)S(1)}, bf16[1024,1408]{1,0:T(8,128)(2,1)}, u32[]{:S(2)}) copy-start(bf16[1024,1408]{1,0:T(8,128)(2,1)} %all-gather.5.cloned.1.call-done) | copy-start | bytes 8650756
  250.5 55.6 %all-to-all-start.3 = ((bf16[16,2,64,1024]{3,2,1,0:T(8,128)(2,1)}), bf16[16,2,64,1024]{3,2,1,0:T(8,128)(2,1)}, u32[]{:S(2)}, u32[]{:S(2)}) async-start(bf16[16,2,64,1024]{3,2,1,0:T(8,128)(2,1)} %fusion.6), calls=%async_computation.3 | async-start | bytes 8388608 | tf_op jit(solution)/shard_map/all_to_all | solution.py:37
  255.6 57.7 %copy-start.3 = (f32[192,1024]{1,0:T(8,128)S(1)}, f32[192,1024]{1,0:T(8,128)}, u32[]{:S(2)}) copy-start(f32[192,1024]{1,0:T(8,128)} %copy-done.2) | copy-start | bytes 2359300
  317.4 15.9 %all-to-all-start.4 = ((bf16[8,192,128]{2,1,0:T(8,128)(2,1)}), bf16[8,192,128]{2,1,0:T(8,128)(2,1)S(1)}, u32[]{:S(2)}, u32[]{:S(2)}) async-start(bf16[8,192,128]{2,1,0:T(8,128)(2,1)} %bitcast.175), calls=%async_computation.4 | async-start | bytes 786432 | tf_op jit(solution)/shard_map/all_to_all | solution.py:37
  333.3 55.2 %all-to-all-start.2 = ((bf16[16,2,64,1024]{3,2,1,0:T(8,128)(2,1)}), bf16[16,2,64,1024]{3,2,1,0:T(8,128)(2,1)}, u32[]{:S(2)}, u32[]{:S(2)}) async-start(bf16[16,2,64,1024]{3,2,1,0:T(8,128)(2,1)} %bitcast.185), calls=%async_computation.2 | async-start | bytes 8388608 | tf_op jit(solution)/shard_map/all_to_all | solution.py:37
  359.1 33.9 %copy-start.20 = (bf16[1536,256]{1,0:T(8,128)(2,1)}, bf16[1536,256]{1,0:T(8,128)(2,1)S(1)}, u32[]{:S(2)}) copy-start(bf16[1536,256]{1,0:T(8,128)(2,1)S(1)} %constant_dynamic-update-slice_fusion) | copy-start | bytes 2359300
  359.1 33.7 %copy-start.8 = (bf16[192,1024]{1,0:T(8,128)(2,1)S(1)}, bf16[192,1024]{1,0:T(8,128)(2,1)}, u32[]{:S(2)}) copy-start(bf16[192,1024]{1,0:T(8,128)(2,1)} %copy-done.7) | copy-start | bytes 1179652
  359.1 33.7 %copy-start.41 = (bf16[192,32]{0,1:T(8,128)(2,1)S(1)}, bf16[192,32]{0,1:T(8,128)(2,1)}, u32[]{:S(2)}) copy-start(bf16[192,32]{0,1:T(8,128)(2,1)} %copy-done.40) | copy-start | bytes 36868
  359.1 34.5 %copy-start.6 = (f32[192,1024]{1,0:T(8,128)S(1)}, f32[192,1024]{1,0:T(8,128)}, u32[]{:S(2)}) copy-start(f32[192,1024]{1,0:T(8,128)} %copy-done.5) | copy-start | bytes 2359300
  388.5 15.1 %all-to-all-start.6 = ((bf16[16,64,256]{2,1,0:T(8,128)(2,1)}), bf16[16,64,256]{2,1,0:T(8,128)(2,1)}, u32[]{:S(2)}, u32[]{:S(2)}) async-start(bf16[16,64,256]{2,1,0:T(8,128)(2,1)} %bitcast.43), calls=%async_computation.6 | async-start | bytes 1048576 | tf_op jit(solution)/shard_map/all_to_all | solution.py:37
  403.7 34.4 %all-to-all-start.7 = ((bf16[16,64,1152]{2,1,0:T(8,128)(2,1)}), bf16[16,64,1152]{2,1,0:T(8,128)(2,1)S(1)}, u32[]{:S(2)}, u32[]{:S(2)}) async-start(bf16[16,64,1152]{2,1,0:T(8,128)(2,1)} %concatenate.54), calls=%async_computation.7 | async-start | bytes 4718592 | tf_op jit(solution)/shard_map/all_to_all | solution.py:37
  438.1 17.9 %all-to-all-start.5 = ((bf16[8,192,256]{2,1,0:T(8,128)(2,1)}), bf16[8,192,256]{2,1,0:T(8,128)(2,1)}, u32[]{:S(2)}, u32[]{:S(2)}) async-start(bf16[8,192,256]{2,1,0:T(8,128)(2,1)} %bitcast.199), calls=%async_computation.5 | async-start | bytes 1572864 | tf_op jit(solution)/shard_map/all_to_all | solution.py:37
  455.9 13.2 %all-to-all-start.8 = ((bf16[8,8,1152]{2,1,0:T(8,128)(2,1)}), bf16[8,8,1152]{2,1,0:T(8,128)(2,1)S(1)}, u32[]{:S(2)}, u32[]{:S(2)}) async-start(bf16[8,8,1152]{2,1,0:T(8,128)(2,1)} %bitcast.48), calls=%async_computation.8 | async-start | bytes 294912 | tf_op jit(solution)/shard_map/all_to_all | solution.py:37
  469.1 93.7 %all-to-all-start.10 = ((bf16[8,768,512]{2,1,0:T(8,128)(2,1)}), bf16[8,768,512]{2,1,0:T(8,128)(2,1)}, u32[]{:S(2)}, u32[]{:S(2)}) async-start(bf16[8,768,512]{2,1,0:T(8,128)(2,1)} %bitcast.180), calls=%async_computation.10 | async-start | bytes 12582912 | tf_op jit(solution)/shard_map/all_to_all | solution.py:37
  475.7 120.5 %all-gather.11.cloned.1.call-start = ((), (), s32[]{:S(2)}) async-start(), calls=%async_computation.15 | async-start | bytes 4456448 | tf_op jit(solution)/shard_map/all_gather | solution.py:437
  563.6 14.2 %all-to-all-start.9 = ((bf16[8,208,128]{2,1,0:T(8,128)(2,1)}), bf16[8,208,128]{2,1,0:T(8,128)(2,1)S(1)}, u32[]{:S(2)}, u32[]{:S(2)}) async-start(bf16[8,208,128]{2,1,0:T(8,128)(2,1)} %broadcast_in_dim.158), calls=%async_computation.9 | async-start | bytes 851968 | tf_op jit(solution)/shard_map/all_to_all | solution.py:37
  581.1 91.5 %all-to-all-start.11 = ((bf16[8,768,512]{2,1,0:T(8,128)(2,1)}), bf16[8,768,512]{2,1,0:T(8,128)(2,1)}, u32[]{:S(2)}, u32[]{:S(2)}) async-start(bf16[8,768,512]{2,1,0:T(8,128)(2,1)} %broadcast_in_dim.159), calls=%async_computation.11 | async-start | bytes 12582912 | tf_op jit(solution)/shard_map/all_to_all | solution.py:37
  604.3 77.7 %copy-start.31 = (f32[64,512]{1,0:T(8,128)}, f32[64,512]{1,0:T(8,128)S(1)}, u32[]{:S(2)}) copy-start(f32[64,512]{1,0:T(8,128)S(1)} %reshape.426) | copy-start | bytes 393220
  604.6 77.4 %copy-start.32 = (f32[64,512]{1,0:T(8,128)}, f32[64,512]{1,0:T(8,128)S(1)}, u32[]{:S(2)}) copy-start(f32[64,512]{1,0:T(8,128)S(1)} %reshape.425) | copy-start | bytes 393220
  (51 other events, 274.1 us)
Sparse Core Ops, SparseCore 0:
  12.9 67.2 all-gather.4
  81.9 47.5 all-gather.8
  150.8 44.2 all-gather.6
  478.5 86.8 all-gather.10

commit v2 on v1

v2 whole, which is shorter than its diff:
```python
import jax
import jax.numpy as jnp
from jax import lax
from jax.experimental import pallas as pl
from jax.experimental.pallas import tpu as pltpu
from jax.sharding import PartitionSpec as P

D = 1024
H = 16
KVH = 8
HD = 64
FF = 512
E = 32
TOP = 8
SEQ = 1536
TOK = 192
NS = 16
NR = 8
SLOTS = 64
QB = 256
NQ = SEQ // QB
EPSILON = 1e-06
MASKED = -1e30
SCALE = HD ** (-0.5)
BLOCKS = 4
CHUNKS = NS // BLOCKS
CHUNK_ROWS = BLOCKS * SLOTS
VMEM = 56 * 1024 * 1024
BF = jnp.bfloat16
F32 = jnp.float32

NT = (((1,), (1,)), ((), ()))
TN = (((0,), (0,)), ((), ()))


def mm(a, b, dims=(((1,), (0,)), ((), ()))):
    return lax.dot_general(a, b, dims, preferred_element_type=F32)


def split_all(x, axis):
    return lax.all_to_all(x, axis, 0, 0, tiled=True)


def spread_all(x, axis, count):
    return split_all(jnp.broadcast_to(x[None], (count,) + x.shape), axis)


def stacked_heads(block):
    return jnp.concatenate([block[:, :HD], block[:, HD:]], axis=0)


def allowed_keys(key_block, query_block, start_row):
    key_index = lax.broadcasted_iota(jnp.int32, (QB, 2 * QB), 0) + key_block * QB
    column = lax.broadcasted_iota(jnp.int32, (1, 2 * QB), 1)
    query_row = jnp.where(column >= QB, column - QB, column) + query_block * QB
    return (key_index >= start_row) & (key_index <= query_row)


def rotary_swap(value):
    lane = lax.broadcasted_iota(jnp.int32, value.shape, 1) % HD
    width = value.shape[1]
    return jnp.where(
        lane < HD // 2,
        pltpu.roll(value, width - HD // 2, 1),
        pltpu.roll(value, HD // 2, 1),
    )


def project_kernel(tokens_ref, weight_ref, small_ref, cos_ref, sin_ref, qkv_ref, normed_ref, gains_ref):
    @pl.when(pl.program_id(0) == 0)
    def norm():
        gains = small_ref[...].astype(F32).T[32:40]
        gains_ref[...] = gains
        wide = tokens_ref[...].astype(F32)
        inverse = lax.rsqrt(jnp.mean(wide * wide, axis=-1, keepdims=True) + EPSILON)
        normed_ref[...] = (wide * inverse * gains[0:1]).astype(BF)

    raw = mm(normed_ref[...], weight_ref[...])
    qkv_ref[0] = (raw * cos_ref[...] + rotary_swap(raw) * sin_ref[...]).astype(BF)


def project(tokens, gathered, cos, sin):
    fixed = lambda rows, width, at: pl.BlockSpec((rows, width), lambda g: (0, at))
    return pl.pallas_call(
        project_kernel,
        grid=(NR,),
        in_specs=[
            fixed(TOK, D, 0),
            pl.BlockSpec((D, 256), lambda g: (0, g)),
            fixed(D, 128, 24),
            fixed(TOK, 256, 0),
            fixed(TOK, 256, 0),
        ],
        out_specs=[
            pl.BlockSpec((1, TOK, 256), lambda g: (g, 0, 0)),
            fixed(TOK, D, 0),
            fixed(8, D, 0),
        ],
        out_shape=[
            jax.ShapeDtypeStruct((NR, TOK, 256), BF),
            jax.ShapeDtypeStruct((TOK, D), BF),
            jax.ShapeDtypeStruct((8, D), F32),
        ],
        compiler_params=pltpu.CompilerParams(vmem_limit_bytes=VMEM),
    )(tokens, gathered, gathered, cos, sin)


def attend_kernel(q_ref, kv_ref, start_ref, out_ref, lse_ref):
    i = pl.program_id(0)
    q2 = stacked_heads(q_ref[...])
    start_row = jnp.concatenate([start_ref[0], start_ref[0]], axis=1)

    def step(j, carry):
        largest, summed, total = carry
        kv = kv_ref[pl.ds(pl.multiple_of(j * QB, QB), QB), :]
        scores = mm(kv[:, :HD], q2, NT)
        scores = jnp.where(allowed_keys(j, i, start_row), scores, MASKED)
        newest = jnp.maximum(largest, jnp.max(scores, axis=0, keepdims=True))
        chances = jnp.exp(scores - newest)
        factor = jnp.exp(largest - newest)
        summed = summed * factor + jnp.sum(chances, axis=0, keepdims=True)
        total = total * factor + mm(kv[:, HD:], chances.astype(BF), TN)
        return (newest, summed, total)

    largest, summed, total = lax.fori_loop(
        0,
        i + 1,
        step,
        (
            jnp.full((1, 2 * QB), MASKED, F32),
            jnp.zeros((1, 2 * QB), F32),
            jnp.zeros((HD, 2 * QB), F32),
        ),
    )
    total = total / summed
    out_ref[...] = jnp.concatenate([total[:, :QB], total[:, QB:]], axis=0).T.astype(BF)
    lse_ref[0] = largest + jnp.log(summed)


def attend(qkv, start):
    return pl.pallas_call(
        attend_kernel,
        grid=(NQ,),
        in_specs=[
            pl.BlockSpec((QB, 2 * HD), lambda i: (i, 0)),
            pl.BlockSpec((SEQ, 2 * HD), lambda i: (0, 1)),
            pl.BlockSpec((1, 1, QB), lambda i: (i, 0, 0)),
        ],
        out_specs=[
            pl.BlockSpec((QB, 2 * HD), lambda i: (i, 0)),
            pl.BlockSpec((1, 1, 2 * QB), lambda i: (i, 0, 0)),
        ],
        out_shape=[
            jax.ShapeDtypeStruct((SEQ, 2 * HD), BF),
            jax.ShapeDtypeStruct((NQ, 1, 2 * QB), F32),
        ],
        compiler_params=pltpu.CompilerParams(vmem_limit_bytes=VMEM),
    )(qkv, qkv, start)


def attend_back_kernel(
    q_ref,
    kv_ref,
    grad_ref,
    start_ref,
    lse_ref,
    cos_t_ref,
    sin_t_ref,
    cos_ref,
    sin_ref,
    out_ref,
    chances_ref,
    pressure_ref,
    dk_ref,
    dv_ref,
):
    i = pl.program_id(0)

    @pl.when(i == 0)
    def clear():
        dk_ref[...] = jnp.zeros_like(dk_ref)
        dv_ref[...] = jnp.zeros_like(dv_ref)

    q2 = stacked_heads(q_ref[...])
    grad2 = stacked_heads(grad_ref[...])
    start_row = jnp.concatenate([start_ref[0], start_ref[0]], axis=1)
    lse = lse_ref[0]

    def first(j, delta):
        rows = pl.ds(pl.multiple_of(j * QB, QB), QB)
        kv = kv_ref[rows, :]
        scores = mm(kv[:, :HD], q2, NT)
        chances = jnp.where(allowed_keys(j, i, start_row), jnp.exp(scores - lse), 0.0)
        pressure = mm(kv[:, HD:], grad2, NT)
        chances_ref[rows, :] = chances
        pressure_ref[rows, :] = pressure
        return delta + jnp.sum(chances * pressure, axis=0, keepdims=True)

    delta = lax.fori_loop(0, i + 1, first, jnp.zeros((1, 2 * QB), F32))

    def second(j, total):
        rows = pl.ds(pl.multiple_of(j * QB, QB), QB)
        chances = chances_ref[rows, :]
        score_grad = (chances * (pressure_ref[rows, :] - delta)).astype(BF)
        dv_ref[rows, :] += mm(chances.astype(BF), grad2)
        dk_ref[rows, :] += mm(score_grad, q2)
        return total + mm(kv_ref[rows, :HD], score_grad, TN)

    total = lax.fori_loop(0, i + 1, second, jnp.zeros((HD, 2 * QB), F32)) * SCALE
    cosine, sine = cos_t_ref[...], sin_t_ref[...]
    half = HD // 2
    parts = []
    for head in range(2):
        front = total[:half, head * QB : (head + 1) * QB]
        back = total[half:, head * QB : (head + 1) * QB]
        parts += [front * cosine + back * sine, back * cosine - front * sine]
    query_rows = pl.ds(pl.multiple_of(i * QB, QB), QB)
    out_ref[query_rows, : 2 * HD] = jnp.concatenate(parts, axis=0).T.astype(BF)

    @pl.when(i == NQ - 1)
    def finish():
        for j in range(NQ):
            rows = slice(j * QB, (j + 1) * QB)
            dk = dk_ref[rows, :]
            swapped = jnp.concatenate([dk[:, half:], dk[:, :half]], axis=1)
            dk = dk * cos_ref[rows, :] - swapped * sin_ref[rows, :]
            out_ref[rows, 2 * HD :] = jnp.concatenate([dk, dv_ref[rows, :]], axis=1).astype(BF)


def attend_back(qkv, grad, start, lse, cos_t, sin_t, cos, sin):
    whole = lambda width, at: pl.BlockSpec((SEQ, width), lambda i: (0, at))
    block = pl.BlockSpec((QB, 2 * HD), lambda i: (i, 0))
    table = pl.BlockSpec((HD // 2, QB), lambda i: (0, i))
    return pl.pallas_call(
        attend_back_kernel,
        grid=(NQ,),
        in_specs=[
            block,
            whole(2 * HD, 1),
            block,
            pl.BlockSpec((1, 1, QB), lambda i: (i, 0, 0)),
            pl.BlockSpec((1, 1, 2 * QB), lambda i: (i, 0, 0)),
            table,
            table,
            whole(HD, 0),
            whole(HD, 0),
        ],
        out_specs=whole(4 * HD, 0),
        out_shape=jax.ShapeDtypeStruct((SEQ, 4 * HD), BF),
        scratch_shapes=[
            pltpu.VMEM((SEQ, 2 * QB), F32),
            pltpu.VMEM((SEQ, 2 * QB), F32),
            pltpu.VMEM((SEQ, HD), F32),
            pltpu.VMEM((SEQ, HD), F32),
        ],
        compiler_params=pltpu.CompilerParams(vmem_limit_bytes=VMEM),
    )(qkv, qkv, grad, start, lse, cos_t, sin_t, cos, sin)


def hi_lo(value):
    high = value.astype(BF).astype(F32)
    rest = value - high
    middle = rest.astype(BF).astype(F32)
    return high, middle, (rest - middle).astype(BF).astype(F32)


def route_kernel(
    mixed_ref, tokens_ref, out_ref, small_ref, gains_ref, chosen_ref, middle_ref, rows_ref, gates_ref
):
    mixed = jnp.concatenate([mixed_ref[g] for g in range(NR)], axis=1)
    middle = tokens_ref[...].astype(F32) + mm(mixed, out_ref[...])
    middle_ref[...] = middle
    inverse = lax.rsqrt(jnp.mean(middle * middle, axis=-1, keepdims=True) + EPSILON)
    normed = (middle * inverse * gains_ref[1:2, :]).astype(BF)
    rows_ref[:, :D] = normed
    chosen = chosen_ref[...] > 0.0
    logits = jnp.where(chosen, mm(normed, small_ref[...]), MASKED)
    powers = jnp.exp(logits - jnp.max(logits, axis=-1, keepdims=True))
    powers = jnp.where(chosen, powers, 0.0)
    gates = powers / jnp.sum(powers, axis=-1, keepdims=True)
    gates_ref[...] = gates
    high, middle_part, low = hi_lo(gates)
    rows_ref[:, D:] = (high + pltpu.roll(middle_part, 32, 1) + pltpu.roll(low, 64, 1)).astype(BF)


def route(mixed, tokens, gathered, gains, chosen):
    fixed = lambda rows, width, at: pl.BlockSpec((rows, width), lambda i: (0, at))
    return pl.pallas_call(
        route_kernel,
        grid=(1,),
        in_specs=[
            pl.BlockSpec((NR, TOK, 128), lambda i: (0, 0, 0)),
            fixed(TOK, D, 0),
            fixed(D, D, 2),
            fixed(D, 128, 24),
            fixed(8, D, 0),
            fixed(TOK, 128, 0),
        ],
        out_specs=[fixed(TOK, D, 0), fixed(TOK, D + 128, 0), fixed(TOK, 128, 0)],
        out_shape=[
            jax.ShapeDtypeStruct((TOK, D), F32),
            jax.ShapeDtypeStruct((TOK, D + 128), BF),
            jax.ShapeDtypeStruct((TOK, 128), F32),
        ],
        compiler_params=pltpu.CompilerParams(vmem_limit_bytes=VMEM),
    )(mixed, tokens, gathered, gathered, gains, chosen)


def expert_kernel(
    rows_ref,
    cot_ref,
    slots_ref,
    own_ref,
    weight_ref,
    combined_ref,
    back_ref,
    grad_ref,
    x_ref,
    g_ref,
    hidden_ref,
    dgate_ref,
    dup_ref,
):
    step = pl.program_id(0)

    @pl.when(step < CHUNKS)
    def forward_backward():
        row_index = lax.broadcasted_iota(jnp.int32, (SLOTS, 128), 0)
        lane_index = lax.broadcasted_iota(jnp.int32, (SLOTS, 128), 1)
        slot_index = lax.broadcasted_iota(jnp.int32, (SLOTS, TOK), 0).astype(F32)
        x_parts, cot_parts, all_picks, weighted = [[], []], [[], []], [], []
        for b in range(BLOCKS):
            tokens = slice(b * TOK, (b + 1) * TOK)
            picks = jnp.concatenate(
                [(slots_ref[e, 0, b : b + 1, :] == slot_index).astype(F32) for e in range(2)], axis=0
            ).astype(BF)
            all_picks.append(picks)
            picked = mm(picks, rows_ref[tokens, :])
            picked_cot = mm(picks, cot_ref[tokens, :D])
            for e in range(2):
                x_parts[e].append(picked[e * SLOTS : (e + 1) * SLOTS])
                cot_parts[e].append(picked_cot[e * SLOTS : (e + 1) * SLOTS])
        here = pl.ds(pl.multiple_of(step * CHUNK_ROWS, CHUNK_ROWS), CHUNK_ROWS)
        for e in range(2):
            both = jnp.concatenate(x_parts[e], axis=0)
            gates = jnp.sum(both[:, D:] * own_ref[e], axis=1, keepdims=True)
            x = both[:, :D].astype(BF)
            cot = jnp.concatenate(cot_parts[e], axis=0)
            gate_w, up_w, down_w = weight_ref[e, 0], weight_ref[e, 1], weight_ref[e, 2]
            gate = mm(x, gate_w)
            up = mm(x, up_w)
            sigmoid = 1.0 / (1.0 + jnp.exp(-gate))
            silu = gate * sigmoid
            hidden = (silu * up).astype(BF)
            grad_out = (gates * cot).astype(BF)
            grad_hidden = mm(grad_out, down_w)
            grad_gate = (grad_hidden * up * sigmoid * (1.0 + gate * (1.0 - sigmoid))).astype(BF)
            grad_up = (grad_hidden * silu).astype(BF)
            x_ref[e, here, :] = x
            g_ref[e, here, :] = grad_out
            hidden_ref[e, here, :] = hidden
            dgate_ref[e, here, :] = grad_gate
            dup_ref[e, here, :] = grad_up
            produced = mm(hidden, down_w, NT).astype(BF).astype(F32)
            weighted.append((gates * produced).astype(BF))
            gate_grads = jnp.sum(cot * produced, axis=1, keepdims=True)
            grad_in = mm(grad_gate, gate_w, NT) + mm(grad_up, up_w, NT)
            for b in range(BLOCKS):
                block = slice(b * SLOTS, (b + 1) * SLOTS)
                row = jnp.sum(
                    jnp.where(row_index == lane_index, gate_grads[block], 0.0), axis=0, keepdims=True
                )
                spare = jnp.zeros((SLOTS, 128), F32)
                for place, part in enumerate(hi_lo(row)):
                    spare = jnp.where(row_index == 60 + place, part, spare)
                back_ref[b, e, :, :128] = (grad_in[block, :128] + spare).astype(BF)
                back_ref[b, e, :, 128:] = grad_in[block, 128:].astype(BF)
        for b in range(BLOCKS):
            block = slice(b * SLOTS, (b + 1) * SLOTS)
            rows = jnp.concatenate([weighted[0][block], weighted[1][block]], axis=0)
            combined_ref[b % 2, 0, b // 2] = mm(all_picks[b], rows, TN).astype(BF)

    for e in range(2):
        for n, (left, right) in enumerate(((x_ref, dgate_ref), (x_ref, dup_ref), (g_ref, hidden_ref))):

            @pl.when(step == CHUNKS + 3 * e + n)
            def weight_grads(left=left, right=right, e=e):
                grad_ref[0, 0] = mm(left[e], right[e], TN).astype(BF)


def run_experts(rows, cot, slots, own, experts):
    chunk = lambda i: jnp.minimum(i, CHUNKS - 1)
    after = lambda i: jnp.maximum(i - CHUNKS, 0)
    taken = pl.BlockSpec((BLOCKS * TOK, D + 128), lambda i: (chunk(i), 0))
    made = pl.BlockSpec((BLOCKS, 2, SLOTS, D), lambda i: (chunk(i), 0, 0, 0))
    return pl.pallas_call(
        expert_kernel,
        grid=(CHUNKS + 6,),
        in_specs=[
            taken,
            taken,
            pl.BlockSpec((2, 1, BLOCKS, TOK), lambda i: (0, chunk(i), 0, 0)),
            pl.BlockSpec((2, 1, 128), lambda i: (0, 0, 0)),
            pl.BlockSpec((2, 3, D, FF), lambda i: (0, 0, 0, 0), pipeline_mode=pl.Buffered(1)),
        ],
        out_specs=[
            pl.BlockSpec((2, 1, 2, TOK, D), lambda i: (0, chunk(i), 0, 0, 0)),
            made,
            pl.BlockSpec((1, 1, D, FF), lambda i: (after(i) // 3, after(i) % 3, 0, 0)),
        ],
        out_shape=[
            jax.ShapeDtypeStruct((2, 4, 2, TOK, D), BF),
            jax.ShapeDtypeStruct((NS, 2, SLOTS, D), BF),
            jax.ShapeDtypeStruct((2, 3, D, FF), BF),
        ],
        scratch_shapes=[
            pltpu.VMEM((2, NS * SLOTS, D), BF),
            pltpu.VMEM((2, NS * SLOTS, D), BF),
            pltpu.VMEM((2, NS * SLOTS, FF), BF),
            pltpu.VMEM((2, NS * SLOTS, FF), BF),
            pltpu.VMEM((2, NS * SLOTS, FF), BF),
        ],
        compiler_params=pltpu.CompilerParams(vmem_limit_bytes=VMEM),
    )(rows, cot, slots, own, experts)


def token_kernel(
    back_ref,
    spots_ref,
    spread_ref,
    gate_rows_ref,
    gates_ref,
    cot_ref,
    middle_ref,
    normed_ref,
    gains_ref,
    small_ref,
    out_ref,
    mixed_ref,
    middle_grad_ref,
    mixed_grad_ref,
    dense_ref,
):
    spots = spots_ref[...]
    rows = mm(spots, back_ref[...])
    gate_grad = jnp.zeros((TOK, 128), F32)
    for p in range(3):
        gate_grad += mm(spots * gate_rows_ref[p : p + 1, :], spread_ref[...])
    gates = gates_ref[...]
    chosen_grad = gates * (gate_grad - jnp.sum(gates * gate_grad, axis=-1, keepdims=True))
    logit_grad = chosen_grad.astype(BF)
    normed_grad = mm(logit_grad, small_ref[...], NT) + rows
    middle = middle_ref[...]
    inverse = lax.rsqrt(jnp.mean(middle * middle, axis=-1, keepdims=True) + EPSILON)
    hat = middle * inverse
    scaled = normed_grad * gains_ref[1:2, :]
    middle_grad = cot_ref[...].astype(F32) + inverse * (
        scaled - hat * jnp.mean(scaled * hat, axis=-1, keepdims=True)
    )
    middle_grad_ref[...] = middle_grad
    branch = middle_grad.astype(BF)
    mixed_grad = mm(branch, out_ref[...], NT).astype(BF)
    for g in range(NR):
        mixed_grad_ref[g] = mixed_grad[:, g * 128 : (g + 1) * 128]
    gain_grad = jnp.sum(normed_grad * hat, axis=0, keepdims=True)
    lane = lax.broadcasted_iota(jnp.int32, (D, 128), 1)
    gain_column = jnp.broadcast_to(gain_grad, (128, D)).T
    router_grad = mm(normed_ref[...], logit_grad, TN)
    dense_ref[:, D:] = jnp.where(lane == 32, gain_column, router_grad).astype(BF)
    for g in range(NR):
        dense_ref[g * 128 : (g + 1) * 128, :D] = mm(mixed_ref[g], branch, TN).astype(BF)


def token_back(back, spots, spread, gate_rows, gates, cot, middle, rows, gains, gathered, mixed):
    fixed = lambda count, width, at=0: pl.BlockSpec((count, width), lambda i: (0, at))
    return pl.pallas_call(
        token_kernel,
        grid=(1,),
        in_specs=[
            fixed(E * SLOTS, D),
            fixed(TOK, E * SLOTS),
            fixed(E * SLOTS, 128),
            fixed(3, E * SLOTS),
            fixed(TOK, 128),
            fixed(TOK, D),
            fixed(TOK, D),
            fixed(TOK, D),
            fixed(8, D),
            fixed(D, 128, 24),
            fixed(D, D, 2),
            pl.BlockSpec((NR, TOK, 128), lambda i: (0, 0, 0)),
        ],
        out_specs=[
            fixed(TOK, D),
            pl.BlockSpec((NR, TOK, 128), lambda i: (0, 0, 0)),
            fixed(D, D + 128),
        ],
        out_shape=[
            jax.ShapeDtypeStruct((TOK, D), F32),
            jax.ShapeDtypeStruct((NR, TOK, 128), BF),
            jax.ShapeDtypeStruct((D, D + 128), BF),
        ],
        compiler_params=pltpu.CompilerParams(vmem_limit_bytes=VMEM),
    )(back, spots, spread, gate_rows, gates, cot, middle, rows, gains, gathered, gathered, mixed)


def after(value, *others):
    return lax.optimization_barrier((value,) + others)[0]


def heads_kernel(parts_ref, query_ref, key_ref, value_ref, gain_ref, dq_ref, dk_ref, dv_ref, norm_ref):
    total = jnp.zeros((64, 128), F32)
    for pair in range(NR // 2):
        first, second = parts_ref[2 * pair].astype(F32), parts_ref[2 * pair + 1].astype(F32)
        lanes = slice(pair * 128, (pair + 1) * 128)
        for at, part in ((2 * pair, first), (2 * pair + 1, second)):
            wide = slice(at * 128, (at + 1) * 128)
            dq_ref[:, wide] = part[:, :128]
            total += part[:, :128] * query_ref[:, wide].astype(F32)
        dk = jnp.concatenate([first[:, 128:192], second[:, 128:192]], axis=1)
        dv = jnp.concatenate([first[:, 192:], second[:, 192:]], axis=1)
        dk_ref[:, lanes] = dk
        dv_ref[:, lanes] = dv
        total += dk * key_ref[:, lanes].astype(F32) + dv * value_ref[:, lanes].astype(F32)
    norm_ref[...] = jnp.sum(total, axis=1, keepdims=True) / gain_ref[...]


def finish_heads(parts, query_weight, key_matrix, value_matrix, norm_one):
    return pl.pallas_call(
        heads_kernel,
        out_shape=[
            jax.ShapeDtypeStruct((64, 1024), F32),
            jax.ShapeDtypeStruct((64, 512), F32),
            jax.ShapeDtypeStruct((64, 512), F32),
            jax.ShapeDtypeStruct((64, 1), F32),
        ],
    )(parts, query_weight, key_matrix, value_matrix, norm_one.astype(F32)[:, None])


def widen_kernel(place_ref, rows_ref, *refs):
    refs[-1][...] = rows_ref[...].astype(F32)


def widen(rows, place, total=None):
    block = 512
    steps = rows.shape[0] // block
    given = () if total is None else (total,)
    return pl.pallas_call(
        widen_kernel,
        grid_spec=pltpu.PrefetchScalarGridSpec(
            num_scalar_prefetch=1,
            grid=(steps,),
            in_specs=[pl.BlockSpec((block, FF), lambda i, place: (i, 0))]
            + [pl.BlockSpec(memory_space=pl.ANY)] * len(given),
            out_specs=pl.BlockSpec((block, FF), lambda i, place: (place[0] * steps + i, 0)),
        ),
        out_shape=jax.ShapeDtypeStruct((6 * D, FF), F32),
        input_output_aliases={2: 0} if given else {},
    )(jnp.reshape(place, (1,)).astype(jnp.int32), rows, *given)


def exchange(x, bits, axis="replica"):
    return lax.ppermute(x, axis, [(i, i ^ bits) for i in range(lax.axis_size(axis))])


def halves(x, bit):
    half = x.shape[0] // 2
    take = lambda at: lax.dynamic_slice_in_dim(x, at * half, half, 0)
    return take(bit), take(1 - bit)


def in_order(own, other, bit):
    first = jnp.where(bit == 0, own, other)
    return jnp.concatenate([first, jnp.where(bit == 0, other, own)], axis=0)


def add_low(a, b):
    return (a.astype(F32) + b.astype(F32)).astype(BF)


def per_device(
    tokens,
    norm_one,
    query_weight,
    key_matrix,
    value_matrix,
    out_weight,
    norm_two,
    router,
    experts,
    routes,
    segments,
    cotangent,
):
    shard = lax.axis_index("shard")
    replica = lax.axis_index("replica")
    along_x = replica // 2
    side = replica % 2
    low_bit, high_bit = along_x % 2, along_x // 2
    mixed_bit = low_bit ^ high_bit

    grouped = jnp.concatenate(
        [
            query_weight.reshape(64, NR, 128),
            key_matrix.reshape(64, NR, HD),
            value_matrix.reshape(64, NR, HD),
        ],
        axis=2,
    ).reshape(64, 2048)
    small = jnp.concatenate(
        [router, norm_one[:, None], norm_two[:, None], jnp.zeros((64, 94), BF)], axis=1
    )
    gathered = lax.all_gather(
        jnp.concatenate([grouped, out_weight, small], axis=1), "shard", axis=0, tiled=True
    )

    segments_seq = spread_all(segments, "replica", NR).reshape(SEQ)
    first_segment = shard * 3
    count_one = jnp.sum((segments_seq == first_segment).astype(jnp.int32))
    count_two = jnp.sum((segments_seq == first_segment + 1).astype(jnp.int32))
    start = jnp.where(
        segments_seq == first_segment,
        0,
        jnp.where(segments_seq == first_segment + 1, count_one, count_one + count_two),
    ).reshape(NQ, 1, QB)

    chosen = jnp.any(routes[:, :, None] == jnp.arange(128, dtype=jnp.int32), axis=1)
    earlier = jnp.tril(jnp.ones((TOK, TOK), BF), -1)
    slot = jnp.where(chosen, mm(earlier, chosen.astype(BF)), -1.0)
    cot_rows = jnp.concatenate([cotangent, slot.astype(BF)], axis=1)
    cot_all = lax.all_gather(cot_rows, "shard", axis=0, tiled=True)
    spots = slot[:, :E, None] == jnp.arange(SLOTS, dtype=F32)
    spots = spots.astype(BF).reshape(TOK, E * SLOTS)
    spread = (
        jnp.arange(E * SLOTS)[:, None] // SLOTS == jnp.arange(128)[None, :]
    ).astype(BF)

    half = HD // 2
    frequency = 10000.0 ** (-2.0 * jnp.arange(half, dtype=F32) / HD)
    angles = jnp.arange(SEQ, dtype=F32)[:, None] * frequency[None, :]
    cosine, sine = jnp.cos(angles), jnp.sin(angles)
    cos_head = jnp.concatenate([cosine, cosine], axis=1)
    sin_head = jnp.concatenate([-sine, sine], axis=1)
    cos_here = lax.dynamic_slice(cos_head, (replica * TOK, 0), (TOK, HD))
    sin_here = lax.dynamic_slice(sin_head, (replica * TOK, 0), (TOK, HD))
    cos_group = jnp.concatenate(
        [cos_here * SCALE, cos_here * SCALE, cos_here, jnp.ones((TOK, HD), F32)], axis=1
    )
    sin_group = jnp.concatenate(
        [sin_here * SCALE, sin_here * SCALE, sin_here, jnp.zeros((TOK, HD), F32)], axis=1
    )

    tokens_in, start, spots, spread = lax.optimization_barrier((tokens, start, spots, spread))
    qkv_here, normed_one, gains = project(tokens_in, gathered, cos_group, sin_group)
    qkv = split_all(qkv_here, "replica").reshape(SEQ, 256)
    normed_one, qkv = lax.optimization_barrier((normed_one, qkv))
    normed_pair = in_order(normed_one, exchange(normed_one, 1), side)
    mixed_heads, lse = attend(qkv, start)
    mixed = split_all(mixed_heads.reshape(NR, TOK, 128), "replica")
    mixed, normed_pair = lax.optimization_barrier((mixed, normed_pair))
    normed_pairs = [normed_pair] + [exchange(normed_pair, 2 * k) for k in (1, 2, 3)]
    middle, rows_out, gates = route(mixed, tokens, gathered, gains, chosen.astype(F32))

    rows_all = lax.all_gather(rows_out, "shard", axis=0, tiled=True)
    normed_seq = jnp.concatenate(normed_pairs, axis=0)
    own_slots = lax.dynamic_slice(cot_all, (0, D + 2 * shard), (NS * TOK, 2)).astype(F32)
    own_slots = own_slots.T.reshape(2, CHUNKS, BLOCKS, TOK)
    lane = jnp.arange(128)[None, :]
    own = jnp.stack(
        [((lane % E == 2 * shard + e) & (lane < 3 * E)).astype(F32) for e in range(2)]
    )
    combined, grad_in, expert_grad = run_experts(rows_all, cot_all, own_slots, own, experts)
    back = split_all(after(grad_in, normed_seq), "shard")

    rows = expert_grad.reshape(2, 3 * D, FF)
    keep_a, send_a = halves(rows[0], mixed_bit)
    keep_b, send_b = halves(rows[1], high_bit)
    got_a, got_b = exchange(send_a, 2), exchange(send_b, 6)
    keep_a, send_a = halves(add_low(keep_a, got_a), low_bit)
    keep_b, send_b = halves(add_low(keep_b, got_b), low_bit)
    core, row, layer = shard % 2, shard // 2 % 2, shard // 4
    pick = lambda x, at: lax.dynamic_index_in_dim(x, at, 0, keepdims=False)
    from_core = exchange(pick(combined, 1 - core), 1, "shard")
    back, send_a, send_b, from_core = lax.optimization_barrier((back, send_a, send_b, from_core))
    got_a, got_b = exchange(send_a, 6), exchange(send_b, 2)
    sums = add_low(pick(combined, core), from_core)
    keep = [[pick(sums[:, y], layer), pick(sums[:, y], layer ^ step)] for y, step in ((0, 3), (1, 1))]
    send = [
        jnp.stack([pick(sums[:, y], layer ^ first), pick(sums[:, y], layer ^ 2)])
        for y, first in ((0, 1), (1, 3))
    ]
    layers = [exchange(send[0], 4, "shard"), exchange(send[1], 12, "shard")]

    gate_rows = back.reshape(E, SLOTS, D)[:, 60:63, :SLOTS].transpose(1, 0, 2).reshape(3, E * SLOTS)
    middle_grad, mixed_grad, dense = token_back(
        back.reshape(E * SLOTS, D),
        spots,
        spread,
        gate_rows,
        gates,
        cotangent,
        middle,
        rows_out,
        gains,
        gathered,
        mixed,
    )
    grad_heads = split_all(mixed_grad, "replica").reshape(SEQ, 128)
    grad_heads, got_a, got_b, *layers = lax.optimization_barrier((grad_heads, got_a, got_b, *layers))
    keep = [[add_low(keep[y][n], layers[y][n]) for n in range(2)] for y in range(2)]
    layers = [exchange(keep[0][1], 12, "shard"), exchange(keep[1][1], 4, "shard")]
    keep_a, send_a = halves(add_low(keep_a, got_a), side)
    keep_b, send_b = halves(add_low(keep_b, got_b), side)
    got = exchange(jnp.concatenate([send_a, send_b], axis=0), 1)
    head_grad = attend_back(
        qkv, grad_heads, start, lse, cosine.T, sine.T, cos_head, sin_head
    )
    head_grad, got, *layers = lax.optimization_barrier((head_grad, got, *layers))
    sides = [add_low(keep[y][0], layers[y]) for y in range(2)]
    own_side = jnp.where(row == 0, sides[0], sides[1])
    from_side = exchange(jnp.where(row == 0, sides[1], sides[0]), 2, "shard")
    own = add_low(jnp.concatenate([keep_a, keep_b], axis=0), got)
    other = exchange(own, 1)
    half = own.shape[0] // 2
    head_rows = jnp.concatenate(
        [
            lax.dynamic_slice_in_dim(head_grad, (along_x ^ k) * 2 * TOK, 2 * TOK, 0)
            for k in range(4)
        ],
        axis=0,
    )
    heads_grad = mm(normed_seq, head_rows, TN).astype(BF)
    dense_parts = split_all(after(dense, grad_heads).reshape(NS * NR, 8, 1152), ("shard", "replica"))
    dense_sum = jnp.sum(dense_parts.reshape(NS * NR, 8, 1152).astype(F32), axis=0).astype(BF)
    heads_grad = after(heads_grad, dense_parts)
    heads_parts = split_all(heads_grad.reshape(NS, 64, 256), "shard")
    heads_sum = jnp.sum(heads_parts.astype(F32), axis=0).astype(BF)
    head_grad, heads_parts, other = lax.optimization_barrier((head_grad, heads_parts, other))
    own_a, own_b = in_order(own[:half], other[:half], side), in_order(own[half:], other[half:], side)
    other_a, other_b = exchange(own_a, 6), exchange(own_b, 2)

    by_token = split_all(head_grad.reshape(NR, TOK, 256), "replica")
    normed_grad = mm(by_token.transpose(1, 0, 2).reshape(TOK, 2048), gathered[:, :2048], NT)
    tokens_wide = tokens.astype(F32)
    inverse = lax.rsqrt(jnp.mean(tokens_wide * tokens_wide, axis=-1, keepdims=True) + EPSILON)
    hat = tokens_wide * inverse
    scaled = normed_grad * gains[0:1]
    tokens_grad = (
        middle_grad + inverse * (scaled - hat * jnp.mean(scaled * hat, axis=-1, keepdims=True))
    ).astype(BF)

    layer_out = (middle + own_side.astype(F32) + from_side.astype(F32)).astype(BF)

    last = jnp.concatenate([heads_sum.reshape(128, 128), dense_sum.reshape(72, 128)], axis=0)
    last = jnp.pad(last, ((0, 8), (0, 0)))
    last, by_token, other_a, other_b = lax.optimization_barrier((last, by_token, other_a, other_b))
    own_a, own_b = in_order(own_a, other_a, low_bit), in_order(own_b, other_b, low_bit)
    other_a, other_b = exchange(own_a, 2), exchange(own_b, 6)
    last = spread_all(last, "replica", NR)
    query_grad, key_grad, value_grad, norm_one_grad = finish_heads(
        last[:, :128].reshape(NR, 64, 256), query_weight, key_matrix, value_matrix, norm_one
    )
    dense_last = last[:, 128:200].reshape(64, 1152).astype(F32)
    expert_total = widen(own_a, mixed_bit)
    expert_total = widen(own_b, 2 + high_bit, expert_total)
    expert_total = widen(other_a, 1 - mixed_bit, expert_total)
    expert_total = widen(other_b, 3 - high_bit, expert_total).reshape(2, 3, D, FF)
    return (
        layer_out,
        tokens_grad,
        norm_one_grad[:, 0],
        query_grad,
        key_grad,
        value_grad,
        dense_last[:, :1024],
        dense_last[:, 1056],
        dense_last[:, 1024:1056],
        expert_total,
    )


def solution(mesh):
    return jax.shard_map(
        per_device,
        mesh=mesh,
        in_specs=(
            P(("shard", "replica"), None),
            P("shard"),
            P("shard", None),
            P("shard", None),
            P("shard", None),
            P("shard", None),
            P("shard"),
            P("shard", None),
            P("shard", None, None, None),
            P(("shard", "replica"), None),
            P(("shard", "replica")),
            P(("shard", "replica"), None),
        ),
        out_specs=(
            P(("shard", "replica"), None),
            P(("shard", "replica"), None),
            P("shard"),
            P("shard", None),
            P("shard", None),
            P("shard", None),
            P("shard", None),
            P("shard"),
            P("shard", None),
            P("shard", None, None, None),
        ),
        check_vma=False,
    )
```

time: 701 us -> 496 us (0.71)
  the two profiles are of different devices: /device:TPU:0 before, /device:TPU:32 now
where the time goes in v2:
time: 496 us; the launch traced here: 487 us
  waiting for transfers between devices  179 us (36%)
  Pallas kernels  102 us (21%)
  starting transfers between devices  71.5 us (14%)
  other arithmetic  50 us (10%)
  local copies, waits for them, and re-layouts  40 us (8%)
  blocking collectives  21.4 us (4%)
  between operations  16.2 us (3%)
  matrix products  6.37 us (1%)
    ppermute x20, waiting for transfers between devices, exchange(): lax.ppermute(x, axis, [(i, i ^ bits) for i in range(lax.axis_size(axis))])  82.5 us
    all_to_all x8, waiting for transfers between devices, split_all(): return lax.all_to_all(x, axis, 0, 0, tiled=True)  55.9 us
    all_to_all x8, starting transfers between devices, split_all(): return lax.all_to_all(x, axis, 0, 0, tiled=True)  42.3 us
    pallas_call x1, Pallas kernels, run_experts(): pl.pallas_call(expert_kernel, grid=(CHUNKS + 6,), in_specs=[taken, taken,...  33.9 us
    ppermute x20, starting transfers between devices, exchange(): lax.ppermute(x, axis, [(i, i ^ bits) for i in range(lax.axis_size(axis))])  29 us
    all_gather x1, waiting for transfers between devices, per_device(): lax.all_gather(jnp.concatenate([grouped, out_weight, small], axis=1), 'sh...  22.9 us
    all_to_all x1, blocking collectives, split_all(): return lax.all_to_all(x, axis, 0, 0, tiled=True)  21.4 us
    pallas_call x1, Pallas kernels, attend_back(): pl.pallas_call(attend_back_kernel, grid=(NQ,), in_specs=[block, whole(2 *...  18 us
  transfers between devices with their start and end apart: 31, of which 16 were waited for; matrix products, arithmetic and copies ran while one was open for 16% of the time, Pallas kernels for 13%

profile of v2, /device:TPU:32, one launch (start us, length us, event | category | flops | bytes accessed | tf_op | source)
XLA Modules:
  0.0 486.8 jit_solution(14289512015830140705)
XLA Ops:
  13.9 6.9 %all-to-all-start = ((s32[8,1,192]{2,1,0:T(1,128)}), s32[8,1,192]{2,1,0:T(1,128)S(1)}, u32[]{:S(2)}, u32[]{:S(2)}) async-start(s32[8,1,192]{2,1,0:T(1,128)} %broadcast_in_dim.64), calls=%async_computation | async-start | bytes 16384 | tf_op jit(solution)/shard_map/all_to_all | solution.py:41
  34.5 22.9 %all-gather.4.cloned.1.call-done.weight_ref.small_ref.out_ref = bf16[1024,3200]{1,0:T(8,128)(2,1)} async-done(((bf16[64,3200]{1,0:T(8,128)(2,1)}), bf16[1024,3200]{1,0:T(8,128)(2,1)}) %all-gather.4.cloned.1.call-update) | async-done | bytes 6553616 | tf_op jit(solution)/shard_map/all_gather | solution.py:613
  57.3 7.8 %shard_map.195 = (bf16[8,192,256]{2,1,0:T(8,128)(2,1)}, bf16[192,1024]{1,0:T(8,128)(2,1)}, f32[8,1024]{1,0:T(8,128)}) custom-call(bf16[192,1024]{1,0:T(8,128)(2,1)} %tokens_ref.2, bf16[1024,3200]{1,0:T(8,128)(2,1)} %all-gather.4.cloned.1.call-done.weight_ref.small_ref.out_ref, bf16[1024,3200]{1,0:T(8,128)(2,1)} %all-gather.4.cloned.1.call-done.weight_ref.small_ref.out_ref, ...), custom_call_target="tpu_custom_call" | custom-call | tf_op jit(solution)/shard_map/pallas_call | solution.py:84
  65.2 21.4 %all_to_all.46 = bf16[8,192,256]{2,1,0:T(8,128)(2,1)} all-to-all(bf16[8,192,256]{2,1,0:T(8,128)(2,1)} %get-tuple-element.59), channel_id=1, replica_groups=mesh['shard'=16,'replica'=8] {'replica'}, dimensions={0} | all-to-all | bytes 1572864 | tf_op jit(solution)/shard_map/all_to_all | solution.py:41
  88.4 13.1 %shard_map.196 = (bf16[1536,128]{1,0:T(8,128)(2,1)}, f32[6,1,512]{2,1,0:T(1,128)}) custom-call(bf16[1536,256]{1,0:T(8,128)(2,1)} %bitcast.81, bf16[1536,256]{1,0:T(8,128)(2,1)} %bitcast.82, s32[6,1,256]{2,1,0:T(1,128)} %select_n.235.start_ref), custom_call_target="tpu_custom_call" | custom-call | tf_op jit(solution)/shard_map/pallas_call | solution.py:141
  106.2 8.8 %all-to-all-done.2.mixed_ref = bf16[8,192,128]{2,1,0:T(8,128)(2,1)S(1)} async-done(((bf16[8,192,128]{2,1,0:T(8,128)(2,1)}), bf16[8,192,128]{2,1,0:T(8,128)(2,1)S(1)}, u32[]{:S(2)}, u32[]{:S(2)}) %all-to-all-start.2) | async-done | bytes 393248 | tf_op jit(solution)/shard_map/all_to_all | solution.py:41
  129.7 10.4 %collective-permute-done.1 = bf16[384,1024]{1,0:T(8,128)(2,1)S(1)} collective-permute-done((bf16[384,1024]{1,0:T(8,128)(2,1)S(1)}, bf16[384,1024]{1,0:T(8,128)(2,1)S(1)}, u32[]{:S(2)}, u32[]{:S(2)}) %collective-permute-start.1) | collective-permute-done | bytes 786464 | tf_op jit(solution)/shard_map/ppermute | solution.py:563
  141.1 12.7 %collective-permute-done.2 = bf16[384,1024]{1,0:T(8,128)(2,1)} collective-permute-done((bf16[384,1024]{1,0:T(8,128)(2,1)S(1)}, bf16[384,1024]{1,0:T(8,128)(2,1)}, u32[]{:S(2)}, u32[]{:S(2)}) %collective-permute-start.2) | collective-permute-done | bytes 786464 | tf_op jit(solution)/shard_map/ppermute | solution.py:563
  158.6 16.9 %all-gather.6.cloned.1.call-done.rows_ref = bf16[3072,1152]{1,0:T(8,128)(2,1)} async-done(((bf16[192,1152]{1,0:T(8,128)(2,1)}), bf16[3072,1152]{1,0:T(8,128)(2,1)}) %all-gather.6.cloned.1.call-update) | async-done | bytes 7077904 | tf_op jit(solution)/shard_map/all_gather | solution.py:664
  175.6 33.9 %shard_map.198 = (bf16[2,4,2,192,1024]{4,3,2,1,0:T(8,128)(2,1)}, bf16[16,2,64,1024]{3,2,1,0:T(8,128)(2,1)}, bf16[2,3,1024,512]{3,2,1,0:T(8,128)(2,1)}) custom-call(bf16[3072,1152]{1,0:T(8,128)(2,1)} %all-gather.6.cloned.1.call-done.rows_ref, bf16[3072,1152]{1,0:T(8,128)(2,1)} %all-gather.8.cloned.1.call-done.cot_ref, f32[2,4,4,192]{3,2,1,0:T(4,128)} %copy.88.slots_ref, ...), custom_call_target="tpu_custom_call" | custom-call | tf_op jit(solution)/shard_map/pallas_call | solution.py:396
  209.4 5.5 %all-to-all-start.3 = ((bf16[16,2,64,1024]{3,2,1,0:T(8,128)(2,1)}), bf16[16,2,64,1024]{3,2,1,0:T(8,128)(2,1)}, u32[]{:S(2)}, u32[]{:S(2)}) async-start(bf16[16,2,64,1024]{3,2,1,0:T(8,128)(2,1)} %get-tuple-element.71), calls=%async_computation.3 | async-start | bytes 8388608 | tf_op jit(solution)/shard_map/all_to_all | solution.py:41
  226.8 33.7 %collective-permute-done.5 = bf16[1536,512]{1,0:T(8,128)(2,1)} collective-permute-done((bf16[1536,512]{1,0:T(8,128)(2,1)}, bf16[1536,512]{1,0:T(8,128)(2,1)}, u32[]{:S(2)}, u32[]{:S(2)}) %collective-permute-start.5) | collective-permute-done | bytes 1572896 | tf_op jit(solution)/shard_map/ppermute | solution.py:563
  282.0 9.0 %shard_map.199 = (f32[192,1024]{1,0:T(8,128)}, bf16[8,192,128]{2,1,0:T(8,128)(2,1)}, bf16[1024,1152]{1,0:T(8,128)(2,1)}) custom-call(bf16[2048,1024]{1,0:T(8,128)(2,1)} %bitcast.12.back_ref, bf16[192,2048]{1,0:T(8,128)(2,1)} %compare_convert_fusion.spots_ref, bf16[2048,128]{1,0:T(8,128)(2,1)} %fusion.6.spread_ref, bf16[3,2048]{1,0:T(4,128)(2,1)} %reshape.310.gate_rows_ref, ...), custom_call_target="tpu_custom_call" | custom-call | tf_op jit(solution)/shard_map/pallas_call | solution.py:476
  290.9 5.5 %all-to-all-start.4 = ((bf16[8,192,128]{2,1,0:T(8,128)(2,1)}), bf16[8,192,128]{2,1,0:T(8,128)(2,1)S(1)}, u32[]{:S(2)}, u32[]{:S(2)}) async-start(bf16[8,192,128]{2,1,0:T(8,128)(2,1)} %get-tuple-element.78), calls=%async_computation.4 | async-start | bytes 786432 | tf_op jit(solution)/shard_map/all_to_all | solution.py:41
  298.0 7.4 %all-to-all-done.4 = bf16[8,192,128]{2,1,0:T(8,128)(2,1)S(1)} async-done(((bf16[8,192,128]{2,1,0:T(8,128)(2,1)}), bf16[8,192,128]{2,1,0:T(8,128)(2,1)S(1)}, u32[]{:S(2)}, u32[]{:S(2)}) %all-to-all-start.4) | async-done | bytes 393248 | tf_op jit(solution)/shard_map/all_to_all | solution.py:41
  306.2 5.1 %all-to-all-start.5 = ((bf16[128,8,1152]{2,1,0:T(8,128)(2,1)}), bf16[128,8,1152]{2,1,0:T(8,128)(2,1)S(1)}, u32[]{:S(2)}, u32[]{:S(2)}) async-start(bf16[128,8,1152]{2,1,0:T(8,128)(2,1)} %bitcast.91), calls=%async_computation.5 | async-start | bytes 4718592 | tf_op jit(solution)/shard_map/all_to_all | solution.py:41
  324.3 18.0 %shard_map.200 = bf16[1536,256]{1,0:T(8,128)(2,1)} custom-call(bf16[1536,256]{1,0:T(8,128)(2,1)} %bitcast.83, bf16[1536,256]{1,0:T(8,128)(2,1)} %bitcast.84, bf16[1536,128]{1,0:T(8,128)(2,1)} %bitcast.92, s32[6,1,256]{2,1,0:T(1,128)} %select_n.235.start_ref, f32[6,1,512]{2,1,0:T(1,128)} %get-tuple-element.83.lse_ref, ...), custom_call_target="tpu_custom_call" | custom-call | tf_op jit(solution)/shard_map/pallas_call | solution.py:234
  342.4 4.5 collective-permute-done.13
  349.1 7.9 %collective-permute-done.11 = bf16[768,512]{1,0:T(8,128)(2,1)S(1)} collective-permute-done((bf16[768,512]{1,0:T(8,128)(2,1)S(1)}, bf16[768,512]{1,0:T(8,128)(2,1)S(1)}, u32[]{:S(2)}, u32[]{:S(2)}) %collective-permute-start.11) | collective-permute-done | bytes 786464 | tf_op jit(solution)/shard_map/ppermute | solution.py:563
  362.9 6.0 %all-to-all-start.6 = ((bf16[16,64,256]{2,1,0:T(8,128)(2,1)}), bf16[16,64,256]{2,1,0:T(8,128)(2,1)}, u32[]{:S(2)}, u32[]{:S(2)}) async-start(bf16[16,64,256]{2,1,0:T(8,128)(2,1)} %bitcast.98), calls=%async_computation.6 | async-start | bytes 1048576 | tf_op jit(solution)/shard_map/all_to_all | solution.py:41
  369.0 10.4 %collective-permute-done.15 = bf16[768,512]{1,0:T(8,128)(2,1)} collective-permute-done((bf16[768,512]{1,0:T(8,128)(2,1)S(1)}, bf16[768,512]{1,0:T(8,128)(2,1)}, u32[]{:S(2)}, u32[]{:S(2)}) %collective-permute-start.15) | collective-permute-done | bytes 786464 | tf_op jit(solution)/shard_map/ppermute | solution.py:563
  389.0 4.5 all-to-all-start.7
  402.1 17.1 %all-to-all-done.7 = bf16[8,192,256]{2,1,0:T(8,128)(2,1)} async-done(((bf16[8,192,256]{2,1,0:T(8,128)(2,1)}), bf16[8,192,256]{2,1,0:T(8,128)(2,1)}, u32[]{:S(2)}, u32[]{:S(2)}) %all-to-all-start.7) | async-done | bytes 786464 | tf_op jit(solution)/shard_map/all_to_all | solution.py:41
  446.4 20.0 %all-to-all-done.8 = bf16[8,208,128]{2,1,0:T(8,128)(2,1)S(1)} async-done(((bf16[8,208,128]{2,1,0:T(8,128)(2,1)}), bf16[8,208,128]{2,1,0:T(8,128)(2,1)S(1)}, u32[]{:S(2)}, u32[]{:S(2)}) %all-to-all-start.8) | async-done | bytes 426016 | tf_op jit(solution)/shard_map/all_to_all | solution.py:41
  (239 shorter events, 161.2 us)
Async XLA Ops:
  7.2 50.1 %all-gather.4.cloned.1.call-start = ((), (), s32[]{:S(2)}) async-start(), calls=%async_computation.9 | async-start | bytes 6963200 | tf_op jit(solution)/shard_map/all_gather | solution.py:613
  11.7 114.5 %all-gather.8.cloned.1.call-start = ((), (), s32[]{:S(2)}) async-start(), calls=%async_computation.11 | async-start | bytes 7520256 | tf_op jit(solution)/shard_map/all_gather | solution.py:631
  106.0 69.6 %all-gather.6.cloned.1.call-start = ((), (), s32[]{:S(2)}) async-start(), calls=%async_computation.10 | async-start | bytes 7520256 | tf_op jit(solution)/shard_map/all_gather | solution.py:664
  120.1 33.7 %collective-permute-start.2 = (bf16[384,1024]{1,0:T(8,128)(2,1)S(1)}, bf16[384,1024]{1,0:T(8,128)(2,1)}, u32[]{:S(2)}, u32[]{:S(2)}) collective-permute-start(bf16[384,1024]{1,0:T(8,128)(2,1)S(1)} %pad_maximum_fusion.2), channel_id=1, source_target_pairs={{0,4},{1,5},{2,6},{3,7},{4,0},{5,1},{6,2},{7,3},{8,12},{9,13},{10,... | collective-permute-start | bytes 2359304 | tf_op jit(solution)/shard_map/ppermute | solution.py:563
  122.4 34.1 %collective-permute-start.3 = (bf16[384,1024]{1,0:T(8,128)(2,1)S(1)}, bf16[384,1024]{1,0:T(8,128)(2,1)}, u32[]{:S(2)}, u32[]{:S(2)}) collective-permute-start(bf16[384,1024]{1,0:T(8,128)(2,1)S(1)} %pad_maximum_fusion.2), channel_id=1, source_target_pairs={{0,6},{1,7},{2,4},{3,5},{4,2},{5,3},{6,0},{7,1},{8,14},{9,15},{10,... | collective-permute-start | bytes 2359304 | tf_op jit(solution)/shard_map/ppermute | solution.py:563
  209.4 57.7 %all-to-all-start.3 = ((bf16[16,2,64,1024]{3,2,1,0:T(8,128)(2,1)}), bf16[16,2,64,1024]{3,2,1,0:T(8,128)(2,1)}, u32[]{:S(2)}, u32[]{:S(2)}) async-start(bf16[16,2,64,1024]{3,2,1,0:T(8,128)(2,1)} %get-tuple-element.71), calls=%async_computation.3 | async-start | bytes 8388608 | tf_op jit(solution)/shard_map/all_to_all | solution.py:41
  219.0 48.1 %collective-permute-start.6 = (bf16[4,2,192,1024]{3,2,1,0:T(8,128)(2,1)}, bf16[4,2,192,1024]{3,2,1,0:T(8,128)(2,1)}, u32[]{:S(2)}, u32[]{:S(2)}) collective-permute-start(bf16[4,2,192,1024]{3,2,1,0:T(8,128)(2,1)} %dynamic-slice_bitcast_fusion), channel_id=1, source_target_pairs={{0,8},{8,0},{16,24},{24,16},{32,40},{40,32},{48,56},{56,48},{64,72... | collective-permute-start | bytes 9437192 | tf_op jit(solution)/shard_map/ppermute | solution.py:563
  222.5 38.0 %collective-permute-start.5 = (bf16[1536,512]{1,0:T(8,128)(2,1)}, bf16[1536,512]{1,0:T(8,128)(2,1)}, u32[]{:S(2)}, u32[]{:S(2)}) collective-permute-start(bf16[1536,512]{1,0:T(8,128)(2,1)} %constant_dynamic-slice_fusion.9), channel_id=1, source_target_pairs={{0,6},{1,7},{2,4},{3,5},{4,2},{5,3},{6,0},{7,1},{8,14},{9,15},{10,... | collective-permute-start | bytes 4718600 | tf_op jit(solution)/shard_map/ppermute | solution.py:563
  226.6 37.4 %collective-permute-start.4 = (bf16[1536,512]{1,0:T(8,128)(2,1)}, bf16[1536,512]{1,0:T(8,128)(2,1)}, u32[]{:S(2)}, u32[]{:S(2)}) collective-permute-start(bf16[1536,512]{1,0:T(8,128)(2,1)} %constant_dynamic-slice_fusion.11), channel_id=1, source_target_pairs={{0,2},{1,3},{2,0},{3,1},{4,6},{5,7},{6,4},{7,5},{8,10},{9,11},{10,... | collective-permute-start | bytes 4718600 | tf_op jit(solution)/shard_map/ppermute | solution.py:563
  273.4 32.1 %collective-permute-start.10 = (bf16[2,192,1024]{2,1,0:T(8,128)(2,1)}, bf16[2,192,1024]{2,1,0:T(8,128)(2,1)}, u32[]{:S(2)}, u32[]{:S(2)}) collective-permute-start(bf16[2,192,1024]{2,1,0:T(8,128)(2,1)} %pad_maximum_fusion.4), channel_id=1, source_target_pairs={{0,96},{8,104},{16,112},{24,120},{32,64},{40,72},{48,80},{56,88},{... | collective-permute-start | bytes 2359304 | tf_op jit(solution)/shard_map/ppermute | solution.py:563
  275.9 29.6 %collective-permute-start.9 = (bf16[2,192,1024]{2,1,0:T(8,128)(2,1)}, bf16[2,192,1024]{2,1,0:T(8,128)(2,1)}, u32[]{:S(2)}, u32[]{:S(2)}) collective-permute-start(bf16[2,192,1024]{2,1,0:T(8,128)(2,1)} %pad_maximum_fusion.3), channel_id=1, source_target_pairs={{0,32},{8,40},{16,48},{24,56},{32,0},{40,8},{48,16},{56,24},{64,96... | collective-permute-start | bytes 2359304 | tf_op jit(solution)/shard_map/ppermute | solution.py:563
  277.7 27.8 %collective-permute-start.7 = (bf16[768,512]{1,0:T(8,128)(2,1)}, bf16[768,512]{1,0:T(8,128)(2,1)}, u32[]{:S(2)}, u32[]{:S(2)}) collective-permute-start(bf16[768,512]{1,0:T(8,128)(2,1)} %constant_dynamic-slice_fusion.10), channel_id=1, source_target_pairs={{0,6},{1,7},{2,4},{3,5},{4,2},{5,3},{6,0},{7,1},{8,14},{9,15},{10,... | collective-permute-start | bytes 2359304 | tf_op jit(solution)/shard_map/ppermute | solution.py:563
  280.4 25.1 %collective-permute-start.8 = (bf16[768,512]{1,0:T(8,128)(2,1)}, bf16[768,512]{1,0:T(8,128)(2,1)S(1)}, u32[]{:S(2)}, u32[]{:S(2)}) collective-permute-start(bf16[768,512]{1,0:T(8,128)(2,1)} %constant_dynamic-slice_fusion.8), channel_id=1, source_target_pairs={{0,2},{1,3},{2,0},{3,1},{4,6},{5,7},{6,4},{7,5},{8,10},{9,11},{10,... | collective-permute-start | bytes 2359304 | tf_op jit(solution)/shard_map/ppermute | solution.py:563
  306.2 56.7 %all-to-all-start.5 = ((bf16[128,8,1152]{2,1,0:T(8,128)(2,1)}), bf16[128,8,1152]{2,1,0:T(8,128)(2,1)S(1)}, u32[]{:S(2)}, u32[]{:S(2)}) async-start(bf16[128,8,1152]{2,1,0:T(8,128)(2,1)} %bitcast.91), calls=%async_computation.5 | async-start | bytes 4718592 | tf_op jit(solution)/shard_map/all_to_all | solution.py:41
  313.6 43.5 %collective-permute-start.11 = (bf16[768,512]{1,0:T(8,128)(2,1)S(1)}, bf16[768,512]{1,0:T(8,128)(2,1)S(1)}, u32[]{:S(2)}, u32[]{:S(2)}) collective-permute-start(bf16[768,512]{1,0:T(8,128)(2,1)S(1)} %pad_maximum_fusion.5), channel_id=1, source_target_pairs={{0,1},{1,0},{2,3},{3,2},{4,5},{5,4},{6,7},{7,6},{8,9},{9,8},{10,11... | collective-permute-start | bytes 2359304 | tf_op jit(solution)/shard_map/ppermute | solution.py:563
  318.0 28.9 %collective-permute-start.13 = (bf16[192,1024]{1,0:T(8,128)(2,1)S(1)}, bf16[192,1024]{1,0:T(8,128)(2,1)S(1)}, u32[]{:S(2)}, u32[]{:S(2)}) collective-permute-start(bf16[192,1024]{1,0:T(8,128)(2,1)S(1)} %fusion.23), channel_id=1, source_target_pairs={{0,32},{8,40},{16,48},{24,56},{32,0},{40,8},{48,16},{56,24},{64,96... | collective-permute-start | bytes 1179656 | tf_op jit(solution)/shard_map/ppermute | solution.py:563
  319.6 29.5 %collective-permute-start.12 = (bf16[192,1024]{1,0:T(8,128)(2,1)S(1)}, bf16[192,1024]{1,0:T(8,128)(2,1)S(1)}, u32[]{:S(2)}, u32[]{:S(2)}) collective-permute-start(bf16[192,1024]{1,0:T(8,128)(2,1)S(1)} %fusion.24), channel_id=1, source_target_pairs={{0,96},{8,104},{16,112},{24,120},{32,64},{40,72},{48,80},{56,88},{... | collective-permute-start | bytes 1179656 | tf_op jit(solution)/shard_map/ppermute | solution.py:563
  384.6 34.7 %collective-permute-start.17 = (bf16[768,512]{1,0:T(8,128)(2,1)}, bf16[768,512]{1,0:T(8,128)(2,1)}, u32[]{:S(2)}, u32[]{:S(2)}) collective-permute-start(bf16[768,512]{1,0:T(8,128)(2,1)} %pad_maximum_fusion.7), channel_id=1, source_target_pairs={{0,2},{1,3},{2,0},{3,1},{4,6},{5,7},{6,4},{7,5},{8,10},{9,11},{10,... | collective-permute-start | bytes 2359304 | tf_op jit(solution)/shard_map/ppermute | solution.py:563
  386.8 32.4 %collective-permute-start.16 = (bf16[768,512]{1,0:T(8,128)(2,1)}, bf16[768,512]{1,0:T(8,128)(2,1)}, u32[]{:S(2)}, u32[]{:S(2)}) collective-permute-start(bf16[768,512]{1,0:T(8,128)(2,1)} %pad_maximum_fusion.6), channel_id=1, source_target_pairs={{0,6},{1,7},{2,4},{3,5},{4,2},{5,3},{6,0},{7,1},{8,14},{9,15},{10,... | collective-permute-start | bytes 2359304 | tf_op jit(solution)/shard_map/ppermute | solution.py:563
  389.0 30.2 %all-to-all-start.7 = ((bf16[8,192,256]{2,1,0:T(8,128)(2,1)}), bf16[8,192,256]{2,1,0:T(8,128)(2,1)}, u32[]{:S(2)}, u32[]{:S(2)}) async-start(bf16[8,192,256]{2,1,0:T(8,128)(2,1)} %bitcast.29), calls=%async_computation.7 | async-start | bytes 1572864 | tf_op jit(solution)/shard_map/all_to_all | solution.py:41
  398.1 28.1 %collective-permute-start.14 = (bf16[192,1024]{1,0:T(8,128)(2,1)}, bf16[192,1024]{1,0:T(8,128)(2,1)}, u32[]{:S(2)}, u32[]{:S(2)}) collective-permute-start(bf16[192,1024]{1,0:T(8,128)(2,1)} %get-tuple-element.166), channel_id=1, source_target_pairs={{0,16},{8,24},{16,0},{24,8},{32,48},{40,56},{48,32},{56,40},{64,80... | collective-permute-start | bytes 1179656 | tf_op jit(solution)/shard_map/ppermute | solution.py:563
  423.8 48.8 %collective-permute-start.19 = (bf16[1536,512]{1,0:T(8,128)(2,1)}, bf16[1536,512]{1,0:T(8,128)(2,1)}, u32[]{:S(2)}, u32[]{:S(2)}) collective-permute-start(bf16[1536,512]{1,0:T(8,128)(2,1)} %pad_maximum_fusion.1.rows_ref), channel_id=1, source_target_pairs={{0,2},{1,3},{2,0},{3,1},{4,6},{5,7},{6,4},{7,5},{8,10},{9,11},{10,... | collective-permute-start | bytes 4718600 | tf_op jit(solution)/shard_map/ppermute | solution.py:563
  423.9 52.3 %collective-permute-start.18 = (bf16[1536,512]{1,0:T(8,128)(2,1)S(1)}, bf16[1536,512]{1,0:T(8,128)(2,1)}, u32[]{:S(2)}, u32[]{:S(2)}) collective-permute-start(bf16[1536,512]{1,0:T(8,128)(2,1)S(1)} %pad_maximum_fusion.rows_ref), channel_id=1, source_target_pairs={{0,6},{1,7},{2,4},{3,5},{4,2},{5,3},{6,0},{7,1},{8,14},{9,15},{10,... | collective-permute-start | bytes 4718600 | tf_op jit(solution)/shard_map/ppermute | solution.py:563
  432.7 33.6 %all-to-all-start.8 = ((bf16[8,208,128]{2,1,0:T(8,128)(2,1)}), bf16[8,208,128]{2,1,0:T(8,128)(2,1)S(1)}, u32[]{:S(2)}, u32[]{:S(2)}) async-start(bf16[8,208,128]{2,1,0:T(8,128)(2,1)} %broadcast_in_dim.76), calls=%async_computation.8 | async-start | bytes 851968 | tf_op jit(solution)/shard_map/all_to_all | solution.py:41
  (45 other events, 318.5 us)
Sparse Core Ops, SparseCore 0:
  11.8 45.5 all-gather.3
  59.0 67.0 all-gather.7
  127.8 47.6 all-gather.5

commit v3 on v2

--- a/solution.py
+++ b/solution.py
@@ -511,7 +511,7 @@
 def heads_kernel(parts_ref, query_ref, key_ref, value_ref, gain_ref, dq_ref, dk_ref, dv_ref, norm_ref):
     total = jnp.zeros((64, 128), F32)
     for pair in range(NR // 2):
-        first, second = parts_ref[2 * pair].astype(F32), parts_ref[2 * pair + 1].astype(F32)
+        first, second = parts_ref[2 * pair, :64].astype(F32), parts_ref[2 * pair + 1, :64].astype(F32)
         lanes = slice(pair * 128, (pair + 1) * 128)
         for at, part in ((2 * pair, first), (2 * pair + 1, second)):
             wide = slice(at * 128, (at + 1) * 128)
@@ -537,26 +537,26 @@
     )(parts, query_weight, key_matrix, value_matrix, norm_one.astype(F32)[:, None])
 
 
-def widen_kernel(place_ref, rows_ref, *refs):
+def widen_kernel(places_ref, rows_ref, *refs):
     refs[-1][...] = rows_ref[...].astype(F32)
 
 
-def widen(rows, place, total=None):
-    block = 512
-    steps = rows.shape[0] // block
+def widen(rows, places, total=None):
+    steps = 4
+    block = rows.shape[0] // steps
     given = () if total is None else (total,)
     return pl.pallas_call(
         widen_kernel,
         grid_spec=pltpu.PrefetchScalarGridSpec(
             num_scalar_prefetch=1,
             grid=(steps,),
-            in_specs=[pl.BlockSpec((block, FF), lambda i, place: (i, 0))]
+            in_specs=[pl.BlockSpec((block, FF), lambda i, places: (i, 0))]
             + [pl.BlockSpec(memory_space=pl.ANY)] * len(given),
-            out_specs=pl.BlockSpec((block, FF), lambda i, place: (place[0] * steps + i, 0)),
+            out_specs=pl.BlockSpec((block, FF), lambda i, places: (places[i], 0)),
         ),
         out_shape=jax.ShapeDtypeStruct((6 * D, FF), F32),
         input_output_aliases={2: 0} if given else {},
-    )(jnp.reshape(place, (1,)).astype(jnp.int32), rows, *given)
+    )(places.astype(jnp.int32), rows, *given)
 
 
 def exchange(x, bits, axis="replica"):
@@ -681,15 +681,8 @@
     core, row, layer = shard % 2, shard // 2 % 2, shard // 4
     pick = lambda x, at: lax.dynamic_index_in_dim(x, at, 0, keepdims=False)
     from_core = exchange(pick(combined, 1 - core), 1, "shard")
-    back, send_a, send_b, from_core = lax.optimization_barrier((back, send_a, send_b, from_core))
+    back, send_a, send_b = lax.optimization_barrier((back, send_a, send_b))
     got_a, got_b = exchange(send_a, 6), exchange(send_b, 2)
-    sums = add_low(pick(combined, core), from_core)
-    keep = [[pick(sums[:, y], layer), pick(sums[:, y], layer ^ step)] for y, step in ((0, 3), (1, 1))]
-    send = [
-        jnp.stack([pick(sums[:, y], layer ^ first), pick(sums[:, y], layer ^ 2)])
-        for y, first in ((0, 1), (1, 3))
-    ]
-    layers = [exchange(send[0], 4, "shard"), exchange(send[1], 12, "shard")]
 
     gate_rows = back.reshape(E, SLOTS, D)[:, 60:63, :SLOTS].transpose(1, 0, 2).reshape(3, E * SLOTS)
     middle_grad, mixed_grad, dense = token_back(
@@ -706,22 +699,17 @@
         mixed,
     )
     grad_heads = split_all(mixed_grad, "replica").reshape(SEQ, 128)
-    grad_heads, got_a, got_b, *layers = lax.optimization_barrier((grad_heads, got_a, got_b, *layers))
-    keep = [[add_low(keep[y][n], layers[y][n]) for n in range(2)] for y in range(2)]
-    layers = [exchange(keep[0][1], 12, "shard"), exchange(keep[1][1], 4, "shard")]
+    grad_heads, got_a, got_b = lax.optimization_barrier((grad_heads, got_a, got_b))
     keep_a, send_a = halves(add_low(keep_a, got_a), side)
     keep_b, send_b = halves(add_low(keep_b, got_b), side)
     got = exchange(jnp.concatenate([send_a, send_b], axis=0), 1)
     head_grad = attend_back(
         qkv, grad_heads, start, lse, cosine.T, sine.T, cos_head, sin_head
     )
-    head_grad, got, *layers = lax.optimization_barrier((head_grad, got, *layers))
-    sides = [add_low(keep[y][0], layers[y]) for y in range(2)]
-    own_side = jnp.where(row == 0, sides[0], sides[1])
-    from_side = exchange(jnp.where(row == 0, sides[1], sides[0]), 2, "shard")
+    head_grad, got = lax.optimization_barrier((head_grad, got))
     own = add_low(jnp.concatenate([keep_a, keep_b], axis=0), got)
+    half = own.shape[0] // 2
     other = exchange(own, 1)
-    half = own.shape[0] // 2
     head_rows = jnp.concatenate(
         [
             lax.dynamic_slice_in_dim(head_grad, (along_x ^ k) * 2 * TOK, 2 * TOK, 0)
@@ -730,16 +718,53 @@
         axis=0,
     )
     heads_grad = mm(normed_seq, head_rows, TN).astype(BF)
-    dense_parts = split_all(after(dense, grad_heads).reshape(NS * NR, 8, 1152), ("shard", "replica"))
-    dense_sum = jnp.sum(dense_parts.reshape(NS * NR, 8, 1152).astype(F32), axis=0).astype(BF)
-    heads_grad = after(heads_grad, dense_parts)
+
+    dense_parts = split_all(after(dense, grad_heads).reshape(NS, 64, 1152), "shard")
+    dense_sum = jnp.sum(dense_parts.astype(F32), axis=0).astype(BF)
+    dense_here = split_all(after(dense_sum, heads_grad).reshape(NR, 8, 1152), "replica")
+    sums = add_low(pick(combined, core), after(from_core, heads_grad))
+    keep = [[pick(sums[:, y], layer), pick(sums[:, y], layer ^ step)] for y, step in ((0, 3), (1, 1))]
+    send = [
+        jnp.stack([pick(sums[:, y], layer ^ first), pick(sums[:, y], layer ^ 2)])
+        for y, first in ((0, 1), (1, 3))
+    ]
+    layers = [exchange(send[0], 4, "shard"), exchange(send[1], 12, "shard")]
+
+    heads_grad, dense_here, other = lax.optimization_barrier((heads_grad, dense_here, other))
     heads_parts = split_all(heads_grad.reshape(NS, 64, 256), "shard")
+    own_a = jnp.concatenate([own[:half], other[:half]], axis=0)
+    own_b = jnp.concatenate([own[half:], other[half:]], axis=0)
+    other_a, other_b = exchange(own_a, 6), exchange(own_b, 2)
+    dense_total = jnp.sum(dense_here.astype(F32), axis=0).astype(BF)
     heads_sum = jnp.sum(heads_parts.astype(F32), axis=0).astype(BF)
-    head_grad, heads_parts, other = lax.optimization_barrier((head_grad, heads_parts, other))
-    own_a, own_b = in_order(own[:half], other[:half], side), in_order(own[half:], other[half:], side)
-    other_a, other_b = exchange(own_a, 6), exchange(own_b, 2)
-
-    by_token = split_all(head_grad.reshape(NR, TOK, 256), "replica")
+    last = jnp.concatenate(
+        [heads_sum, dense_total.reshape(36, 256), jnp.zeros((12, 256), BF)], axis=0
+    )
+    by_token = split_all(after(head_grad, heads_parts).reshape(NR, TOK, 256), "replica")
+    by_token, other_a, other_b, *layers = lax.optimization_barrier(
+        (by_token, other_a, other_b, *layers)
+    )
+    own_a = jnp.concatenate([own_a, other_a], axis=0)
+    own_b = jnp.concatenate([own_b, other_b], axis=0)
+    other_a, other_b = exchange(own_a, 2), exchange(own_b, 6)
+    last = spread_all(after(last, by_token), "replica", NR)
+
+    def places(first, bit, low):
+        return first + 4 * bit + jnp.stack(
+            [2 * at + near for at in (low, 1 - low) for near in (side, 1 - side)]
+        )
+
+    expert_total = widen(own_a, places(0, mixed_bit, low_bit))
+    expert_total = widen(own_b, places(8, high_bit, low_bit), expert_total)
+    last, expert_total = lax.optimization_barrier((last, expert_total))
+    keep = [[add_low(keep[y][n], layers[y][n]) for n in range(2)] for y in range(2)]
+    layers = [exchange(keep[0][1], 12, "shard"), exchange(keep[1][1], 4, "shard")]
+    query_grad, key_grad, value_grad, norm_one_grad = finish_heads(
+        last, query_weight, key_matrix, value_matrix, norm_one
+    )
+    dense_last = last[:, 64:100].reshape(64, 1152).astype(F32)
+
+    layers = [after(part, last) for part in layers]
     normed_grad = mm(by_token.transpose(1, 0, 2).reshape(TOK, 2048), gathered[:, :2048], NT)
     tokens_wide = tokens.astype(F32)
     inverse = lax.rsqrt(jnp.mean(tokens_wide * tokens_wide, axis=-1, keepdims=True) + EPSILON)
@@ -749,22 +774,14 @@
         middle_grad + inverse * (scaled - hat * jnp.mean(scaled * hat, axis=-1, keepdims=True))
     ).astype(BF)
 
+    sides = [add_low(keep[y][0], layers[y]) for y in range(2)]
+    own_side = jnp.where(row == 0, sides[0], sides[1])
+    from_side = exchange(jnp.where(row == 0, sides[1], sides[0]), 2, "shard")
+    from_side = after(from_side, tokens_grad)
     layer_out = (middle + own_side.astype(F32) + from_side.astype(F32)).astype(BF)
-
-    last = jnp.concatenate([heads_sum.reshape(128, 128), dense_sum.reshape(72, 128)], axis=0)
-    last = jnp.pad(last, ((0, 8), (0, 0)))
-    last, by_token, other_a, other_b = lax.optimization_barrier((last, by_token, other_a, other_b))
-    own_a, own_b = in_order(own_a, other_a, low_bit), in_order(own_b, other_b, low_bit)
-    other_a, other_b = exchange(own_a, 2), exchange(own_b, 6)
-    last = spread_all(last, "replica", NR)
-    query_grad, key_grad, value_grad, norm_one_grad = finish_heads(
-        last[:, :128].reshape(NR, 64, 256), query_weight, key_matrix, value_matrix, norm_one
-    )
-    dense_last = last[:, 128:200].reshape(64, 1152).astype(F32)
-    expert_total = widen(own_a, mixed_bit)
-    expert_total = widen(own_b, 2 + high_bit, expert_total)
-    expert_total = widen(other_a, 1 - mixed_bit, expert_total)
-    expert_total = widen(other_b, 3 - high_bit, expert_total).reshape(2, 3, D, FF)
+    expert_total = widen(other_a, places(0, 1 - mixed_bit, 1 - low_bit), expert_total)
+    expert_total = widen(other_b, places(8, 1 - high_bit, 1 - low_bit), expert_total)
+    expert_total = expert_total.reshape(2, 3, D, FF)
     return (
         layer_out,
         tokens_grad,

time: 496 us -> 475 us (0.958)
  the two profiles are of different devices: /device:TPU:32 before, /device:TPU:0 now
where the time goes in v3:
time: 475 us; the launch traced here: 466 us
  waiting for transfers between devices  139 us (29%)
  Pallas kernels  106 us (22%)
  starting transfers between devices  77.4 us (16%)
  other arithmetic  51.7 us (11%)
  local copies, waits for them, and re-layouts  45 us (9%)
  blocking collectives  22.4 us (5%)
  between operations  16.1 us (3%)
  matrix products  8.75 us (2%)
    ppermute x20, waiting for transfers between devices, exchange(): lax.ppermute(x, axis, [(i, i ^ bits) for i in range(lax.axis_size(axis))])  71.1 us
    all_to_all x9, starting transfers between devices, split_all(): return lax.all_to_all(x, axis, 0, 0, tiled=True)  48.1 us
    all_to_all x9, waiting for transfers between devices, split_all(): return lax.all_to_all(x, axis, 0, 0, tiled=True)  33.9 us
    pallas_call x1, Pallas kernels, run_experts(): pl.pallas_call(expert_kernel, grid=(CHUNKS + 6,), in_specs=[taken, taken,...  33.9 us
    ppermute x20, starting transfers between devices, exchange(): lax.ppermute(x, axis, [(i, i ^ bits) for i in range(lax.axis_size(axis))])  29.2 us
    all_gather x1, waiting for transfers between devices, per_device(): lax.all_gather(jnp.concatenate([grouped, out_weight, small], axis=1), 'sh...  23.2 us
    all_to_all x1, blocking collectives, split_all(): return lax.all_to_all(x, axis, 0, 0, tiled=True)  22.4 us
    pallas_call x4, Pallas kernels, widen(): pl.pallas_call(widen_kernel, grid_spec=pltpu.PrefetchScalarGridSpec(num_s...  18.2 us
  transfers between devices with their start and end apart: 32, of which 17 were waited for; matrix products, arithmetic and copies ran while one was open for 19% of the time, Pallas kernels for 14%

profile of v3, /device:TPU:0, one launch (start us, length us, event | category | flops | bytes accessed | tf_op | source)
XLA Modules:
  0.0 466.1 jit_solution(8460099222977618718)
XLA Ops:
  13.9 7.0 %all-to-all-start = ((s32[8,1,192]{2,1,0:T(1,128)}), s32[8,1,192]{2,1,0:T(1,128)S(1)}, u32[]{:S(2)}, u32[]{:S(2)}) async-start(s32[8,1,192]{2,1,0:T(1,128)} %broadcast_in_dim.67), calls=%async_computation | async-start | bytes 16384 | tf_op jit(solution)/shard_map/all_to_all | solution.py:41
  34.6 23.2 %all-gather.4.cloned.1.call-done.weight_ref.small_ref.out_ref = bf16[1024,3200]{1,0:T(8,128)(2,1)} async-done(((bf16[64,3200]{1,0:T(8,128)(2,1)}), bf16[1024,3200]{1,0:T(8,128)(2,1)}) %all-gather.4.cloned.1.call-update) | async-done | bytes 6553616 | tf_op jit(solution)/shard_map/all_gather | solution.py:613
  57.8 7.9 %shard_map.195 = (bf16[8,192,256]{2,1,0:T(8,128)(2,1)}, bf16[192,1024]{1,0:T(8,128)(2,1)}, f32[8,1024]{1,0:T(8,128)}) custom-call(bf16[192,1024]{1,0:T(8,128)(2,1)} %tokens_ref.2, bf16[1024,3200]{1,0:T(8,128)(2,1)} %all-gather.4.cloned.1.call-done.weight_ref.small_ref.out_ref, bf16[1024,3200]{1,0:T(8,128)(2,1)} %all-gather.4.cloned.1.call-done.weight_ref.small_ref.out_ref, ...), custom_call_target="tpu_custom_call" | custom-call | tf_op jit(solution)/shard_map/pallas_call | solution.py:84
  65.7 22.4 %all_to_all.51 = bf16[8,192,256]{2,1,0:T(8,128)(2,1)} all-to-all(bf16[8,192,256]{2,1,0:T(8,128)(2,1)} %get-tuple-element.65), channel_id=1, replica_groups=mesh['shard'=16,'replica'=8] {'replica'}, dimensions={0} | all-to-all | bytes 1572864 | tf_op jit(solution)/shard_map/all_to_all | solution.py:41
  89.0 13.1 %shard_map.196 = (bf16[1536,128]{1,0:T(8,128)(2,1)}, f32[6,1,512]{2,1,0:T(1,128)}) custom-call(bf16[1536,256]{1,0:T(8,128)(2,1)} %bitcast.80, bf16[1536,256]{1,0:T(8,128)(2,1)} %bitcast.81, s32[6,1,256]{2,1,0:T(1,128)} %select_n.195.start_ref), custom_call_target="tpu_custom_call" | custom-call | tf_op jit(solution)/shard_map/pallas_call | solution.py:141
  102.1 6.5 %all-to-all-start.2 = ((bf16[8,192,128]{2,1,0:T(8,128)(2,1)}), bf16[8,192,128]{2,1,0:T(8,128)(2,1)S(1)}, u32[]{:S(2)}, u32[]{:S(2)}) async-start(bf16[8,192,128]{2,1,0:T(8,128)(2,1)} %bitcast.102), calls=%async_computation.2 | async-start | bytes 786432 | tf_op jit(solution)/shard_map/all_to_all | solution.py:41
  109.4 9.2 %all-to-all-done.2.mixed_ref = bf16[8,192,128]{2,1,0:T(8,128)(2,1)S(1)} async-done(((bf16[8,192,128]{2,1,0:T(8,128)(2,1)}), bf16[8,192,128]{2,1,0:T(8,128)(2,1)S(1)}, u32[]{:S(2)}, u32[]{:S(2)}) %all-to-all-start.2) | async-done | bytes 393248 | tf_op jit(solution)/shard_map/all_to_all | solution.py:41
  132.3 11.4 %collective-permute-done.2 = bf16[384,1024]{1,0:T(8,128)(2,1)S(1)} collective-permute-done((bf16[384,1024]{1,0:T(8,128)(2,1)S(1)}, bf16[384,1024]{1,0:T(8,128)(2,1)S(1)}, u32[]{:S(2)}, u32[]{:S(2)}) %collective-permute-start.2) | collective-permute-done | bytes 786464 | tf_op jit(solution)/shard_map/ppermute | solution.py:563
  144.8 15.8 %collective-permute-done.3 = bf16[384,1024]{1,0:T(8,128)(2,1)} collective-permute-done((bf16[384,1024]{1,0:T(8,128)(2,1)S(1)}, bf16[384,1024]{1,0:T(8,128)(2,1)}, u32[]{:S(2)}, u32[]{:S(2)}) %collective-permute-start.3) | collective-permute-done | bytes 786464 | tf_op jit(solution)/shard_map/ppermute | solution.py:563
  165.4 10.6 %all-gather.6.cloned.1.call-done.rows_ref = bf16[3072,1152]{1,0:T(8,128)(2,1)} async-done(((bf16[192,1152]{1,0:T(8,128)(2,1)}), bf16[3072,1152]{1,0:T(8,128)(2,1)}) %all-gather.6.cloned.1.call-update) | async-done | bytes 7077904 | tf_op jit(solution)/shard_map/all_gather | solution.py:664
  176.0 33.9 %shard_map.198 = (bf16[2,4,2,192,1024]{4,3,2,1,0:T(8,128)(2,1)}, bf16[16,2,64,1024]{3,2,1,0:T(8,128)(2,1)}, bf16[2,3,1024,512]{3,2,1,0:T(8,128)(2,1)}) custom-call(bf16[3072,1152]{1,0:T(8,128)(2,1)} %all-gather.6.cloned.1.call-done.rows_ref, bf16[3072,1152]{1,0:T(8,128)(2,1)} %all-gather.8.cloned.1.call-done.cot_ref, f32[2,4,4,192]{3,2,1,0:T(4,128)} %copy.77.slots_ref, ...), custom_call_target="tpu_custom_call" | custom-call | tf_op jit(solution)/shard_map/pallas_call | solution.py:396
  209.9 5.1 %all-to-all-start.3 = ((bf16[16,2,64,1024]{3,2,1,0:T(8,128)(2,1)}), bf16[16,2,64,1024]{3,2,1,0:T(8,128)(2,1)}, u32[]{:S(2)}, u32[]{:S(2)}) async-start(bf16[16,2,64,1024]{3,2,1,0:T(8,128)(2,1)} %get-tuple-element.77), calls=%async_computation.3 | async-start | bytes 8388608 | tf_op jit(solution)/shard_map/all_to_all | solution.py:41
  229.0 29.8 %collective-permute-done.6 = bf16[1536,512]{1,0:T(8,128)(2,1)} collective-permute-done((bf16[1536,512]{1,0:T(8,128)(2,1)}, bf16[1536,512]{1,0:T(8,128)(2,1)}, u32[]{:S(2)}, u32[]{:S(2)}) %collective-permute-start.6) | collective-permute-done | bytes 1572896 | tf_op jit(solution)/shard_map/ppermute | solution.py:563
  270.0 9.1 %shard_map.199 = (f32[192,1024]{1,0:T(8,128)}, bf16[8,192,128]{2,1,0:T(8,128)(2,1)}, bf16[1024,1152]{1,0:T(8,128)(2,1)}) custom-call(bf16[2048,1024]{1,0:T(8,128)(2,1)} %bitcast.11.back_ref, bf16[192,2048]{1,0:T(8,128)(2,1)} %compare_convert_fusion.spots_ref, bf16[2048,128]{1,0:T(8,128)(2,1)} %fusion.6.spread_ref, bf16[3,2048]{1,0:T(4,128)(2,1)} %reshape.295.gate_rows_ref, ...), custom_call_target="tpu_custom_call" | custom-call | tf_op jit(solution)/shard_map/pallas_call | solution.py:476
  279.1 5.4 %all-to-all-start.4 = ((bf16[8,192,128]{2,1,0:T(8,128)(2,1)}), bf16[8,192,128]{2,1,0:T(8,128)(2,1)S(1)}, u32[]{:S(2)}, u32[]{:S(2)}) async-start(bf16[8,192,128]{2,1,0:T(8,128)(2,1)} %get-tuple-element.83), calls=%async_computation.4 | async-start | bytes 786432 | tf_op jit(solution)/shard_map/all_to_all | solution.py:41
  286.9 7.0 %all-to-all-done.4 = bf16[8,192,128]{2,1,0:T(8,128)(2,1)S(1)} async-done(((bf16[8,192,128]{2,1,0:T(8,128)(2,1)}), bf16[8,192,128]{2,1,0:T(8,128)(2,1)S(1)}, u32[]{:S(2)}, u32[]{:S(2)}) %all-to-all-start.4) | async-done | bytes 393248 | tf_op jit(solution)/shard_map/all_to_all | solution.py:41
  301.8 5.0 %all-to-all-start.5 = ((bf16[16,64,1152]{2,1,0:T(8,128)(2,1)}), bf16[16,64,1152]{2,1,0:T(8,128)(2,1)S(1)}, u32[]{:S(2)}, u32[]{:S(2)}) async-start(bf16[16,64,1152]{2,1,0:T(8,128)(2,1)} %bitcast.93), calls=%async_computation.5 | async-start | bytes 4718592 | tf_op jit(solution)/shard_map/all_to_all | solution.py:41
  307.0 18.0 %shard_map.200 = bf16[1536,256]{1,0:T(8,128)(2,1)} custom-call(bf16[1536,256]{1,0:T(8,128)(2,1)} %bitcast.82, bf16[1536,256]{1,0:T(8,128)(2,1)} %bitcast.83, bf16[1536,128]{1,0:T(8,128)(2,1)} %bitcast.94, s32[6,1,256]{2,1,0:T(1,128)} %select_n.195.start_ref, f32[6,1,512]{2,1,0:T(1,128)} %get-tuple-element.87.lse_ref, ...), custom_call_target="tpu_custom_call" | custom-call | tf_op jit(solution)/shard_map/pallas_call | solution.py:234
  347.7 5.2 %all-to-all-start.6 = ((bf16[8,8,1152]{2,1,0:T(8,128)(2,1)}), bf16[8,8,1152]{2,1,0:T(8,128)(2,1)S(1)}, u32[]{:S(2)}, u32[]{:S(2)}) async-start(bf16[8,8,1152]{2,1,0:T(8,128)(2,1)} %bitcast.98), calls=%async_computation.6 | async-start | bytes 294912 | tf_op jit(solution)/shard_map/all_to_all | solution.py:41
  353.0 7.5 %collective-permute-done.10 = bf16[768,512]{1,0:T(8,128)(2,1)} collective-permute-done((bf16[768,512]{1,0:T(8,128)(2,1)S(1)}, bf16[768,512]{1,0:T(8,128)(2,1)}, u32[]{:S(2)}, u32[]{:S(2)}) %collective-permute-start.10) | collective-permute-done | bytes 786464 | tf_op jit(solution)/shard_map/ppermute | solution.py:563
  361.0 4.8 %all-to-all-start.7 = ((bf16[16,64,256]{2,1,0:T(8,128)(2,1)}), bf16[16,64,256]{2,1,0:T(8,128)(2,1)S(1)}, u32[]{:S(2)}, u32[]{:S(2)}) async-start(bf16[16,64,256]{2,1,0:T(8,128)(2,1)} %bitcast.100), calls=%async_computation.7 | async-start | bytes 1048576 | tf_op jit(solution)/shard_map/all_to_all | solution.py:41
  370.4 6.2 %all-to-all-done.7 = bf16[16,64,256]{2,1,0:T(8,128)(2,1)S(1)} async-done(((bf16[16,64,256]{2,1,0:T(8,128)(2,1)}), bf16[16,64,256]{2,1,0:T(8,128)(2,1)S(1)}, u32[]{:S(2)}, u32[]{:S(2)}) %all-to-all-start.7) | async-done | bytes 524320 | tf_op jit(solution)/shard_map/all_to_all | solution.py:41
  377.4 5.3 %all-to-all-start.8 = ((bf16[8,192,256]{2,1,0:T(8,128)(2,1)}), bf16[8,192,256]{2,1,0:T(8,128)(2,1)S(1)}, u32[]{:S(2)}, u32[]{:S(2)}) async-start(bf16[8,192,256]{2,1,0:T(8,128)(2,1)} %bitcast.19), calls=%async_computation.8 | async-start | bytes 1572864 | tf_op jit(solution)/shard_map/all_to_all | solution.py:41
  391.1 8.9 %all-to-all-done.8 = bf16[8,192,256]{2,1,0:T(8,128)(2,1)S(1)} async-done(((bf16[8,192,256]{2,1,0:T(8,128)(2,1)}), bf16[8,192,256]{2,1,0:T(8,128)(2,1)S(1)}, u32[]{:S(2)}, u32[]{:S(2)}) %all-to-all-start.8) | async-done | bytes 786464 | tf_op jit(solution)/shard_map/all_to_all | solution.py:41
  (246 shorter events, 171.6 us)
Async XLA Ops:
  7.2 50.6 %all-gather.4.cloned.1.call-start = ((), (), s32[]{:S(2)}) async-start(), calls=%async_computation.10 | async-start | bytes 6963200 | tf_op jit(solution)/shard_map/all_gather | solution.py:613
  11.6 117.1 %all-gather.8.cloned.1.call-start = ((), (), s32[]{:S(2)}) async-start(), calls=%async_computation.12 | async-start | bytes 7520256 | tf_op jit(solution)/shard_map/all_gather | solution.py:631
  88.1 21.1 %collective-permute-start = (bf16[192,1024]{1,0:T(8,128)(2,1)S(1)}, bf16[192,1024]{1,0:T(8,128)(2,1)S(1)}, u32[]{:S(2)}, u32[]{:S(2)}) collective-permute-start(bf16[192,1024]{1,0:T(8,128)(2,1)S(1)} %copy-done.30), channel_id=1, source_target_pairs={{0,1},{1,0},{2,3},{3,2},{4,5},{5,4},{6,7},{7,6},{8,9},{9,8},{10,11... | collective-permute-start | bytes 1179656 | tf_op jit(solution)/shard_map/ppermute | solution.py:563
  108.6 67.4 %all-gather.6.cloned.1.call-start = ((), (), s32[]{:S(2)}) async-start(), calls=%async_computation.11 | async-start | bytes 7520256 | tf_op jit(solution)/shard_map/all_gather | solution.py:664
  123.2 20.6 %collective-permute-start.2 = (bf16[384,1024]{1,0:T(8,128)(2,1)S(1)}, bf16[384,1024]{1,0:T(8,128)(2,1)S(1)}, u32[]{:S(2)}, u32[]{:S(2)}) collective-permute-start(bf16[384,1024]{1,0:T(8,128)(2,1)S(1)} %pad_maximum_fusion.2), channel_id=1, source_target_pairs={{0,2},{1,3},{2,0},{3,1},{4,6},{5,7},{6,4},{7,5},{8,10},{9,11},{10,... | collective-permute-start | bytes 2359304 | tf_op jit(solution)/shard_map/ppermute | solution.py:563
  124.3 36.3 %collective-permute-start.3 = (bf16[384,1024]{1,0:T(8,128)(2,1)S(1)}, bf16[384,1024]{1,0:T(8,128)(2,1)}, u32[]{:S(2)}, u32[]{:S(2)}) collective-permute-start(bf16[384,1024]{1,0:T(8,128)(2,1)S(1)} %pad_maximum_fusion.2), channel_id=1, source_target_pairs={{0,4},{1,5},{2,6},{3,7},{4,0},{5,1},{6,2},{7,3},{8,12},{9,13},{10,... | collective-permute-start | bytes 2359304 | tf_op jit(solution)/shard_map/ppermute | solution.py:563
  126.7 36.7 %collective-permute-start.4 = (bf16[384,1024]{1,0:T(8,128)(2,1)S(1)}, bf16[384,1024]{1,0:T(8,128)(2,1)}, u32[]{:S(2)}, u32[]{:S(2)}) collective-permute-start(bf16[384,1024]{1,0:T(8,128)(2,1)S(1)} %pad_maximum_fusion.2), channel_id=1, source_target_pairs={{0,6},{1,7},{2,4},{3,5},{4,2},{5,3},{6,0},{7,1},{8,14},{9,15},{10,... | collective-permute-start | bytes 2359304 | tf_op jit(solution)/shard_map/ppermute | solution.py:563
  209.9 55.8 %all-to-all-start.3 = ((bf16[16,2,64,1024]{3,2,1,0:T(8,128)(2,1)}), bf16[16,2,64,1024]{3,2,1,0:T(8,128)(2,1)}, u32[]{:S(2)}, u32[]{:S(2)}) async-start(bf16[16,2,64,1024]{3,2,1,0:T(8,128)(2,1)} %get-tuple-element.77), calls=%async_computation.3 | async-start | bytes 8388608 | tf_op jit(solution)/shard_map/all_to_all | solution.py:41
  220.5 38.3 %collective-permute-start.6 = (bf16[1536,512]{1,0:T(8,128)(2,1)}, bf16[1536,512]{1,0:T(8,128)(2,1)}, u32[]{:S(2)}, u32[]{:S(2)}) collective-permute-start(bf16[1536,512]{1,0:T(8,128)(2,1)} %constant_dynamic-slice_fusion.9), channel_id=1, source_target_pairs={{0,6},{1,7},{2,4},{3,5},{4,2},{5,3},{6,0},{7,1},{8,14},{9,15},{10,... | collective-permute-start | bytes 4718600 | tf_op jit(solution)/shard_map/ppermute | solution.py:563
  224.7 37.0 %collective-permute-start.5 = (bf16[1536,512]{1,0:T(8,128)(2,1)}, bf16[1536,512]{1,0:T(8,128)(2,1)}, u32[]{:S(2)}, u32[]{:S(2)}) collective-permute-start(bf16[1536,512]{1,0:T(8,128)(2,1)} %constant_dynamic-slice_fusion.11), channel_id=1, source_target_pairs={{0,2},{1,3},{2,0},{3,1},{4,6},{5,7},{6,4},{7,5},{8,10},{9,11},{10,... | collective-permute-start | bytes 4718600 | tf_op jit(solution)/shard_map/ppermute | solution.py:563
  229.0 101.2 %collective-permute-start.1 = (bf16[4,2,192,1024]{3,2,1,0:T(8,128)(2,1)}, bf16[4,2,192,1024]{3,2,1,0:T(8,128)(2,1)}, u32[]{:S(2)}, u32[]{:S(2)}) collective-permute-start(bf16[4,2,192,1024]{3,2,1,0:T(8,128)(2,1)} %dynamic-slice_bitcast_fusion), channel_id=1, source_target_pairs={{0,8},{8,0},{16,24},{24,16},{32,40},{40,32},{48,56},{56,48},{64,72... | collective-permute-start | bytes 9437192 | tf_op jit(solution)/shard_map/ppermute | solution.py:563
  265.7 28.1 %collective-permute-start.7 = (bf16[768,512]{1,0:T(8,128)(2,1)}, bf16[768,512]{1,0:T(8,128)(2,1)}, u32[]{:S(2)}, u32[]{:S(2)}) collective-permute-start(bf16[768,512]{1,0:T(8,128)(2,1)} %constant_dynamic-slice_fusion.10), channel_id=1, source_target_pairs={{0,6},{1,7},{2,4},{3,5},{4,2},{5,3},{6,0},{7,1},{8,14},{9,15},{10,... | collective-permute-start | bytes 2359304 | tf_op jit(solution)/shard_map/ppermute | solution.py:563
  268.4 25.4 %collective-permute-start.8 = (bf16[768,512]{1,0:T(8,128)(2,1)}, bf16[768,512]{1,0:T(8,128)(2,1)}, u32[]{:S(2)}, u32[]{:S(2)}) collective-permute-start(bf16[768,512]{1,0:T(8,128)(2,1)} %constant_dynamic-slice_fusion.8), channel_id=1, source_target_pairs={{0,2},{1,3},{2,0},{3,1},{4,6},{5,7},{6,4},{7,5},{8,10},{9,11},{10,... | collective-permute-start | bytes 2359304 | tf_op jit(solution)/shard_map/ppermute | solution.py:563
  298.6 26.3 %collective-permute-start.9 = (bf16[768,512]{1,0:T(8,128)(2,1)S(1)}, bf16[768,512]{1,0:T(8,128)(2,1)}, u32[]{:S(2)}, u32[]{:S(2)}) collective-permute-start(bf16[768,512]{1,0:T(8,128)(2,1)S(1)} %pad_maximum_fusion.3), channel_id=1, source_target_pairs={{0,1},{1,0},{2,3},{3,2},{4,5},{5,4},{6,7},{7,6},{8,9},{9,8},{10,11... | collective-permute-start | bytes 2359304 | tf_op jit(solution)/shard_map/ppermute | solution.py:563
  301.8 44.9 %all-to-all-start.5 = ((bf16[16,64,1152]{2,1,0:T(8,128)(2,1)}), bf16[16,64,1152]{2,1,0:T(8,128)(2,1)S(1)}, u32[]{:S(2)}, u32[]{:S(2)}) async-start(bf16[16,64,1152]{2,1,0:T(8,128)(2,1)} %bitcast.93), calls=%async_computation.5 | async-start | bytes 4718592 | tf_op jit(solution)/shard_map/all_to_all | solution.py:41
  331.6 28.9 %collective-permute-start.10 = (bf16[768,512]{1,0:T(8,128)(2,1)S(1)}, bf16[768,512]{1,0:T(8,128)(2,1)}, u32[]{:S(2)}, u32[]{:S(2)}) collective-permute-start(bf16[768,512]{1,0:T(8,128)(2,1)S(1)} %add_convert_fusion.2), channel_id=1, source_target_pairs={{0,1},{1,0},{2,3},{3,2},{4,5},{5,4},{6,7},{7,6},{8,9},{9,8},{10,11... | collective-permute-start | bytes 2359304 | tf_op jit(solution)/shard_map/ppermute | solution.py:563
  340.2 46.6 %collective-permute-start.14 = (bf16[2,192,1024]{2,1,0:T(8,128)(2,1)}, bf16[2,192,1024]{2,1,0:T(8,128)(2,1)}, u32[]{:S(2)}, u32[]{:S(2)}) collective-permute-start(bf16[2,192,1024]{2,1,0:T(8,128)(2,1)} %pad_maximum_fusion.7), channel_id=1, source_target_pairs={{0,96},{8,104},{16,112},{24,120},{32,64},{40,72},{48,80},{56,88},{... | collective-permute-start | bytes 2359304 | tf_op jit(solution)/shard_map/ppermute | solution.py:563
  344.3 42.4 %collective-permute-start.13 = (bf16[2,192,1024]{2,1,0:T(8,128)(2,1)}, bf16[2,192,1024]{2,1,0:T(8,128)(2,1)}, u32[]{:S(2)}, u32[]{:S(2)}) collective-permute-start(bf16[2,192,1024]{2,1,0:T(8,128)(2,1)} %pad_maximum_fusion.6), channel_id=1, source_target_pairs={{0,32},{8,40},{16,48},{24,56},{32,0},{40,8},{48,16},{56,24},{64,96... | collective-permute-start | bytes 2359304 | tf_op jit(solution)/shard_map/ppermute | solution.py:563
  367.9 20.7 %collective-permute-start.12 = (bf16[768,512]{1,0:T(8,128)(2,1)}, bf16[768,512]{1,0:T(8,128)(2,1)}, u32[]{:S(2)}, u32[]{:S(2)}) collective-permute-start(bf16[768,512]{1,0:T(8,128)(2,1)} %pad_maximum_fusion.5), channel_id=1, source_target_pairs={{0,2},{1,3},{2,0},{3,1},{4,6},{5,7},{6,4},{7,5},{8,10},{9,11},{10,... | collective-permute-start | bytes 2359304 | tf_op jit(solution)/shard_map/ppermute | solution.py:563
  369.2 21.9 %collective-permute-start.11 = (bf16[768,512]{1,0:T(8,128)(2,1)}, bf16[768,512]{1,0:T(8,128)(2,1)}, u32[]{:S(2)}, u32[]{:S(2)}) collective-permute-start(bf16[768,512]{1,0:T(8,128)(2,1)} %pad_maximum_fusion.4), channel_id=1, source_target_pairs={{0,6},{1,7},{2,4},{3,5},{4,2},{5,3},{6,0},{7,1},{8,14},{9,15},{10,... | collective-permute-start | bytes 2359304 | tf_op jit(solution)/shard_map/ppermute | solution.py:563
  377.4 22.6 %all-to-all-start.8 = ((bf16[8,192,256]{2,1,0:T(8,128)(2,1)}), bf16[8,192,256]{2,1,0:T(8,128)(2,1)S(1)}, u32[]{:S(2)}, u32[]{:S(2)}) async-start(bf16[8,192,256]{2,1,0:T(8,128)(2,1)} %bitcast.19), calls=%async_computation.8 | async-start | bytes 1572864 | tf_op jit(solution)/shard_map/all_to_all | solution.py:41
  405.4 29.4 %all-to-all-start.9 = ((bf16[8,112,256]{2,1,0:T(8,128)(2,1)}), bf16[8,112,256]{2,1,0:T(8,128)(2,1)S(1)}, u32[]{:S(2)}, u32[]{:S(2)}) async-start(bf16[8,112,256]{2,1,0:T(8,128)(2,1)} %broadcast_in_dim.80), calls=%async_computation.9 | async-start | bytes 917504 | tf_op jit(solution)/shard_map/all_to_all | solution.py:41
  409.2 40.9 %collective-permute-start.19 = (bf16[1536,512]{1,0:T(8,128)(2,1)}, bf16[1536,512]{1,0:T(8,128)(2,1)}, u32[]{:S(2)}, u32[]{:S(2)}) collective-permute-start(bf16[1536,512]{1,0:T(8,128)(2,1)} %pad_maximum_fusion.1.rows_ref), channel_id=1, source_target_pairs={{0,2},{1,3},{2,0},{3,1},{4,6},{5,7},{6,4},{7,5},{8,10},{9,11},{10,... | collective-permute-start | bytes 4718600 | tf_op jit(solution)/shard_map/ppermute | solution.py:563
  411.2 43.4 %collective-permute-start.18 = (bf16[1536,512]{1,0:T(8,128)(2,1)S(1)}, bf16[1536,512]{1,0:T(8,128)(2,1)}, u32[]{:S(2)}, u32[]{:S(2)}) collective-permute-start(bf16[1536,512]{1,0:T(8,128)(2,1)S(1)} %pad_maximum_fusion.rows_ref), channel_id=1, source_target_pairs={{0,6},{1,7},{2,4},{3,5},{4,2},{5,3},{6,0},{7,1},{8,14},{9,15},{10,... | collective-permute-start | bytes 4718600 | tf_op jit(solution)/shard_map/ppermute | solution.py:563
  (47 other events, 356.3 us)
Sparse Core Ops, SparseCore 0:
  11.8 45.9 all-gather.3
  59.5 67.8 all-gather.7
  129.1 46.8 all-gather.5

commit v4 on v3

--- a/solution.py
+++ b/solution.py
@@ -537,26 +537,35 @@
     )(parts, query_weight, key_matrix, value_matrix, norm_one.astype(F32)[:, None])
 
 
-def widen_kernel(places_ref, rows_ref, *refs):
-    refs[-1][...] = rows_ref[...].astype(F32)
-
-
-def widen(rows, places, total=None):
-    steps = 4
-    block = rows.shape[0] // steps
+def widen_kernel(places_ref, *refs):
+    step = pl.program_id(0)
+    out_ref = refs[-1]
+    for n in range(places_ref.shape[0] // 2):
+
+        @pl.when(step // 2 == n)
+        def store(n=n):
+            out_ref[...] = refs[n][...].astype(F32)
+
+
+def widen(arrays, places, total=None):
+    block = arrays[0].shape[0] // 2
     given = () if total is None else (total,)
+
+    def taken(n):
+        return pl.BlockSpec((block, FF), lambda i, places: (jnp.clip(i - 2 * n, 0, 1), 0))
+
     return pl.pallas_call(
         widen_kernel,
         grid_spec=pltpu.PrefetchScalarGridSpec(
             num_scalar_prefetch=1,
-            grid=(steps,),
-            in_specs=[pl.BlockSpec((block, FF), lambda i, places: (i, 0))]
+            grid=(2 * len(arrays),),
+            in_specs=[taken(n) for n in range(len(arrays))]
             + [pl.BlockSpec(memory_space=pl.ANY)] * len(given),
             out_specs=pl.BlockSpec((block, FF), lambda i, places: (places[i], 0)),
         ),
         out_shape=jax.ShapeDtypeStruct((6 * D, FF), F32),
-        input_output_aliases={2: 0} if given else {},
-    )(places.astype(jnp.int32), rows, *given)
+        input_output_aliases={1 + len(arrays): 0} if given else {},
+    )(jnp.concatenate(places).astype(jnp.int32), *arrays, *given)
 
 
 def exchange(x, bits, axis="replica"):
@@ -680,8 +689,9 @@
     keep_b, send_b = halves(add_low(keep_b, got_b), low_bit)
     core, row, layer = shard % 2, shard // 2 % 2, shard // 4
     pick = lambda x, at: lax.dynamic_index_in_dim(x, at, 0, keepdims=False)
-    from_core = exchange(pick(combined, 1 - core), 1, "shard")
-    back, send_a, send_b = lax.optimization_barrier((back, send_a, send_b))
+    for_core = pick(combined, 1 - core)
+    back, send_a, send_b, for_core = lax.optimization_barrier((back, send_a, send_b, for_core))
+    from_core = exchange(for_core, 1, "shard")
     got_a, got_b = exchange(send_a, 6), exchange(send_b, 2)
 
     gate_rows = back.reshape(E, SLOTS, D)[:, 60:63, :SLOTS].transpose(1, 0, 2).reshape(3, E * SLOTS)
@@ -741,30 +751,35 @@
         [heads_sum, dense_total.reshape(36, 256), jnp.zeros((12, 256), BF)], axis=0
     )
     by_token = split_all(after(head_grad, heads_parts).reshape(NR, TOK, 256), "replica")
-    by_token, other_a, other_b, *layers = lax.optimization_barrier(
-        (by_token, other_a, other_b, *layers)
-    )
-    own_a = jnp.concatenate([own_a, other_a], axis=0)
-    own_b = jnp.concatenate([own_b, other_b], axis=0)
-    other_a, other_b = exchange(own_a, 2), exchange(own_b, 6)
-    last = spread_all(after(last, by_token), "replica", NR)
-
-    def places(first, bit, low):
-        return first + 4 * bit + jnp.stack(
-            [2 * at + near for at in (low, 1 - low) for near in (side, 1 - side)]
-        )
-
-    expert_total = widen(own_a, places(0, mixed_bit, low_bit))
-    expert_total = widen(own_b, places(8, high_bit, low_bit), expert_total)
-    last, expert_total = lax.optimization_barrier((last, expert_total))
+    layers = [after(part, heads_sum) for part in layers]
     keep = [[add_low(keep[y][n], layers[y][n]) for n in range(2)] for y in range(2)]
     layers = [exchange(keep[0][1], 12, "shard"), exchange(keep[1][1], 4, "shard")]
+    next_a, next_b = exchange(after(own_a, heads_sum), 2), exchange(after(own_b, heads_sum), 6)
+    by_token, other_a, other_b = lax.optimization_barrier((by_token, other_a, other_b))
+    rest_a, rest_b = exchange(other_a, 2), exchange(other_b, 6)
+    last = spread_all(after(last, by_token), "replica", NR)
+
+    def places(first, bit, low):
+        return first + 4 * bit + 2 * low + jnp.stack([side, 1 - side])
+
+    expert_total = widen(
+        [own_a, own_b, other_a, other_b, next_a, next_b],
+        [
+            places(0, mixed_bit, low_bit),
+            places(8, high_bit, low_bit),
+            places(0, mixed_bit, 1 - low_bit),
+            places(8, high_bit, 1 - low_bit),
+            places(0, 1 - mixed_bit, 1 - low_bit),
+            places(8, 1 - high_bit, 1 - low_bit),
+        ],
+    )
+    last, expert_total = lax.optimization_barrier((last, expert_total))
     query_grad, key_grad, value_grad, norm_one_grad = finish_heads(
         last, query_weight, key_matrix, value_matrix, norm_one
     )
     dense_last = last[:, 64:100].reshape(64, 1152).astype(F32)
 
-    layers = [after(part, last) for part in layers]
+    layers = [after(part, by_token) for part in layers]
     normed_grad = mm(by_token.transpose(1, 0, 2).reshape(TOK, 2048), gathered[:, :2048], NT)
     tokens_wide = tokens.astype(F32)
     inverse = lax.rsqrt(jnp.mean(tokens_wide * tokens_wide, axis=-1, keepdims=True) + EPSILON)
@@ -779,8 +794,11 @@
     from_side = exchange(jnp.where(row == 0, sides[1], sides[0]), 2, "shard")
     from_side = after(from_side, tokens_grad)
     layer_out = (middle + own_side.astype(F32) + from_side.astype(F32)).astype(BF)
-    expert_total = widen(other_a, places(0, 1 - mixed_bit, 1 - low_bit), expert_total)
-    expert_total = widen(other_b, places(8, 1 - high_bit, 1 - low_bit), expert_total)
+    expert_total = widen(
+        [rest_a, rest_b],
+        [places(0, 1 - mixed_bit, low_bit), places(8, 1 - high_bit, low_bit)],
+        expert_total,
+    )
     expert_total = expert_total.reshape(2, 3, D, FF)
     return (
         layer_out,

time: 475 us -> 481 us (1.013)
  local copies, waits for them, and re-layouts: 45 us -> 50.8 us
    ppermute x20 -> x22, waiting for transfers between devices: 71.1 us -> 80.8 us  [exchange(): lax.ppermute(x, axis, [(i, i ^ bits) for i in range(lax.axis_size(axis))])]
    all_to_all x9, waiting for transfers between devices: 33.9 us -> 24.7 us  [split_all(): return lax.all_to_all(x, axis, 0, 0, tiled=True)]
    pallas_call x4 -> x2, Pallas kernels: 18.2 us -> 15.7 us  [widen(): pl.pallas_call(widen_kernel, grid_spec=pltpu.PrefetchScalarGridSpec(num_s...]
    ppermute x20 -> x22, starting transfers between devices: 29.2 us -> 30.7 us  [exchange(): lax.ppermute(x, axis, [(i, i ^ bits) for i in range(lax.axis_size(axis))])]
  transfers between devices with their start and end apart: 32 -> 34, of which waited for: 17 -> 14; matrix products, arithmetic and copies ran while one was open for 19% -> 21% of each run, Pallas kernels for 14% -> 14%
where the time goes in v4:
time: 481 us; the launch traced here: 472 us
  waiting for transfers between devices  139 us (29%)
  Pallas kernels  103 us (21%)
  starting transfers between devices  79.5 us (17%)
  other arithmetic  52.2 us (11%)
  local copies, waits for them, and re-layouts  50.8 us (11%)
  blocking collectives  22.4 us (5%)
  between operations  16.1 us (3%)
  matrix products  8.04 us (2%)
    ppermute x22, waiting for transfers between devices, exchange(): lax.ppermute(x, axis, [(i, i ^ bits) for i in range(lax.axis_size(axis))])  80.8 us
    all_to_all x9, starting transfers between devices, split_all(): return lax.all_to_all(x, axis, 0, 0, tiled=True)  48.7 us
    pallas_call x1, Pallas kernels, run_experts(): pl.pallas_call(expert_kernel, grid=(CHUNKS + 6,), in_specs=[taken, taken,...  33.9 us
    ppermute x22, starting transfers between devices, exchange(): lax.ppermute(x, axis, [(i, i ^ bits) for i in range(lax.axis_size(axis))])  30.7 us
    all_to_all x9, waiting for transfers between devices, split_all(): return lax.all_to_all(x, axis, 0, 0, tiled=True)  24.7 us
    all_gather x1, waiting for transfers between devices, per_device(): lax.all_gather(jnp.concatenate([grouped, out_weight, small], axis=1), 'sh...  23.2 us
    all_to_all x1, blocking collectives, split_all(): return lax.all_to_all(x, axis, 0, 0, tiled=True)  22.4 us
    pallas_call x1, Pallas kernels, attend_back(): pl.pallas_call(attend_back_kernel, grid=(NQ,), in_specs=[block, whole(2 *...  18 us
  transfers between devices with their start and end apart: 34, of which 14 were waited for; matrix products, arithmetic and copies ran while one was open for 21% of the time, Pallas kernels for 14%

profile of v4, /device:TPU:0, one launch (start us, length us, event | category | flops | bytes accessed | tf_op | source)
XLA Modules:
  0.0 471.8 jit_solution(14517637870696943115)
XLA Ops:
  13.9 7.0 %all-to-all-start = ((s32[8,1,192]{2,1,0:T(1,128)}), s32[8,1,192]{2,1,0:T(1,128)S(1)}, u32[]{:S(2)}, u32[]{:S(2)}) async-start(s32[8,1,192]{2,1,0:T(1,128)} %broadcast_in_dim.67), calls=%async_computation | async-start | bytes 16384 | tf_op jit(solution)/shard_map/all_to_all | solution.py:41
  34.6 23.2 %all-gather.4.cloned.1.call-done.weight_ref.small_ref.out_ref = bf16[1024,3200]{1,0:T(8,128)(2,1)} async-done(((bf16[64,3200]{1,0:T(8,128)(2,1)}), bf16[1024,3200]{1,0:T(8,128)(2,1)}) %all-gather.4.cloned.1.call-update) | async-done | bytes 6553616 | tf_op jit(solution)/shard_map/all_gather | solution.py:622
  57.8 7.9 %shard_map.195 = (bf16[8,192,256]{2,1,0:T(8,128)(2,1)}, bf16[192,1024]{1,0:T(8,128)(2,1)}, f32[8,1024]{1,0:T(8,128)}) custom-call(bf16[192,1024]{1,0:T(8,128)(2,1)} %tokens_ref.2, bf16[1024,3200]{1,0:T(8,128)(2,1)} %all-gather.4.cloned.1.call-done.weight_ref.small_ref.out_ref, bf16[1024,3200]{1,0:T(8,128)(2,1)} %all-gather.4.cloned.1.call-done.weight_ref.small_ref.out_ref, ...), custom_call_target="tpu_custom_call" | custom-call | tf_op jit(solution)/shard_map/pallas_call | solution.py:84
  65.7 22.4 %all_to_all.51 = bf16[8,192,256]{2,1,0:T(8,128)(2,1)} all-to-all(bf16[8,192,256]{2,1,0:T(8,128)(2,1)} %get-tuple-element.68), channel_id=1, replica_groups=mesh['shard'=16,'replica'=8] {'replica'}, dimensions={0} | all-to-all | bytes 1572864 | tf_op jit(solution)/shard_map/all_to_all | solution.py:41
  89.0 13.1 %shard_map.196 = (bf16[1536,128]{1,0:T(8,128)(2,1)}, f32[6,1,512]{2,1,0:T(1,128)}) custom-call(bf16[1536,256]{1,0:T(8,128)(2,1)} %bitcast.78, bf16[1536,256]{1,0:T(8,128)(2,1)} %bitcast.79, s32[6,1,256]{2,1,0:T(1,128)} %select_n.195.start_ref), custom_call_target="tpu_custom_call" | custom-call | tf_op jit(solution)/shard_map/pallas_call | solution.py:141
  102.1 6.5 %all-to-all-start.2 = ((bf16[8,192,128]{2,1,0:T(8,128)(2,1)}), bf16[8,192,128]{2,1,0:T(8,128)(2,1)S(1)}, u32[]{:S(2)}, u32[]{:S(2)}) async-start(bf16[8,192,128]{2,1,0:T(8,128)(2,1)} %bitcast.96), calls=%async_computation.2 | async-start | bytes 786432 | tf_op jit(solution)/shard_map/all_to_all | solution.py:41
  109.4 9.2 %all-to-all-done.2.mixed_ref = bf16[8,192,128]{2,1,0:T(8,128)(2,1)S(1)} async-done(((bf16[8,192,128]{2,1,0:T(8,128)(2,1)}), bf16[8,192,128]{2,1,0:T(8,128)(2,1)S(1)}, u32[]{:S(2)}, u32[]{:S(2)}) %all-to-all-start.2) | async-done | bytes 393248 | tf_op jit(solution)/shard_map/all_to_all | solution.py:41
  132.3 11.4 %collective-permute-done.1 = bf16[384,1024]{1,0:T(8,128)(2,1)S(1)} collective-permute-done((bf16[384,1024]{1,0:T(8,128)(2,1)S(1)}, bf16[384,1024]{1,0:T(8,128)(2,1)S(1)}, u32[]{:S(2)}, u32[]{:S(2)}) %collective-permute-start.1) | collective-permute-done | bytes 786464 | tf_op jit(solution)/shard_map/ppermute | solution.py:572
  144.8 15.8 %collective-permute-done.2 = bf16[384,1024]{1,0:T(8,128)(2,1)} collective-permute-done((bf16[384,1024]{1,0:T(8,128)(2,1)S(1)}, bf16[384,1024]{1,0:T(8,128)(2,1)}, u32[]{:S(2)}, u32[]{:S(2)}) %collective-permute-start.2) | collective-permute-done | bytes 786464 | tf_op jit(solution)/shard_map/ppermute | solution.py:572
  165.4 10.6 %all-gather.6.cloned.1.call-done.rows_ref = bf16[3072,1152]{1,0:T(8,128)(2,1)} async-done(((bf16[192,1152]{1,0:T(8,128)(2,1)}), bf16[3072,1152]{1,0:T(8,128)(2,1)}) %all-gather.6.cloned.1.call-update) | async-done | bytes 7077904 | tf_op jit(solution)/shard_map/all_gather | solution.py:673
  176.0 33.9 %shard_map.198 = (bf16[2,4,2,192,1024]{4,3,2,1,0:T(8,128)(2,1)}, bf16[16,2,64,1024]{3,2,1,0:T(8,128)(2,1)}, bf16[2,3,1024,512]{3,2,1,0:T(8,128)(2,1)}) custom-call(bf16[3072,1152]{1,0:T(8,128)(2,1)} %all-gather.6.cloned.1.call-done.rows_ref, bf16[3072,1152]{1,0:T(8,128)(2,1)} %all-gather.8.cloned.1.call-done.cot_ref, f32[2,4,4,192]{3,2,1,0:T(4,128)} %copy.75.slots_ref, ...), custom_call_target="tpu_custom_call" | custom-call | tf_op jit(solution)/shard_map/pallas_call | solution.py:396
  209.9 5.2 %all-to-all-start.3 = ((bf16[16,2,64,1024]{3,2,1,0:T(8,128)(2,1)}), bf16[16,2,64,1024]{3,2,1,0:T(8,128)(2,1)}, u32[]{:S(2)}, u32[]{:S(2)}) async-start(bf16[16,2,64,1024]{3,2,1,0:T(8,128)(2,1)} %get-tuple-element.80), calls=%async_computation.3 | async-start | bytes 8388608 | tf_op jit(solution)/shard_map/all_to_all | solution.py:41
  229.7 28.1 %collective-permute-done.4 = bf16[1536,512]{1,0:T(8,128)(2,1)} collective-permute-done((bf16[1536,512]{1,0:T(8,128)(2,1)}, bf16[1536,512]{1,0:T(8,128)(2,1)}, u32[]{:S(2)}, u32[]{:S(2)}) %collective-permute-start.4) | collective-permute-done | bytes 1572896 | tf_op jit(solution)/shard_map/ppermute | solution.py:572
  270.1 9.0 %shard_map.199 = (f32[192,1024]{1,0:T(8,128)}, bf16[8,192,128]{2,1,0:T(8,128)(2,1)}, bf16[1024,1152]{1,0:T(8,128)(2,1)}) custom-call(bf16[2048,1024]{1,0:T(8,128)(2,1)} %bitcast.11.back_ref, bf16[192,2048]{1,0:T(8,128)(2,1)} %compare_convert_fusion.spots_ref, bf16[2048,128]{1,0:T(8,128)(2,1)} %fusion.6.spread_ref, bf16[3,2048]{1,0:T(4,128)(2,1)} %reshape.295.gate_rows_ref, ...), custom_call_target="tpu_custom_call" | custom-call | tf_op jit(solution)/shard_map/pallas_call | solution.py:476
  279.1 5.7 %all-to-all-start.4 = ((bf16[8,192,128]{2,1,0:T(8,128)(2,1)}), bf16[8,192,128]{2,1,0:T(8,128)(2,1)S(1)}, u32[]{:S(2)}, u32[]{:S(2)}) async-start(bf16[8,192,128]{2,1,0:T(8,128)(2,1)} %get-tuple-element.87), calls=%async_computation.4 | async-start | bytes 786432 | tf_op jit(solution)/shard_map/all_to_all | solution.py:41
  286.0 8.1 %all-to-all-done.4 = bf16[8,192,128]{2,1,0:T(8,128)(2,1)S(1)} async-done(((bf16[8,192,128]{2,1,0:T(8,128)(2,1)}), bf16[8,192,128]{2,1,0:T(8,128)(2,1)S(1)}, u32[]{:S(2)}, u32[]{:S(2)}) %all-to-all-start.4) | async-done | bytes 393248 | tf_op jit(solution)/shard_map/all_to_all | solution.py:41
  315.3 18.0 %shard_map.200 = bf16[1536,256]{1,0:T(8,128)(2,1)} custom-call(bf16[1536,256]{1,0:T(8,128)(2,1)} %bitcast.80, bf16[1536,256]{1,0:T(8,128)(2,1)} %bitcast.81, bf16[1536,128]{1,0:T(8,128)(2,1)} %bitcast.89, s32[6,1,256]{2,1,0:T(1,128)} %select_n.195.start_ref, f32[6,1,512]{2,1,0:T(1,128)} %get-tuple-element.91.lse_ref, ...), custom_call_target="tpu_custom_call" | custom-call | tf_op jit(solution)/shard_map/pallas_call | solution.py:234
  333.4 13.6 %collective-permute-done.9 = bf16[768,512]{1,0:T(8,128)(2,1)} collective-permute-done((bf16[768,512]{1,0:T(8,128)(2,1)}, bf16[768,512]{1,0:T(8,128)(2,1)}, u32[]{:S(2)}, u32[]{:S(2)}) %collective-permute-start.9) | collective-permute-done | bytes 786464 | tf_op jit(solution)/shard_map/ppermute | solution.py:572
  361.2 9.8 %collective-permute-done.11 = bf16[768,512]{1,0:T(8,128)(2,1)} collective-permute-done((bf16[768,512]{1,0:T(8,128)(2,1)S(1)}, bf16[768,512]{1,0:T(8,128)(2,1)}, u32[]{:S(2)}, u32[]{:S(2)}) %collective-permute-start.11) | collective-permute-done | bytes 786464 | tf_op jit(solution)/shard_map/ppermute | solution.py:572
  396.5 6.7 %all-to-all-start.8 = ((bf16[8,192,256]{2,1,0:T(8,128)(2,1)}), bf16[8,192,256]{2,1,0:T(8,128)(2,1)}, u32[]{:S(2)}, u32[]{:S(2)}) async-start(bf16[8,192,256]{2,1,0:T(8,128)(2,1)} %bitcast.24), calls=%async_computation.8 | async-start | bytes 1572864 | tf_op jit(solution)/shard_map/all_to_all | solution.py:41
  413.7 7.3 %all-to-all-done.8 = bf16[8,192,256]{2,1,0:T(8,128)(2,1)} async-done(((bf16[8,192,256]{2,1,0:T(8,128)(2,1)}), bf16[8,192,256]{2,1,0:T(8,128)(2,1)}, u32[]{:S(2)}, u32[]{:S(2)}) %all-to-all-start.8) | async-done | bytes 786464 | tf_op jit(solution)/shard_map/all_to_all | solution.py:41
  423.9 4.8 %all-to-all-start.9 = ((bf16[8,112,256]{2,1,0:T(8,128)(2,1)}), bf16[8,112,256]{2,1,0:T(8,128)(2,1)}, u32[]{:S(2)}, u32[]{:S(2)}) async-start(bf16[8,112,256]{2,1,0:T(8,128)(2,1)} %broadcast_in_dim.80), calls=%async_computation.9 | async-start | bytes 917504 | tf_op jit(solution)/shard_map/all_to_all | solution.py:41
  441.5 11.0 %shard_map.201.refs_2_ = f32[6144,512]{1,0:T(8,128)} custom-call(s32[12]{0:T(128)} %concatenate.66.places_ref, bf16[768,512]{1,0:T(8,128)(2,1)} %pad_maximum_fusion.3.refs_0_, bf16[768,512]{1,0:T(8,128)(2,1)} %pad_maximum_fusion.4.refs_1_, bf16[768,512]{1,0:T(8,128)(2,1)} %collective-permute-done.13.refs_2_, ...), custom_call_target="tpu_custom_call" | custom-call | tf_op jit(solution)/shard_map/pallas_call | solution.py:557
  460.1 4.8 %shard_map.203 = f32[6144,512]{1,0:T(8,128)} custom-call(s32[4]{0:T(128)} %pad_add_fusion.1.places_ref, bf16[768,512]{1,0:T(8,128)(2,1)} %collective-permute-done.20.refs_0_, bf16[768,512]{1,0:T(8,128)(2,1)} %collective-permute-done.21.refs_1_, f32[6144,512]{1,0:T(8,128)} %shard_map.201.refs_2_), custom_call_target="tpu_custom_call", output_to_operand_aliasing={{}: (3, {})} | custom-call | tf_op jit(solution)/shard_map/pallas_call | solution.py:557
  (245 shorter events, 162.7 us)
Async XLA Ops:
  7.2 50.6 %all-gather.4.cloned.1.call-start = ((), (), s32[]{:S(2)}) async-start(), calls=%async_computation.10 | async-start | bytes 6963200 | tf_op jit(solution)/shard_map/all_gather | solution.py:622
  11.6 117.1 %all-gather.8.cloned.1.call-start = ((), (), s32[]{:S(2)}) async-start(), calls=%async_computation.12 | async-start | bytes 7520256 | tf_op jit(solution)/shard_map/all_gather | solution.py:640
  108.6 67.4 %all-gather.6.cloned.1.call-start = ((), (), s32[]{:S(2)}) async-start(), calls=%async_computation.11 | async-start | bytes 7520256 | tf_op jit(solution)/shard_map/all_gather | solution.py:673
  124.3 36.3 %collective-permute-start.2 = (bf16[384,1024]{1,0:T(8,128)(2,1)S(1)}, bf16[384,1024]{1,0:T(8,128)(2,1)}, u32[]{:S(2)}, u32[]{:S(2)}) collective-permute-start(bf16[384,1024]{1,0:T(8,128)(2,1)S(1)} %pad_maximum_fusion), channel_id=1, source_target_pairs={{0,4},{1,5},{2,6},{3,7},{4,0},{5,1},{6,2},{7,3},{8,12},{9,13},{10,... | collective-permute-start | bytes 2359304 | tf_op jit(solution)/shard_map/ppermute | solution.py:572
  126.7 36.7 %collective-permute-start.3 = (bf16[384,1024]{1,0:T(8,128)(2,1)S(1)}, bf16[384,1024]{1,0:T(8,128)(2,1)}, u32[]{:S(2)}, u32[]{:S(2)}) collective-permute-start(bf16[384,1024]{1,0:T(8,128)(2,1)S(1)} %pad_maximum_fusion), channel_id=1, source_target_pairs={{0,6},{1,7},{2,4},{3,5},{4,2},{5,3},{6,0},{7,1},{8,14},{9,15},{10,... | collective-permute-start | bytes 2359304 | tf_op jit(solution)/shard_map/ppermute | solution.py:572
  209.9 55.6 %all-to-all-start.3 = ((bf16[16,2,64,1024]{3,2,1,0:T(8,128)(2,1)}), bf16[16,2,64,1024]{3,2,1,0:T(8,128)(2,1)}, u32[]{:S(2)}, u32[]{:S(2)}) async-start(bf16[16,2,64,1024]{3,2,1,0:T(8,128)(2,1)} %get-tuple-element.80), calls=%async_computation.3 | async-start | bytes 8388608 | tf_op jit(solution)/shard_map/all_to_all | solution.py:41
  220.6 37.1 %collective-permute-start.4 = (bf16[1536,512]{1,0:T(8,128)(2,1)}, bf16[1536,512]{1,0:T(8,128)(2,1)}, u32[]{:S(2)}, u32[]{:S(2)}) collective-permute-start(bf16[1536,512]{1,0:T(8,128)(2,1)} %constant_dynamic-slice_fusion.11), channel_id=1, source_target_pairs={{0,2},{1,3},{2,0},{3,1},{4,6},{5,7},{6,4},{7,5},{8,10},{9,11},{10,... | collective-permute-start | bytes 4718600 | tf_op jit(solution)/shard_map/ppermute | solution.py:572
  223.6 37.9 %collective-permute-start.5 = (bf16[1536,512]{1,0:T(8,128)(2,1)}, bf16[1536,512]{1,0:T(8,128)(2,1)}, u32[]{:S(2)}, u32[]{:S(2)}) collective-permute-start(bf16[1536,512]{1,0:T(8,128)(2,1)} %constant_dynamic-slice_fusion.9), channel_id=1, source_target_pairs={{0,6},{1,7},{2,4},{3,5},{4,2},{5,3},{6,0},{7,1},{8,14},{9,15},{10,... | collective-permute-start | bytes 4718600 | tf_op jit(solution)/shard_map/ppermute | solution.py:572
  265.9 28.2 %collective-permute-start.7 = (bf16[768,512]{1,0:T(8,128)(2,1)S(1)}, bf16[768,512]{1,0:T(8,128)(2,1)S(1)}, u32[]{:S(2)}, u32[]{:S(2)}) collective-permute-start(bf16[768,512]{1,0:T(8,128)(2,1)S(1)} %copy-done.24), channel_id=1, source_target_pairs={{0,6},{1,7},{2,4},{3,5},{4,2},{5,3},{6,0},{7,1},{8,14},{9,15},{10,... | collective-permute-start | bytes 2359304 | tf_op jit(solution)/shard_map/ppermute | solution.py:572
  268.1 25.9 %collective-permute-start.8 = (bf16[768,512]{1,0:T(8,128)(2,1)}, bf16[768,512]{1,0:T(8,128)(2,1)S(1)}, u32[]{:S(2)}, u32[]{:S(2)}) collective-permute-start(bf16[768,512]{1,0:T(8,128)(2,1)} %constant_dynamic-slice_fusion.8), channel_id=1, source_target_pairs={{0,2},{1,3},{2,0},{3,1},{4,6},{5,7},{6,4},{7,5},{8,10},{9,11},{10,... | collective-permute-start | bytes 2359304 | tf_op jit(solution)/shard_map/ppermute | solution.py:572
  286.0 90.6 %collective-permute-start.6 = (bf16[4,2,192,1024]{3,2,1,0:T(8,128)(2,1)}, bf16[4,2,192,1024]{3,2,1,0:T(8,128)(2,1)}, u32[]{:S(2)}, u32[]{:S(2)}) collective-permute-start(bf16[4,2,192,1024]{3,2,1,0:T(8,128)(2,1)} %dynamic-slice_bitcast_fusion), channel_id=1, source_target_pairs={{0,8},{8,0},{16,24},{24,16},{32,40},{40,32},{48,56},{56,48},{64,72... | collective-permute-start | bytes 9437192 | tf_op jit(solution)/shard_map/ppermute | solution.py:572
  295.3 59.9 %all-to-all-start.5 = ((bf16[16,64,1152]{2,1,0:T(8,128)(2,1)}), bf16[16,64,1152]{2,1,0:T(8,128)(2,1)S(1)}, u32[]{:S(2)}, u32[]{:S(2)}) async-start(bf16[16,64,1152]{2,1,0:T(8,128)(2,1)} %bitcast.88), calls=%async_computation.5 | async-start | bytes 4718592 | tf_op jit(solution)/shard_map/all_to_all | solution.py:41
  304.7 42.2 %collective-permute-start.9 = (bf16[768,512]{1,0:T(8,128)(2,1)}, bf16[768,512]{1,0:T(8,128)(2,1)}, u32[]{:S(2)}, u32[]{:S(2)}) collective-permute-start(bf16[768,512]{1,0:T(8,128)(2,1)} %pad_maximum_fusion.1), channel_id=1, source_target_pairs={{0,1},{1,0},{2,3},{3,2},{4,5},{5,4},{6,7},{7,6},{8,9},{9,8},{10,11... | collective-permute-start | bytes 2359304 | tf_op jit(solution)/shard_map/ppermute | solution.py:572
  371.1 23.7 %all-to-all-start.7 = ((bf16[16,64,256]{2,1,0:T(8,128)(2,1)}), bf16[16,64,256]{2,1,0:T(8,128)(2,1)}, u32[]{:S(2)}, u32[]{:S(2)}) async-start(bf16[16,64,256]{2,1,0:T(8,128)(2,1)} %bitcast.20), calls=%async_computation.7 | async-start | bytes 1048576 | tf_op jit(solution)/shard_map/all_to_all | solution.py:41
  382.3 24.4 %collective-permute-start.10 = (bf16[2,192,1024]{2,1,0:T(8,128)(2,1)}, bf16[2,192,1024]{2,1,0:T(8,128)(2,1)}, u32[]{:S(2)}, u32[]{:S(2)}) collective-permute-start(bf16[2,192,1024]{2,1,0:T(8,128)(2,1)} %pad_maximum_fusion.2), channel_id=1, source_target_pairs={{0,32},{8,40},{16,48},{24,56},{32,0},{40,8},{48,16},{56,24},{64,96... | collective-permute-start | bytes 2359304 | tf_op jit(solution)/shard_map/ppermute | solution.py:572
  385.1 25.6 %collective-permute-start.15 = (bf16[2,192,1024]{2,1,0:T(8,128)(2,1)}, bf16[2,192,1024]{2,1,0:T(8,128)(2,1)}, u32[]{:S(2)}, u32[]{:S(2)}) collective-permute-start(bf16[2,192,1024]{2,1,0:T(8,128)(2,1)} %pad_maximum_fusion.5), channel_id=1, source_target_pairs={{0,96},{8,104},{16,112},{24,120},{32,64},{40,72},{48,80},{56,88},{... | collective-permute-start | bytes 2359304 | tf_op jit(solution)/shard_map/ppermute | solution.py:572
  388.1 25.6 %collective-permute-start.13 = (bf16[768,512]{1,0:T(8,128)(2,1)}, bf16[768,512]{1,0:T(8,128)(2,1)}, u32[]{:S(2)}, u32[]{:S(2)}) collective-permute-start(bf16[768,512]{1,0:T(8,128)(2,1)} %pad_maximum_fusion.3.refs_0_), channel_id=1, source_target_pairs={{0,6},{1,7},{2,4},{3,5},{4,2},{5,3},{6,0},{7,1},{8,14},{9,15},{10,... | collective-permute-start | bytes 2359304 | tf_op jit(solution)/shard_map/ppermute | solution.py:572
  396.5 24.5 %all-to-all-start.8 = ((bf16[8,192,256]{2,1,0:T(8,128)(2,1)}), bf16[8,192,256]{2,1,0:T(8,128)(2,1)}, u32[]{:S(2)}, u32[]{:S(2)}) async-start(bf16[8,192,256]{2,1,0:T(8,128)(2,1)} %bitcast.24), calls=%async_computation.8 | async-start | bytes 1572864 | tf_op jit(solution)/shard_map/all_to_all | solution.py:41
  403.2 38.3 %collective-permute-start.18 = (bf16[768,512]{1,0:T(8,128)(2,1)}, bf16[768,512]{1,0:T(8,128)(2,1)}, u32[]{:S(2)}, u32[]{:S(2)}) collective-permute-start(bf16[768,512]{1,0:T(8,128)(2,1)} %pad_maximum_fusion.3.refs_0_), channel_id=1, source_target_pairs={{0,2},{1,3},{2,0},{3,1},{4,6},{5,7},{6,4},{7,5},{8,10},{9,11},{10,... | collective-permute-start | bytes 2359304 | tf_op jit(solution)/shard_map/ppermute | solution.py:572
  406.7 34.8 %collective-permute-start.19 = (bf16[768,512]{1,0:T(8,128)(2,1)}, bf16[768,512]{1,0:T(8,128)(2,1)}, u32[]{:S(2)}, u32[]{:S(2)}) collective-permute-start(bf16[768,512]{1,0:T(8,128)(2,1)} %pad_maximum_fusion.4.refs_1_), channel_id=1, source_target_pairs={{0,6},{1,7},{2,4},{3,5},{4,2},{5,3},{6,0},{7,1},{8,14},{9,15},{10,... | collective-permute-start | bytes 2359304 | tf_op jit(solution)/shard_map/ppermute | solution.py:572
  410.7 24.2 %collective-permute-start.12 = (bf16[192,1024]{1,0:T(8,128)(2,1)}, bf16[192,1024]{1,0:T(8,128)(2,1)}, u32[]{:S(2)}, u32[]{:S(2)}) collective-permute-start(bf16[192,1024]{1,0:T(8,128)(2,1)} %fusion.24), channel_id=1, source_target_pairs={{0,96},{8,104},{16,112},{24,120},{32,64},{40,72},{48,80},{56,88},{... | collective-permute-start | bytes 1179656 | tf_op jit(solution)/shard_map/ppermute | solution.py:572
  423.9 28.6 %all-to-all-start.9 = ((bf16[8,112,256]{2,1,0:T(8,128)(2,1)}), bf16[8,112,256]{2,1,0:T(8,128)(2,1)}, u32[]{:S(2)}, u32[]{:S(2)}) async-start(bf16[8,112,256]{2,1,0:T(8,128)(2,1)} %broadcast_in_dim.80), calls=%async_computation.9 | async-start | bytes 917504 | tf_op jit(solution)/shard_map/all_to_all | solution.py:41
  428.7 31.3 %collective-permute-start.20 = (bf16[768,512]{1,0:T(8,128)(2,1)}, bf16[768,512]{1,0:T(8,128)(2,1)}, u32[]{:S(2)}, u32[]{:S(2)}) collective-permute-start(bf16[768,512]{1,0:T(8,128)(2,1)} %collective-permute-done.13.refs_2_), channel_id=1, source_target_pairs={{0,2},{1,3},{2,0},{3,1},{4,6},{5,7},{6,4},{7,5},{8,10},{9,11},{10,... | collective-permute-start | bytes 2359304 | tf_op jit(solution)/shard_map/ppermute | solution.py:572
  434.9 25.2 %collective-permute-start.21 = (bf16[768,512]{1,0:T(8,128)(2,1)}, bf16[768,512]{1,0:T(8,128)(2,1)}, u32[]{:S(2)}, u32[]{:S(2)}) collective-permute-start(bf16[768,512]{1,0:T(8,128)(2,1)} %collective-permute-done.14.refs_3_), channel_id=1, source_target_pairs={{0,6},{1,7},{2,4},{3,5},{4,2},{5,3},{6,0},{7,1},{8,14},{9,15},{10,... | collective-permute-start | bytes 2359304 | tf_op jit(solution)/shard_map/ppermute | solution.py:572
  (49 other events, 436.1 us)
Sparse Core Ops, SparseCore 0:
  11.8 45.9 all-gather.3
  59.5 67.8 all-gather.7
  129.1 46.8 all-gather.5

commit v5 on v4

--- a/solution.py
+++ b/solution.py
@@ -751,11 +751,10 @@
         [heads_sum, dense_total.reshape(36, 256), jnp.zeros((12, 256), BF)], axis=0
     )
     by_token = split_all(after(head_grad, heads_parts).reshape(NR, TOK, 256), "replica")
-    layers = [after(part, heads_sum) for part in layers]
-    keep = [[add_low(keep[y][n], layers[y][n]) for n in range(2)] for y in range(2)]
-    layers = [exchange(keep[0][1], 12, "shard"), exchange(keep[1][1], 4, "shard")]
     next_a, next_b = exchange(after(own_a, heads_sum), 2), exchange(after(own_b, heads_sum), 6)
-    by_token, other_a, other_b = lax.optimization_barrier((by_token, other_a, other_b))
+    by_token, other_a, other_b, *layers = lax.optimization_barrier(
+        (by_token, other_a, other_b, *layers)
+    )
     rest_a, rest_b = exchange(other_a, 2), exchange(other_b, 6)
     last = spread_all(after(last, by_token), "replica", NR)
 
@@ -774,12 +773,14 @@
         ],
     )
     last, expert_total = lax.optimization_barrier((last, expert_total))
+    keep = [[add_low(keep[y][n], layers[y][n]) for n in range(2)] for y in range(2)]
+    layers = [exchange(keep[0][1], 12, "shard"), exchange(keep[1][1], 4, "shard")]
     query_grad, key_grad, value_grad, norm_one_grad = finish_heads(
         last, query_weight, key_matrix, value_matrix, norm_one
     )
     dense_last = last[:, 64:100].reshape(64, 1152).astype(F32)
 
-    layers = [after(part, by_token) for part in layers]
+    layers = [after(part, last) for part in layers]
     normed_grad = mm(by_token.transpose(1, 0, 2).reshape(TOK, 2048), gathered[:, :2048], NT)
     tokens_wide = tokens.astype(F32)
     inverse = lax.rsqrt(jnp.mean(tokens_wide * tokens_wide, axis=-1, keepdims=True) + EPSILON)

time: 481 us -> 478 us (level)
    ppermute x22, waiting for transfers between devices: 80.8 us -> 86.3 us  [exchange(): lax.ppermute(x, axis, [(i, i ^ bits) for i in range(lax.axis_size(axis))])]
    all_to_all x9, waiting for transfers between devices: 24.7 us -> 19.4 us  [split_all(): return lax.all_to_all(x, axis, 0, 0, tiled=True)]
    unnamed x87 -> x79, local copies, waits for them, and re-layouts: 12.1 us -> 11.5 us
  transfers between devices with their start and end apart: 34 -> 34, of which waited for: 14 -> 14; matrix products, arithmetic and copies ran while one was open for 21% -> 21% of each run, Pallas kernels for 14% -> 15%
where the time goes in v5:
time: 478 us; the launch traced here: 469 us
  waiting for transfers between devices  140 us (29%)
  Pallas kernels  104 us (22%)
  starting transfers between devices  78.5 us (16%)
  other arithmetic  52.7 us (11%)
  local copies, waits for them, and re-layouts  47.4 us (10%)
  blocking collectives  22.4 us (5%)
  between operations  16.1 us (3%)
  matrix products  8.57 us (2%)
    ppermute x22, waiting for transfers between devices, exchange(): lax.ppermute(x, axis, [(i, i ^ bits) for i in range(lax.axis_size(axis))])  86.3 us
    all_to_all x9, starting transfers between devices, split_all(): return lax.all_to_all(x, axis, 0, 0, tiled=True)  47.9 us
    pallas_call x1, Pallas kernels, run_experts(): pl.pallas_call(expert_kernel, grid=(CHUNKS + 6,), in_specs=[taken, taken,...  33.9 us
    ppermute x22, starting transfers between devices, exchange(): lax.ppermute(x, axis, [(i, i ^ bits) for i in range(lax.axis_size(axis))])  30.5 us
    all_gather x1, waiting for transfers between devices, per_device(): lax.all_gather(jnp.concatenate([grouped, out_weight, small], axis=1), 'sh...  23.2 us
    all_to_all x1, blocking collectives, split_all(): return lax.all_to_all(x, axis, 0, 0, tiled=True)  22.4 us
    all_to_all x9, waiting for transfers between devices, split_all(): return lax.all_to_all(x, axis, 0, 0, tiled=True)  19.4 us
    pallas_call x1, Pallas kernels, attend_back(): pl.pallas_call(attend_back_kernel, grid=(NQ,), in_specs=[block, whole(2 *...  18 us
  transfers between devices with their start and end apart: 34, of which 14 were waited for; matrix products, arithmetic and copies ran while one was open for 21% of the time, Pallas kernels for 15%

profile of v5, /device:TPU:0, one launch (start us, length us, event | category | flops | bytes accessed | tf_op | source)
XLA Modules:
  0.0 468.9 jit_solution(17640499577926141201)
XLA Ops:
  13.9 7.0 %all-to-all-start = ((s32[8,1,192]{2,1,0:T(1,128)}), s32[8,1,192]{2,1,0:T(1,128)S(1)}, u32[]{:S(2)}, u32[]{:S(2)}) async-start(s32[8,1,192]{2,1,0:T(1,128)} %broadcast_in_dim.67), calls=%async_computation | async-start | bytes 16384 | tf_op jit(solution)/shard_map/all_to_all | solution.py:41
  34.6 23.2 %all-gather.4.cloned.1.call-done.weight_ref.small_ref.out_ref = bf16[1024,3200]{1,0:T(8,128)(2,1)} async-done(((bf16[64,3200]{1,0:T(8,128)(2,1)}), bf16[1024,3200]{1,0:T(8,128)(2,1)}) %all-gather.4.cloned.1.call-update) | async-done | bytes 6553616 | tf_op jit(solution)/shard_map/all_gather | solution.py:622
  57.8 7.8 %shard_map.195 = (bf16[8,192,256]{2,1,0:T(8,128)(2,1)}, bf16[192,1024]{1,0:T(8,128)(2,1)}, f32[8,1024]{1,0:T(8,128)}) custom-call(bf16[192,1024]{1,0:T(8,128)(2,1)} %tokens_ref.2, bf16[1024,3200]{1,0:T(8,128)(2,1)} %all-gather.4.cloned.1.call-done.weight_ref.small_ref.out_ref, bf16[1024,3200]{1,0:T(8,128)(2,1)} %all-gather.4.cloned.1.call-done.weight_ref.small_ref.out_ref, ...), custom_call_target="tpu_custom_call" | custom-call | tf_op jit(solution)/shard_map/pallas_call | solution.py:84
  65.6 22.4 %all_to_all.51 = bf16[8,192,256]{2,1,0:T(8,128)(2,1)} all-to-all(bf16[8,192,256]{2,1,0:T(8,128)(2,1)} %get-tuple-element.68), channel_id=1, replica_groups=mesh['shard'=16,'replica'=8] {'replica'}, dimensions={0} | all-to-all | bytes 1572864 | tf_op jit(solution)/shard_map/all_to_all | solution.py:41
  88.9 13.1 %shard_map.196 = (bf16[1536,128]{1,0:T(8,128)(2,1)}, f32[6,1,512]{2,1,0:T(1,128)}) custom-call(bf16[1536,256]{1,0:T(8,128)(2,1)} %bitcast.78, bf16[1536,256]{1,0:T(8,128)(2,1)} %bitcast.79, s32[6,1,256]{2,1,0:T(1,128)} %select_n.195.start_ref), custom_call_target="tpu_custom_call" | custom-call | tf_op jit(solution)/shard_map/pallas_call | solution.py:141
  102.0 6.5 %all-to-all-start.2 = ((bf16[8,192,128]{2,1,0:T(8,128)(2,1)}), bf16[8,192,128]{2,1,0:T(8,128)(2,1)S(1)}, u32[]{:S(2)}, u32[]{:S(2)}) async-start(bf16[8,192,128]{2,1,0:T(8,128)(2,1)} %bitcast.95), calls=%async_computation.2 | async-start | bytes 786432 | tf_op jit(solution)/shard_map/all_to_all | solution.py:41
  109.3 9.2 %all-to-all-done.2.mixed_ref = bf16[8,192,128]{2,1,0:T(8,128)(2,1)S(1)} async-done(((bf16[8,192,128]{2,1,0:T(8,128)(2,1)}), bf16[8,192,128]{2,1,0:T(8,128)(2,1)S(1)}, u32[]{:S(2)}, u32[]{:S(2)}) %all-to-all-start.2) | async-done | bytes 393248 | tf_op jit(solution)/shard_map/all_to_all | solution.py:41
  132.3 11.4 %collective-permute-done.1 = bf16[384,1024]{1,0:T(8,128)(2,1)S(1)} collective-permute-done((bf16[384,1024]{1,0:T(8,128)(2,1)S(1)}, bf16[384,1024]{1,0:T(8,128)(2,1)S(1)}, u32[]{:S(2)}, u32[]{:S(2)}) %collective-permute-start.1) | collective-permute-done | bytes 786464 | tf_op jit(solution)/shard_map/ppermute | solution.py:572
  144.7 15.9 %collective-permute-done.2 = bf16[384,1024]{1,0:T(8,128)(2,1)} collective-permute-done((bf16[384,1024]{1,0:T(8,128)(2,1)S(1)}, bf16[384,1024]{1,0:T(8,128)(2,1)}, u32[]{:S(2)}, u32[]{:S(2)}) %collective-permute-start.2) | collective-permute-done | bytes 786464 | tf_op jit(solution)/shard_map/ppermute | solution.py:572
  165.4 10.6 %all-gather.6.cloned.1.call-done.rows_ref = bf16[3072,1152]{1,0:T(8,128)(2,1)} async-done(((bf16[192,1152]{1,0:T(8,128)(2,1)}), bf16[3072,1152]{1,0:T(8,128)(2,1)}) %all-gather.6.cloned.1.call-update) | async-done | bytes 7077904 | tf_op jit(solution)/shard_map/all_gather | solution.py:673
  176.0 33.9 %shard_map.198 = (bf16[2,4,2,192,1024]{4,3,2,1,0:T(8,128)(2,1)}, bf16[16,2,64,1024]{3,2,1,0:T(8,128)(2,1)}, bf16[2,3,1024,512]{3,2,1,0:T(8,128)(2,1)}) custom-call(bf16[3072,1152]{1,0:T(8,128)(2,1)} %all-gather.6.cloned.1.call-done.rows_ref, bf16[3072,1152]{1,0:T(8,128)(2,1)} %all-gather.8.cloned.1.call-done.cot_ref, f32[2,4,4,192]{3,2,1,0:T(4,128)} %copy.75.slots_ref, ...), custom_call_target="tpu_custom_call" | custom-call | tf_op jit(solution)/shard_map/pallas_call | solution.py:396
  209.9 5.1 %all-to-all-start.3 = ((bf16[16,2,64,1024]{3,2,1,0:T(8,128)(2,1)}), bf16[16,2,64,1024]{3,2,1,0:T(8,128)(2,1)}, u32[]{:S(2)}, u32[]{:S(2)}) async-start(bf16[16,2,64,1024]{3,2,1,0:T(8,128)(2,1)} %get-tuple-element.80), calls=%async_computation.3 | async-start | bytes 8388608 | tf_op jit(solution)/shard_map/all_to_all | solution.py:41
  229.1 29.9 %collective-permute-done.5 = bf16[1536,512]{1,0:T(8,128)(2,1)} collective-permute-done((bf16[1536,512]{1,0:T(8,128)(2,1)}, bf16[1536,512]{1,0:T(8,128)(2,1)}, u32[]{:S(2)}, u32[]{:S(2)}) %collective-permute-start.5) | collective-permute-done | bytes 1572896 | tf_op jit(solution)/shard_map/ppermute | solution.py:572
  270.0 9.0 %shard_map.199 = (f32[192,1024]{1,0:T(8,128)}, bf16[8,192,128]{2,1,0:T(8,128)(2,1)}, bf16[1024,1152]{1,0:T(8,128)(2,1)}) custom-call(bf16[2048,1024]{1,0:T(8,128)(2,1)} %bitcast.11.back_ref, bf16[192,2048]{1,0:T(8,128)(2,1)} %compare_convert_fusion.spots_ref, bf16[2048,128]{1,0:T(8,128)(2,1)} %fusion.6.spread_ref, bf16[3,2048]{1,0:T(4,128)(2,1)} %reshape.295.gate_rows_ref, ...), custom_call_target="tpu_custom_call" | custom-call | tf_op jit(solution)/shard_map/pallas_call | solution.py:476
  278.9 5.3 %all-to-all-start.4 = ((bf16[8,192,128]{2,1,0:T(8,128)(2,1)}), bf16[8,192,128]{2,1,0:T(8,128)(2,1)S(1)}, u32[]{:S(2)}, u32[]{:S(2)}) async-start(bf16[8,192,128]{2,1,0:T(8,128)(2,1)} %get-tuple-element.87), calls=%async_computation.4 | async-start | bytes 786432 | tf_op jit(solution)/shard_map/all_to_all | solution.py:41
  284.8 8.8 %all-to-all-done.4 = bf16[8,192,128]{2,1,0:T(8,128)(2,1)S(1)} async-done(((bf16[8,192,128]{2,1,0:T(8,128)(2,1)}), bf16[8,192,128]{2,1,0:T(8,128)(2,1)S(1)}, u32[]{:S(2)}, u32[]{:S(2)}) %all-to-all-start.4) | async-done | bytes 393248 | tf_op jit(solution)/shard_map/all_to_all | solution.py:41
  294.6 4.6 all-to-all-start.5
  310.4 18.0 %shard_map.200 = bf16[1536,256]{1,0:T(8,128)(2,1)} custom-call(bf16[1536,256]{1,0:T(8,128)(2,1)} %bitcast.80, bf16[1536,256]{1,0:T(8,128)(2,1)} %bitcast.81, bf16[1536,128]{1,0:T(8,128)(2,1)} %bitcast.89, s32[6,1,256]{2,1,0:T(1,128)} %select_n.195.start_ref, f32[6,1,512]{2,1,0:T(1,128)} %get-tuple-element.91.lse_ref, ...), custom_call_target="tpu_custom_call" | custom-call | tf_op jit(solution)/shard_map/pallas_call | solution.py:234
  328.4 17.7 %collective-permute-done.9 = bf16[768,512]{1,0:T(8,128)(2,1)} collective-permute-done((bf16[768,512]{1,0:T(8,128)(2,1)}, bf16[768,512]{1,0:T(8,128)(2,1)}, u32[]{:S(2)}, u32[]{:S(2)}) %collective-permute-start.9) | collective-permute-done | bytes 786464 | tf_op jit(solution)/shard_map/ppermute | solution.py:572
  359.8 10.2 %collective-permute-done.10 = bf16[768,512]{1,0:T(8,128)(2,1)} collective-permute-done((bf16[768,512]{1,0:T(8,128)(2,1)S(1)}, bf16[768,512]{1,0:T(8,128)(2,1)}, u32[]{:S(2)}, u32[]{:S(2)}) %collective-permute-start.10) | collective-permute-done | bytes 786464 | tf_op jit(solution)/shard_map/ppermute | solution.py:572
  392.8 6.1 %all-to-all-start.8 = ((bf16[8,192,256]{2,1,0:T(8,128)(2,1)}), bf16[8,192,256]{2,1,0:T(8,128)(2,1)}, u32[]{:S(2)}, u32[]{:S(2)}) async-start(bf16[8,192,256]{2,1,0:T(8,128)(2,1)} %bitcast.19), calls=%async_computation.8 | async-start | bytes 1572864 | tf_op jit(solution)/shard_map/all_to_all | solution.py:41
  426.8 4.6 fusion.9
  433.5 11.0 %shard_map.201.refs_2_ = f32[6144,512]{1,0:T(8,128)} custom-call(s32[12]{0:T(128)} %concatenate.66.places_ref, bf16[768,512]{1,0:T(8,128)(2,1)} %pad_maximum_fusion.2.refs_0_, bf16[768,512]{1,0:T(8,128)(2,1)} %pad_maximum_fusion.3.refs_1_, bf16[768,512]{1,0:T(8,128)(2,1)} %collective-permute-done.11.refs_2_, ...), custom_call_target="tpu_custom_call" | custom-call | tf_op jit(solution)/shard_map/pallas_call | solution.py:557
  456.0 4.9 %shard_map.203 = f32[6144,512]{1,0:T(8,128)} custom-call(s32[4]{0:T(128)} %pad_add_fusion.1.places_ref, bf16[768,512]{1,0:T(8,128)(2,1)} %collective-permute-done.20.refs_0_, bf16[768,512]{1,0:T(8,128)(2,1)} %collective-permute-done.21.refs_1_, f32[6144,512]{1,0:T(8,128)} %shard_map.201.refs_2_), custom_call_target="tpu_custom_call", output_to_operand_aliasing={{}: (3, {})} | custom-call | tf_op jit(solution)/shard_map/pallas_call | solution.py:557
  (237 shorter events, 156.6 us)
Async XLA Ops:
  7.2 50.6 %all-gather.4.cloned.1.call-start = ((), (), s32[]{:S(2)}) async-start(), calls=%async_computation.10 | async-start | bytes 6963200 | tf_op jit(solution)/shard_map/all_gather | solution.py:622
  11.7 117.1 %all-gather.8.cloned.1.call-start = ((), (), s32[]{:S(2)}) async-start(), calls=%async_computation.12 | async-start | bytes 7520256 | tf_op jit(solution)/shard_map/all_gather | solution.py:640
  108.5 67.5 %all-gather.6.cloned.1.call-start = ((), (), s32[]{:S(2)}) async-start(), calls=%async_computation.11 | async-start | bytes 7520256 | tf_op jit(solution)/shard_map/all_gather | solution.py:673
  124.3 36.3 %collective-permute-start.2 = (bf16[384,1024]{1,0:T(8,128)(2,1)S(1)}, bf16[384,1024]{1,0:T(8,128)(2,1)}, u32[]{:S(2)}, u32[]{:S(2)}) collective-permute-start(bf16[384,1024]{1,0:T(8,128)(2,1)S(1)} %pad_maximum_fusion), channel_id=1, source_target_pairs={{0,4},{1,5},{2,6},{3,7},{4,0},{5,1},{6,2},{7,3},{8,12},{9,13},{10,... | collective-permute-start | bytes 2359304 | tf_op jit(solution)/shard_map/ppermute | solution.py:572
  126.6 36.7 %collective-permute-start.3 = (bf16[384,1024]{1,0:T(8,128)(2,1)S(1)}, bf16[384,1024]{1,0:T(8,128)(2,1)}, u32[]{:S(2)}, u32[]{:S(2)}) collective-permute-start(bf16[384,1024]{1,0:T(8,128)(2,1)S(1)} %pad_maximum_fusion), channel_id=1, source_target_pairs={{0,6},{1,7},{2,4},{3,5},{4,2},{5,3},{6,0},{7,1},{8,14},{9,15},{10,... | collective-permute-start | bytes 2359304 | tf_op jit(solution)/shard_map/ppermute | solution.py:572
  209.9 55.6 %all-to-all-start.3 = ((bf16[16,2,64,1024]{3,2,1,0:T(8,128)(2,1)}), bf16[16,2,64,1024]{3,2,1,0:T(8,128)(2,1)}, u32[]{:S(2)}, u32[]{:S(2)}) async-start(bf16[16,2,64,1024]{3,2,1,0:T(8,128)(2,1)} %get-tuple-element.80), calls=%async_computation.3 | async-start | bytes 8388608 | tf_op jit(solution)/shard_map/all_to_all | solution.py:41
  220.7 38.3 %collective-permute-start.5 = (bf16[1536,512]{1,0:T(8,128)(2,1)}, bf16[1536,512]{1,0:T(8,128)(2,1)}, u32[]{:S(2)}, u32[]{:S(2)}) collective-permute-start(bf16[1536,512]{1,0:T(8,128)(2,1)} %constant_dynamic-slice_fusion.9), channel_id=1, source_target_pairs={{0,6},{1,7},{2,4},{3,5},{4,2},{5,3},{6,0},{7,1},{8,14},{9,15},{10,... | collective-permute-start | bytes 4718600 | tf_op jit(solution)/shard_map/ppermute | solution.py:572
  224.8 37.1 %collective-permute-start.4 = (bf16[1536,512]{1,0:T(8,128)(2,1)}, bf16[1536,512]{1,0:T(8,128)(2,1)}, u32[]{:S(2)}, u32[]{:S(2)}) collective-permute-start(bf16[1536,512]{1,0:T(8,128)(2,1)} %constant_dynamic-slice_fusion.11), channel_id=1, source_target_pairs={{0,2},{1,3},{2,0},{3,1},{4,6},{5,7},{6,4},{7,5},{8,10},{9,11},{10,... | collective-permute-start | bytes 4718600 | tf_op jit(solution)/shard_map/ppermute | solution.py:572
  265.5 28.2 %collective-permute-start.7 = (bf16[768,512]{1,0:T(8,128)(2,1)S(1)}, bf16[768,512]{1,0:T(8,128)(2,1)S(1)}, u32[]{:S(2)}, u32[]{:S(2)}) collective-permute-start(bf16[768,512]{1,0:T(8,128)(2,1)S(1)} %constant_dynamic-slice_fusion.10), channel_id=1, source_target_pairs={{0,6},{1,7},{2,4},{3,5},{4,2},{5,3},{6,0},{7,1},{8,14},{9,15},{10,... | collective-permute-start | bytes 2359304 | tf_op jit(solution)/shard_map/ppermute | solution.py:572
  268.2 25.5 %collective-permute-start.8 = (bf16[768,512]{1,0:T(8,128)(2,1)S(1)}, bf16[768,512]{1,0:T(8,128)(2,1)S(1)}, u32[]{:S(2)}, u32[]{:S(2)}) collective-permute-start(bf16[768,512]{1,0:T(8,128)(2,1)S(1)} %copy-done.20), channel_id=1, source_target_pairs={{0,2},{1,3},{2,0},{3,1},{4,6},{5,7},{6,4},{7,5},{8,10},{9,11},{10,... | collective-permute-start | bytes 2359304 | tf_op jit(solution)/shard_map/ppermute | solution.py:572
  284.8 94.2 %collective-permute-start.6 = (bf16[4,2,192,1024]{3,2,1,0:T(8,128)(2,1)}, bf16[4,2,192,1024]{3,2,1,0:T(8,128)(2,1)}, u32[]{:S(2)}, u32[]{:S(2)}) collective-permute-start(bf16[4,2,192,1024]{3,2,1,0:T(8,128)(2,1)} %dynamic-slice_bitcast_fusion), channel_id=1, source_target_pairs={{0,8},{8,0},{16,24},{24,16},{32,40},{40,32},{48,56},{56,48},{64,72... | collective-permute-start | bytes 9437192 | tf_op jit(solution)/shard_map/ppermute | solution.py:572
  294.6 59.7 %all-to-all-start.5 = ((bf16[16,64,1152]{2,1,0:T(8,128)(2,1)}), bf16[16,64,1152]{2,1,0:T(8,128)(2,1)S(1)}, u32[]{:S(2)}, u32[]{:S(2)}) async-start(bf16[16,64,1152]{2,1,0:T(8,128)(2,1)} %bitcast.88), calls=%async_computation.5 | async-start | bytes 4718592 | tf_op jit(solution)/shard_map/all_to_all | solution.py:41
  303.1 43.0 %collective-permute-start.9 = (bf16[768,512]{1,0:T(8,128)(2,1)}, bf16[768,512]{1,0:T(8,128)(2,1)}, u32[]{:S(2)}, u32[]{:S(2)}) collective-permute-start(bf16[768,512]{1,0:T(8,128)(2,1)} %pad_maximum_fusion.1), channel_id=1, source_target_pairs={{0,1},{1,0},{2,3},{3,2},{4,5},{5,4},{6,7},{7,6},{8,9},{9,8},{10,11... | collective-permute-start | bytes 2359304 | tf_op jit(solution)/shard_map/ppermute | solution.py:572
  347.5 22.4 %collective-permute-start.10 = (bf16[768,512]{1,0:T(8,128)(2,1)S(1)}, bf16[768,512]{1,0:T(8,128)(2,1)}, u32[]{:S(2)}, u32[]{:S(2)}) collective-permute-start(bf16[768,512]{1,0:T(8,128)(2,1)S(1)} %add_convert_fusion.2), channel_id=1, source_target_pairs={{0,1},{1,0},{2,3},{3,2},{4,5},{5,4},{6,7},{7,6},{8,9},{9,8},{10,11... | collective-permute-start | bytes 2359304 | tf_op jit(solution)/shard_map/ppermute | solution.py:572
  370.0 22.8 %all-to-all-start.7 = ((bf16[16,64,256]{2,1,0:T(8,128)(2,1)}), bf16[16,64,256]{2,1,0:T(8,128)(2,1)}, u32[]{:S(2)}, u32[]{:S(2)}) async-start(bf16[16,64,256]{2,1,0:T(8,128)(2,1)} %bitcast.18), calls=%async_computation.7 | async-start | bytes 1048576 | tf_op jit(solution)/shard_map/all_to_all | solution.py:41
  376.4 34.1 %collective-permute-start.12 = (bf16[768,512]{1,0:T(8,128)(2,1)}, bf16[768,512]{1,0:T(8,128)(2,1)}, u32[]{:S(2)}, u32[]{:S(2)}) collective-permute-start(bf16[768,512]{1,0:T(8,128)(2,1)} %pad_maximum_fusion.3.refs_1_), channel_id=1, source_target_pairs={{0,2},{1,3},{2,0},{3,1},{4,6},{5,7},{6,4},{7,5},{8,10},{9,11},{10,... | collective-permute-start | bytes 2359304 | tf_op jit(solution)/shard_map/ppermute | solution.py:572
  377.9 32.8 %collective-permute-start.11 = (bf16[768,512]{1,0:T(8,128)(2,1)}, bf16[768,512]{1,0:T(8,128)(2,1)}, u32[]{:S(2)}, u32[]{:S(2)}) collective-permute-start(bf16[768,512]{1,0:T(8,128)(2,1)} %pad_maximum_fusion.2.refs_0_), channel_id=1, source_target_pairs={{0,6},{1,7},{2,4},{3,5},{4,2},{5,3},{6,0},{7,1},{8,14},{9,15},{10,... | collective-permute-start | bytes 2359304 | tf_op jit(solution)/shard_map/ppermute | solution.py:572
  384.8 26.0 %collective-permute-start.14 = (bf16[2,192,1024]{2,1,0:T(8,128)(2,1)}, bf16[2,192,1024]{2,1,0:T(8,128)(2,1)}, u32[]{:S(2)}, u32[]{:S(2)}) collective-permute-start(bf16[2,192,1024]{2,1,0:T(8,128)(2,1)} %pad_maximum_fusion.5), channel_id=1, source_target_pairs={{0,96},{8,104},{16,112},{24,120},{32,64},{40,72},{48,80},{56,88},{... | collective-permute-start | bytes 2359304 | tf_op jit(solution)/shard_map/ppermute | solution.py:572
  388.8 21.9 %collective-permute-start.13 = (bf16[2,192,1024]{2,1,0:T(8,128)(2,1)}, bf16[2,192,1024]{2,1,0:T(8,128)(2,1)}, u32[]{:S(2)}, u32[]{:S(2)}) collective-permute-start(bf16[2,192,1024]{2,1,0:T(8,128)(2,1)} %pad_maximum_fusion.4), channel_id=1, source_target_pairs={{0,32},{8,40},{16,48},{24,56},{32,0},{40,8},{48,16},{56,24},{64,96... | collective-permute-start | bytes 2359304 | tf_op jit(solution)/shard_map/ppermute | solution.py:572
  405.8 25.7 %collective-permute-start.17 = (bf16[768,512]{1,0:T(8,128)(2,1)}, bf16[768,512]{1,0:T(8,128)(2,1)}, u32[]{:S(2)}, u32[]{:S(2)}) collective-permute-start(bf16[768,512]{1,0:T(8,128)(2,1)} %pad_maximum_fusion.3.refs_1_), channel_id=1, source_target_pairs={{0,6},{1,7},{2,4},{3,5},{4,2},{5,3},{6,0},{7,1},{8,14},{9,15},{10,... | collective-permute-start | bytes 2359304 | tf_op jit(solution)/shard_map/ppermute | solution.py:572
  410.5 23.0 %collective-permute-start.16 = (bf16[768,512]{1,0:T(8,128)(2,1)}, bf16[768,512]{1,0:T(8,128)(2,1)}, u32[]{:S(2)}, u32[]{:S(2)}) collective-permute-start(bf16[768,512]{1,0:T(8,128)(2,1)} %pad_maximum_fusion.2.refs_0_), channel_id=1, source_target_pairs={{0,2},{1,3},{2,0},{3,1},{4,6},{5,7},{6,4},{7,5},{8,10},{9,11},{10,... | collective-permute-start | bytes 2359304 | tf_op jit(solution)/shard_map/ppermute | solution.py:572
  413.3 31.2 %all-to-all-start.9 = ((bf16[8,112,256]{2,1,0:T(8,128)(2,1)}), bf16[8,112,256]{2,1,0:T(8,128)(2,1)}, u32[]{:S(2)}, u32[]{:S(2)}) async-start(bf16[8,112,256]{2,1,0:T(8,128)(2,1)} %broadcast_in_dim.80), calls=%async_computation.9 | async-start | bytes 917504 | tf_op jit(solution)/shard_map/all_to_all | solution.py:41
  417.9 38.1 %collective-permute-start.20 = (bf16[768,512]{1,0:T(8,128)(2,1)}, bf16[768,512]{1,0:T(8,128)(2,1)}, u32[]{:S(2)}, u32[]{:S(2)}) collective-permute-start(bf16[768,512]{1,0:T(8,128)(2,1)} %collective-permute-done.11.refs_2_), channel_id=1, source_target_pairs={{0,2},{1,3},{2,0},{3,1},{4,6},{5,7},{6,4},{7,5},{8,10},{9,11},{10,... | collective-permute-start | bytes 2359304 | tf_op jit(solution)/shard_map/ppermute | solution.py:572
  431.5 24.5 %collective-permute-start.21 = (bf16[768,512]{1,0:T(8,128)(2,1)}, bf16[768,512]{1,0:T(8,128)(2,1)}, u32[]{:S(2)}, u32[]{:S(2)}) collective-permute-start(bf16[768,512]{1,0:T(8,128)(2,1)} %collective-permute-done.12.refs_3_), channel_id=1, source_target_pairs={{0,6},{1,7},{2,4},{3,5},{4,2},{5,3},{6,0},{7,1},{8,14},{9,15},{10,... | collective-permute-start | bytes 2359304 | tf_op jit(solution)/shard_map/ppermute | solution.py:572
  (45 other events, 383.8 us)
Sparse Core Ops, SparseCore 0:
  11.8 45.9 all-gather.3
  59.5 67.8 all-gather.7
  129.1 46.8 all-gather.5
